TPU v7x, 32 devices: a whole 2x2x4 slice. The times are simulated.
32 devices in a mesh: dp: 4 (over y, core), ctx: 4 (over z), tp: 2 (over x).
Axes of the slice: x: 2, y: 2, z: 4, core: 2. Of those that a mesh axis runs over, the one named last changes fastest.
Arguments:
- tokens: bfloat16 [12288, 2048], P(('dp', 'ctx')), may hold values from -6 to 6
- segments: int32 [12288], P('dp'), may hold values from 0 to 15, as said below
- query_weight: bfloat16 [2048, 2048], P(('dp', 'ctx'), 'tp'), may hold values from -0.125 to 0.125
- key_weight: bfloat16 [2048, 2048], P(('dp', 'ctx'), 'tp'), may hold values from -0.125 to 0.125
- value_weight: bfloat16 [2048, 2048], P(('dp', 'ctx'), 'tp'), may hold values from -0.125 to 0.125
- out_weight: bfloat16 [2048, 2048], P('tp', ('dp', 'ctx')), may hold values from -0.125 to 0.125
- gate_weight: bfloat16 [2048, 8192], P(('dp', 'ctx'), 'tp'), may hold values from -0.125 to 0.125
- up_weight: bfloat16 [2048, 8192], P(('dp', 'ctx'), 'tp'), may hold values from -0.125 to 0.125
- down_weight: bfloat16 [8192, 2048], P('tp', ('dp', 'ctx')), may hold values from -0.0625 to 0.0625
- query_gain: float32 [2048], P('tp'), may hold values from 0.38 to 2.07
- key_gain: float32 [2048], P('tp'), may hold values from 0.38 to 2.07
- attn_gain: float32 [2048], replicated, may hold values from 0.25 to 1.75
- mlp_gain: float32 [2048], replicated, may hold values from 0.25 to 1.75
- cotangent: bfloat16 [12288, 2048], P(('dp', 'ctx')), may hold values from -6 to 6
Outputs:
- output: bfloat16 [12288, 2048], P(('dp', 'ctx'))
- grad_tokens: float32 [12288, 2048], P(('dp', 'ctx'))
- grad_query: float32 [2048, 2048], P(('dp', 'ctx'), 'tp')
- grad_key: float32 [2048, 2048], P(('dp', 'ctx'), 'tp')
- grad_value: float32 [2048, 2048], P(('dp', 'ctx'), 'tp')
- grad_out: float32 [2048, 2048], P('tp', ('dp', 'ctx'))
- grad_gate: float32 [2048, 8192], P(('dp', 'ctx'), 'tp')
- grad_up: float32 [2048, 8192], P(('dp', 'ctx'), 'tp')
- grad_down: float32 [8192, 2048], P('tp', ('dp', 'ctx'))
- grad_query_gain: float32 [2048], P('tp')
- grad_key_gain: float32 [2048], P('tp')
- grad_attn_gain: float32 [2048], replicated
- grad_mlp_gain: float32 [2048], replicated
Inputs may be any that keep to these rules, and one draw needn't show every extreme that they name: `segments`: numbers never fall along a sequence and differ between sequences; a sequence holds at most four documents, one of which starts within the first 384 tokens of the sequence and ends within the last 384.
All inputs are finite; a program needn't handle non-finite values.
Results may differ from a plain program's by a relative error of at most 0.023.
Values may be sent and summed in bfloat16 or wider, within the bound.
No kernel may reach another device: no remote copies, remote signals or barrier semaphores. Data moves between devices by JAX's collectives and lax.ppermute only.
A program may use at most 448 MiB of HBM per device.

v0:
```python
import jax
import jax.numpy as jnp
from jax import lax
from jax.sharding import PartitionSpec as P

HD = 128


EPSILON = 1e-06
ROPE_BASE = 500000.0
MASKED = -1e30


def positions(doc_ids):
    length_all = doc_ids.shape[0]
    row_index = jnp.arange(length_all, dtype=jnp.int32)
    is_start = jnp.concatenate([jnp.ones((1,), dtype=bool), doc_ids[1:] != doc_ids[:-1]])
    starts = jnp.where(is_start, row_index, jnp.zeros_like(row_index))
    return row_index - lax.cummax(starts, axis=0)


def angles(places, head_size):
    frequency = ROPE_BASE ** (-(jnp.arange(head_size // 2, dtype=jnp.float32) * 2.0 / head_size))
    phases = places.astype(jnp.float32)[:, None] * frequency[None, :]
    return (jnp.cos(phases), jnp.sin(phases))


def rotate(values, cosine, sine_rows):
    half_size = values.shape[-1] // 2
    first_half = values[..., :half_size]
    second_half = values[..., half_size:]
    return jnp.concatenate(
        [
            first_half * cosine - second_half * sine_rows,
            second_half * cosine + first_half * sine_rows,
        ],
        axis=-1,
    )


def unrotate(values, cosine, sine_rows):
    half_size = values.shape[-1] // 2
    first_half = values[..., :half_size]
    second_half = values[..., half_size:]
    return jnp.concatenate(
        [
            first_half * cosine + second_half * sine_rows,
            second_half * cosine - first_half * sine_rows,
        ],
        axis=-1,
    )


def contract_rows(left, right):
    return lax.dot_general(
        left, right, (((0,), (0,)), ((), ())), preferred_element_type=jnp.float32
    )


def contract_cols(left, right):
    return lax.dot_general(
        left, right, (((1,), (1,)), ((), ())), preferred_element_type=jnp.float32
    )


def product(left, right):
    return jnp.dot(left, right, preferred_element_type=jnp.float32)


def body(
    tokens,
    segments,
    query_weight,
    key_weight,
    value_weight,
    out_weight,
    gate_weight,
    up_weight,
    down_weight,
    query_gain,
    key_gain,
    attn_gain,
    mlp_gain,
    cotangent,
):
    shards = (
        query_weight,
        key_weight,
        value_weight,
        gate_weight,
        up_weight,
        out_weight,
        down_weight,
    )
    full_query, full_key, full_value, full_gate, full_up, full_out, full_down = (
        lax.all_gather(shards[0], ("dp", "ctx"), axis=0, tiled=True),
        lax.all_gather(shards[1], ("dp", "ctx"), axis=0, tiled=True),
        lax.all_gather(shards[2], ("dp", "ctx"), axis=0, tiled=True),
        lax.all_gather(shards[3], ("dp", "ctx"), axis=0, tiled=True),
        lax.all_gather(shards[4], ("dp", "ctx"), axis=0, tiled=True),
        lax.all_gather(shards[5], ("dp", "ctx"), axis=1, tiled=True),
        lax.all_gather(shards[6], ("dp", "ctx"), axis=1, tiled=True),
    )
    rows_here = tokens.shape[0]
    model_width = tokens.shape[1]
    local_width = query_gain.shape[0]
    head_count = local_width // HD
    scaling = HD ** (-0.5)
    offset = lax.axis_index("ctx") * rows_here
    all_places = positions(segments)
    my_places = lax.dynamic_slice_in_dim(all_places, offset, rows_here)
    my_docs = lax.dynamic_slice_in_dim(segments, offset, rows_here)
    query_index = offset + jnp.arange(rows_here, dtype=jnp.int32)
    key_index = jnp.arange(segments.shape[0], dtype=jnp.int32)
    allowed = (my_docs[:, None] == segments[None, :]) & (key_index[None, :] <= query_index[:, None])
    inputs_f = tokens.astype(jnp.float32)
    query_raw = product(tokens, full_query)
    key_raw = product(tokens, full_key)
    value_raw = product(tokens, full_value)
    query_sq, key_sq = lax.psum(
        (jnp.sum(query_raw * query_raw, axis=-1), jnp.sum(key_raw * key_raw, axis=-1)), "tp"
    )
    query_scale = lax.rsqrt(query_sq[:, None] / model_width + EPSILON)
    key_scale = lax.rsqrt(key_sq[:, None] / model_width + EPSILON)
    query_unit = query_raw * query_scale
    key_unit = key_raw * key_scale
    cosine, sine_rows = angles(my_places, HD)
    cosine = cosine[:, None]
    sine_rows = sine_rows[:, None]
    query_rot = rotate(
        (query_unit * query_gain).reshape(rows_here, head_count, HD), cosine, sine_rows
    ).astype(jnp.bfloat16)
    key_rot = rotate(
        (key_unit * key_gain).reshape(rows_here, head_count, HD), cosine, sine_rows
    ).astype(jnp.bfloat16)
    value_low = value_raw.astype(jnp.bfloat16).reshape(rows_here, head_count, HD)
    key_all, value_all = (
        lax.all_gather(key_rot, "ctx", axis=0, tiled=True),
        lax.all_gather(value_low, "ctx", axis=0, tiled=True),
    )

    def masked_scores():
        raw_scores = (
            jnp.einsum("qhd,khd->hqk", query_rot, key_all, preferred_element_type=jnp.float32)
            * scaling
        )
        return jnp.where(allowed[None], raw_scores, MASKED)

    scores = masked_scores()
    row_max = jnp.max(scores, axis=-1, keepdims=True)
    exponent = jnp.exp(scores - row_max)
    row_total = jnp.sum(exponent, axis=-1, keepdims=True)
    probs_low = (exponent / row_total).astype(jnp.bfloat16)
    attended = jnp.einsum("hqk,khd->qhd", probs_low, value_all, preferred_element_type=jnp.float32)
    attended = attended.reshape(rows_here, local_width).astype(jnp.bfloat16)
    attn_rows = lax.psum(product(attended, full_out), "tp")
    attn_scale = lax.rsqrt(jnp.mean(attn_rows * attn_rows, axis=-1, keepdims=True) + EPSILON)
    attn_unit = attn_rows * attn_scale
    hidden_rows = inputs_f + attn_unit * attn_gain
    hidden_low = hidden_rows.astype(jnp.bfloat16)
    gate_rows = product(hidden_low, full_gate)
    up_rows = product(hidden_low, full_up)
    sigmoid_gate = jax.nn.sigmoid(gate_rows)
    silu_gate = gate_rows * sigmoid_gate
    act_low = (silu_gate * up_rows).astype(jnp.bfloat16)
    mlp_rows = lax.psum(product(act_low, full_down).astype(jnp.bfloat16), "tp").astype(jnp.float32)
    mlp_scale = lax.rsqrt(jnp.mean(mlp_rows * mlp_rows, axis=-1, keepdims=True) + EPSILON)
    mlp_unit = mlp_rows * mlp_scale
    output = (hidden_rows + mlp_unit * mlp_gain).astype(jnp.bfloat16)
    grad_out_f = cotangent.astype(jnp.float32)
    mlp_gain_part = jnp.sum(grad_out_f * mlp_unit, axis=0)
    scaled_out = grad_out_f * mlp_gain
    grad_mlp_low = (
        mlp_scale
        * (scaled_out - mlp_unit * jnp.mean(scaled_out * mlp_unit, axis=-1, keepdims=True))
    ).astype(jnp.bfloat16)
    down_grad = contract_rows(act_low, grad_mlp_low)
    grad_act = contract_cols(grad_mlp_low, full_down)
    grad_gate_low = (
        grad_act * up_rows * (sigmoid_gate * (1.0 + gate_rows * (1.0 - sigmoid_gate)))
    ).astype(jnp.bfloat16)
    grad_up_low = (grad_act * silu_gate).astype(jnp.bfloat16)
    gate_grad = contract_rows(hidden_low, grad_gate_low)
    up_grad = contract_rows(hidden_low, grad_up_low)
    back_rows = lax.psum(
        contract_cols(grad_gate_low, full_gate) + contract_cols(grad_up_low, full_up), "tp"
    )
    grad_hidden = grad_out_f + back_rows
    attn_gain_part = jnp.sum(grad_hidden * attn_unit, axis=0)
    scaled_hidden = grad_hidden * attn_gain
    grad_attn_low = (
        attn_scale
        * (scaled_hidden - attn_unit * jnp.mean(scaled_hidden * attn_unit, axis=-1, keepdims=True))
    ).astype(jnp.bfloat16)
    out_grad = contract_rows(attended, grad_attn_low)
    grad_att_low = (
        contract_cols(grad_attn_low, full_out)
        .astype(jnp.bfloat16)
        .reshape(rows_here, head_count, HD)
    )
    again_scores = masked_scores()
    softmax_rows = jnp.exp(again_scores - row_max) / row_total
    again_low = softmax_rows.astype(jnp.bfloat16)
    grad_probs = jnp.einsum(
        "qhd,khd->hqk", grad_att_low, value_all, preferred_element_type=jnp.float32
    )
    inner_sum = jnp.sum(softmax_rows * grad_probs, axis=-1, keepdims=True)
    grad_scores = (softmax_rows * (grad_probs - inner_sum)).astype(jnp.bfloat16)
    grad_query_rot = (
        jnp.einsum("hqk,khd->qhd", grad_scores, key_all, preferred_element_type=jnp.float32)
        * scaling
    )
    key_terms = (
        jnp.einsum("hqk,qhd->khd", grad_scores, query_rot, preferred_element_type=jnp.float32)
        * scaling
    )
    value_terms = jnp.einsum(
        "hqk,qhd->khd", again_low, grad_att_low, preferred_element_type=jnp.float32
    )
    key_back, value_back = (
        lax.psum_scatter(
            key_terms.astype(jnp.bfloat16), "ctx", scatter_dimension=0, tiled=True
        ).astype(jnp.float32),
        lax.psum_scatter(
            value_terms.astype(jnp.bfloat16), "ctx", scatter_dimension=0, tiled=True
        ).astype(jnp.float32),
    )
    grad_query_normed = unrotate(grad_query_rot, cosine, sine_rows).reshape(rows_here, local_width)
    grad_key_normed = unrotate(key_back, cosine, sine_rows).reshape(rows_here, local_width)
    query_gain_part = jnp.sum(grad_query_normed * query_unit, axis=0)
    key_gain_part = jnp.sum(grad_key_normed * key_unit, axis=0)
    scaled_query = grad_query_normed * query_gain
    scaled_key = grad_key_normed * key_gain
    query_inner, key_inner = lax.psum(
        (jnp.sum(scaled_query * query_unit, axis=-1), jnp.sum(scaled_key * key_unit, axis=-1)), "tp"
    )
    grad_query_low = (
        query_scale * (scaled_query - query_unit * (query_inner[:, None] / model_width))
    ).astype(jnp.bfloat16)
    grad_key_low = (
        key_scale * (scaled_key - key_unit * (key_inner[:, None] / model_width))
    ).astype(jnp.bfloat16)
    grad_value_low = value_back.reshape(rows_here, local_width).astype(jnp.bfloat16)
    query_grad = contract_rows(tokens, grad_query_low)
    key_grad = contract_rows(tokens, grad_key_low)
    value_grad = contract_rows(tokens, grad_value_low)
    input_part = (
        contract_cols(grad_query_low, full_query)
        + contract_cols(grad_key_low, full_key)
        + contract_cols(grad_value_low, full_value)
    )
    grad_tokens = grad_hidden + lax.psum(input_part.astype(jnp.bfloat16), "tp").astype(jnp.float32)
    query_shard, key_shard, value_shard, gate_shard, up_shard, out_shard, down_shard = (
        lax.psum_scatter(
            query_grad.astype(jnp.bfloat16), ("dp", "ctx"), scatter_dimension=0, tiled=True
        ).astype(jnp.float32),
        lax.psum_scatter(
            key_grad.astype(jnp.bfloat16), ("dp", "ctx"), scatter_dimension=0, tiled=True
        ).astype(jnp.float32),
        lax.psum_scatter(
            value_grad.astype(jnp.bfloat16), ("dp", "ctx"), scatter_dimension=0, tiled=True
        ).astype(jnp.float32),
        lax.psum_scatter(
            gate_grad.astype(jnp.bfloat16), ("dp", "ctx"), scatter_dimension=0, tiled=True
        ).astype(jnp.float32),
        lax.psum_scatter(
            up_grad.astype(jnp.bfloat16), ("dp", "ctx"), scatter_dimension=0, tiled=True
        ).astype(jnp.float32),
        lax.psum_scatter(
            out_grad.astype(jnp.bfloat16), ("dp", "ctx"), scatter_dimension=1, tiled=True
        ).astype(jnp.float32),
        lax.psum_scatter(
            down_grad.astype(jnp.bfloat16), ("dp", "ctx"), scatter_dimension=1, tiled=True
        ).astype(jnp.float32),
    )
    query_gain_grad, key_gain_grad, attn_gain_grad, mlp_gain_grad = lax.psum(
        (query_gain_part, key_gain_part, attn_gain_part, mlp_gain_part), ("dp", "ctx")
    )
    return (
        output,
        grad_tokens,
        query_shard,
        key_shard,
        value_shard,
        out_shard,
        gate_shard,
        up_shard,
        down_shard,
        query_gain_grad,
        key_gain_grad,
        attn_gain_grad,
        mlp_gain_grad,
    )


def solution(mesh):
    in_specs = (
        P(("dp", "ctx"), None),
        P("dp"),
        P(("dp", "ctx"), "tp"),
        P(("dp", "ctx"), "tp"),
        P(("dp", "ctx"), "tp"),
        P("tp", ("dp", "ctx")),
        P(("dp", "ctx"), "tp"),
        P(("dp", "ctx"), "tp"),
        P("tp", ("dp", "ctx")),
        P("tp"),
        P("tp"),
        P(),
        P(),
        P(("dp", "ctx"), None),
    )
    out_specs = (
        P(("dp", "ctx"), None),
        P(("dp", "ctx"), None),
        P(("dp", "ctx"), "tp"),
        P(("dp", "ctx"), "tp"),
        P(("dp", "ctx"), "tp"),
        P("tp", ("dp", "ctx")),
        P(("dp", "ctx"), "tp"),
        P(("dp", "ctx"), "tp"),
        P("tp", ("dp", "ctx")),
        P("tp"),
        P("tp"),
        P(),
        P(),
    )
    return jax.shard_map(body, mesh=mesh, in_specs=in_specs, out_specs=out_specs, check_vma=False)
```

profile of v0, /device:TPU:0, one launch (start us, length us, event | category | flops | bytes accessed | tf_op | source)
XLA Modules:
  0.0 2655.8 jit_solution(16605749336280798548)
XLA Ops:
  13.5 50.2 %all-gather.16.cloned.1.call-done = bf16[2048,1024]{1,0:T(8,128)(2,1)} async-done(((bf16[128,1024]{1,0:T(8,128)(2,1)}), bf16[2048,1024]{1,0:T(8,128)(2,1)}) %all-gather.16.cloned.1.call-update) | async-done | bytes 4194320 | tf_op jit(solution)/shard_map/all_gather | solution.py:97
  70.0 45.1 %all-gather.14.cloned.1.call-done = bf16[2048,1024]{1,0:T(8,128)(2,1)} async-done(((bf16[128,1024]{1,0:T(8,128)(2,1)}), bf16[2048,1024]{1,0:T(8,128)(2,1)}) %all-gather.14.cloned.1.call-update) | async-done | bytes 4194320 | tf_op jit(solution)/shard_map/all_gather | solution.py:96
  141.5 24.9 all-gather.10.cloned.1.call-done
  180.8 101.5 %all-gather.18.cloned.1.call-done = bf16[3072,8,128]{2,0,1:T(8,128)(2,1)} async-done(((bf16[768,8,128]{2,0,1:T(8,128)(2,1)}), bf16[3072,8,128]{2,0,1:T(8,128)(2,1)}) %all-gather.18.cloned.1.call-update) | async-done | bytes 6291472 | tf_op jit(solution)/shard_map/all_gather | solution.py:138
  282.3 34.2 %fusion.41 = (f32[8,768]{1,0:T(8,128)S(1)}, f32[8,768,3072]{2,1,0:T(8,128)}) fusion(pred[768,3072]{1,0:T(8,128)(4,1)} %fusion.10, bf16[3072,8,128]{2,0,1:T(8,128)(2,1)} %all-gather.18.cloned.1.call-done, bf16[768,8,64]{2,0,1:T(8,128)(2,1)} %get-tuple-element.71, bf16[768,8,64]{2,0,1:T(8,128)(2,1)} %get-tuple-element.70), kind=kOutput, calls=%fused_computation.112 | convolution fusion | flops 4910484480 | bytes 85745664 | tf_op jit(solution)/shard_map/sub | solution.py:151
  316.5 81.3 %all-gather.12.cloned.1.call-done = bf16[3072,8,128]{0,2,1:T(8,128)(2,1)} async-done(((bf16[768,8,128]{0,2,1:T(8,128)(2,1)}), bf16[3072,8,128]{0,2,1:T(8,128)(2,1)}) %all-gather.12.cloned.1.call-update) | async-done | bytes 6291472 | tf_op jit(solution)/shard_map/all_gather | solution.py:139
  397.9 29.4 %fusion.30 = bf16[8,128,768]{2,1,0:T(8,128)(2,1)} fusion(bf16[3072,8,128]{0,2,1:T(8,128)(2,1)} %all-gather.12.cloned.1.call-done, f32[8,768,3072]{2,1,0:T(8,128)} %get-tuple-element.95, f32[8,768]{1,0:T(8,128)S(1)} %get-tuple-element.94), kind=kOutput, calls=%fused_computation.83 | convolution fusion | flops 4870373376 | bytes 83386368 | tf_op jit(solution)/shard_map/hqk,khd->qhd/dot_general | solution.py:154
  427.3 24.0 all-gather.20.cloned.1.call-done
  462.4 149.2 %all-reduce.8.cloned.1.call-done = f32[768,2048]{1,0:T(8,128)} async-done(((f32[768,2048]{1,0:T(8,128)}), f32[768,2048]{1,0:T(8,128)}) %all-reduce.8.cloned.1.call-update) | async-done | bytes 6291472 | tf_op jit(solution)/shard_map/psum | solution.py:156
  619.0 122.1 %all-gather.22.cloned.1.call-done = bf16[2048,4096]{1,0:T(8,128)(2,1)} async-done(((bf16[128,4096]{1,0:T(8,128)(2,1)}), bf16[2048,4096]{1,0:T(8,128)(2,1)}) %all-gather.22.cloned.1.call-update) | async-done | bytes 16777232 | tf_op jit(solution)/shard_map/all_gather | solution.py:99
  761.2 107.3 %all-gather.24.cloned.1.call-done = bf16[2048,4096]{1,0:T(8,128)(2,1)} async-done(((bf16[128,4096]{1,0:T(8,128)(2,1)}), bf16[2048,4096]{1,0:T(8,128)(2,1)}) %all-gather.24.cloned.1.call-update) | async-done | bytes 16777232 | tf_op jit(solution)/shard_map/all_gather | solution.py:100
  868.5 24.2 multiply_convert_fusion.4
  892.7 106.5 %all-gather.26.cloned.1.call-done = bf16[4096,2048]{1,0:T(8,128)(2,1)} async-done(((bf16[4096,128]{1,0:T(8,128)(2,1)}), bf16[4096,2048]{1,0:T(8,128)(2,1)}) %all-gather.26.cloned.1.call-update) | async-done | bytes 16777232 | tf_op jit(solution)/shard_map/all_gather | solution.py:102
  1018.9 84.0 %all-reduce.10.cloned.1.call-done = bf16[768,2048]{1,0:T(8,128)(2,1)} async-done(((bf16[768,2048]{1,0:T(8,128)(2,1)}), bf16[768,2048]{1,0:T(8,128)(2,1)}) %all-reduce.10.cloned.1.call-update) | async-done | bytes 3145744 | tf_op jit(solution)/shard_map/psum | solution.py:166
  1109.0 27.7 %multiply_convert_fusion.2 = (bf16[768,4096]{1,0:T(8,128)(2,1)}, bf16[768,4096]{1,0:T(8,128)(2,1)}) fusion(f32[768,4096]{1,0:T(8,128)} %fusion.43, f32[768,4096]{1,0:T(8,128)} %get-tuple-element.97, bf16[4096,2048]{1,0:T(8,128)(2,1)} %all-gather.26.cloned.1.call-done, bf16[768,2048]{1,0:T(8,128)(2,1)S(1)} %copy-done.2, ...), kind=kOutput, calls=%fused_computation.18 | convolution fusion | flops 12938379264 | bytes 60831744 | tf_op jit(solution)/shard_map/dot_general | solution.py:61
  1157.0 21.3 convolution_add_fusion
  1178.4 153.3 %all-reduce.12.cloned.1.call-done = f32[768,2048]{1,0:T(8,128)} async-done(((f32[768,2048]{1,0:T(8,128)}), f32[768,2048]{1,0:T(8,128)}) %all-reduce.12.cloned.1.call-update) | async-done | bytes 6291472 | tf_op jit(solution)/shard_map/psum | solution.py:185
  1352.7 49.8 %multiply_reduce_fusion = (f32[8,768]{1,0:T(8,128)S(1)}, f32[8,768,3072]{2,1,0:T(8,128)}) fusion(f32[8,768,3072]{2,1,0:T(8,128)} %get-tuple-element.95, f32[8,768]{1,0:T(8,128)S(1)} %copy-done.52, bf16[768,8,128]{0,2,1:T(8,128)(2,1)S(1)} %bitcast.117, bf16[3072,8,128]{0,2,1:T(8,128)(2,1)} %all-gather.12.cloned.1.call-done), kind=kOutput, calls=%fused_computation.2 | convolution fusion | flops 4888455168 | bytes 158908416 | tf_op jit(solution)/shard_map/qhd,khd->hqk/dot_general | solution.py:204
  1402.5 59.5 %multiply_convert_fusion = bf16[8,768,3072]{2,1,0:T(8,128)(2,1)} fusion(f32[8,768,3072]{2,1,0:T(8,128)} %get-tuple-element.99, f32[8,768]{1,0:T(8,128)S(1)} %get-tuple-element.98, f32[8,768,3072]{2,1,0:T(8,128)} %get-tuple-element.95, f32[8,768]{1,0:T(8,128)S(1)} %copy-done.52), kind=kLoop, calls=%fused_computation.1 | loop fusion | flops 75497472 | bytes 188792832 | tf_op jit(solution)/shard_map/convert_element_type | solution.py:208
  1462.1 21.6 fusion.24
  1485.0 29.3 %convert_bitcast_fusion = bf16[3072,8,128]{0,2,1:T(8,128)(2,1)} fusion(bf16[768,8,128]{0,2,1:T(8,128)(2,1)S(1)} %bitcast.118, f32[8,768,3072]{2,1,0:T(8,128)} %get-tuple-element.95, f32[8,768]{1,0:T(8,128)S(1)} %copy-done.52), kind=kOutput, calls=%fused_computation.46 | convolution fusion | flops 4872732672 | bytes 83386368 | tf_op jit(solution)/shard_map/hqk,qhd->khd/dot_general | solution.py:217
  1549.5 45.1 %reduce-scatter.20.cloned.1.call-done = bf16[768,8,128]{2,0,1:T(8,128)(2,1)} async-done(((bf16[3072,8,128]{2,0,1:T(8,128)(2,1)}), bf16[768,8,128]{2,0,1:T(8,128)(2,1)}) %reduce-scatter.20.cloned.1.call-update) | async-done | bytes 1572880 | tf_op jit(solution)/shard_map/reduce_scatter | solution.py:221
  1630.1 78.0 %reduce-scatter.22.cloned.1.call-done = bf16[768,8,128]{0,2,1:T(8,128)(2,1)} async-done(((bf16[3072,8,128]{0,2,1:T(8,128)(2,1)}), bf16[768,8,128]{0,2,1:T(8,128)(2,1)}) %reduce-scatter.22.cloned.1.call-update) | async-done | bytes 1572880 | tf_op jit(solution)/shard_map/reduce_scatter | solution.py:224
  1721.7 21.3 convolution_convert_fusion
  1742.9 20.7 copy.92
  1849.2 61.0 %all-reduce = (f32[1024]{0:T(1024)}, f32[1024]{0:T(1024)}, f32[2048]{0:T(1024)}, f32[2048]{0:T(1024)}) all-reduce(f32[1024]{0:T(1024)S(1)} %copy-done.54, f32[1024]{0:T(1024)S(1)} %copy-done.53, f32[2048]{0:T(1024)S(1)} %copy-done.48, f32[2048]{0:T(1024)S(1)} %copy-done.47), channel_id=1, replica_groups=mesh['dp'=4,'ctx'=4,'tp'=2] {'dp','ctx'}, use_global_device_ids=true, to_apply=%region_31.32 | all-reduce | flops 6144 | bytes 49152 | tf_op jit(solution)/shard_map/psum | solution.py:276
  1918.8 136.5 %reduce-scatter.36.cloned.1.call-done = bf16[128,4096]{1,0:T(8,128)(2,1)} async-done(((bf16[2048,4096]{1,0:T(8,128)(2,1)}), bf16[128,4096]{1,0:T(8,128)(2,1)}) %reduce-scatter.36.cloned.1.call-update) | async-done | bytes 1048592
  2058.4 179.0 %reduce-scatter.26.cloned.1.call-done = bf16[128,4096]{1,0:T(8,128)(2,1)} async-done(((bf16[2048,4096]{1,0:T(8,128)(2,1)}), bf16[128,4096]{1,0:T(8,128)(2,1)}) %reduce-scatter.26.cloned.1.call-update) | async-done | bytes 1048592 | tf_op jit(solution)/shard_map/reduce_scatter | solution.py:266
  2240.2 179.5 %reduce-scatter.24.cloned.1.call-done = bf16[128,4096]{1,0:T(8,128)(2,1)} async-done(((bf16[2048,4096]{1,0:T(8,128)(2,1)}), bf16[128,4096]{1,0:T(8,128)(2,1)}) %reduce-scatter.24.cloned.1.call-update) | async-done | bytes 1048592 | tf_op jit(solution)/shard_map/reduce_scatter | solution.py:263
  2422.5 72.8 %reduce-scatter.32.cloned.1.call-done = bf16[128,1024]{1,0:T(8,128)(2,1)} async-done(((bf16[2048,1024]{1,0:T(8,128)(2,1)}), bf16[128,1024]{1,0:T(8,128)(2,1)}) %reduce-scatter.32.cloned.1.call-update) | async-done | bytes 262160
  2497.3 73.7 %reduce-scatter.28.cloned.1.call-done = bf16[128,1024]{1,0:T(8,128)(2,1)} async-done(((bf16[2048,1024]{1,0:T(8,128)(2,1)}), bf16[128,1024]{1,0:T(8,128)(2,1)}) %reduce-scatter.28.cloned.1.call-update) | async-done | bytes 262160
  2573.1 73.6 %reduce-scatter.30.cloned.1.call-done = bf16[128,1024]{1,0:T(8,128)(2,1)} async-done(((bf16[2048,1024]{1,0:T(8,128)(2,1)}), bf16[128,1024]{1,0:T(8,128)(2,1)}) %reduce-scatter.30.cloned.1.call-update) | async-done | bytes 262160
  (243 shorter events, 352.8 us)
Async XLA Ops:
  7.2 56.5 %all-gather.16.cloned.1.call-start = ((), (), s32[]{:S(2)}) async-start(), calls=%async_computation.12 | async-start | bytes 4456448 | tf_op jit(solution)/shard_map/all_gather | solution.py:97
  7.9 107.2 %all-gather.14.cloned.1.call-start = ((), (), s32[]{:S(2)}) async-start(), calls=%async_computation.11 | async-start | bytes 4456448 | tf_op jit(solution)/shard_map/all_gather | solution.py:96
  8.7 157.8 %all-gather.10.cloned.1.call-start = ((), (), s32[]{:S(2)}) async-start(), calls=%async_computation.9 | async-start | bytes 4456448 | tf_op jit(solution)/shard_map/all_gather | solution.py:98
  9.4 272.9 %all-gather.18.cloned.1.call-start = ((), (), s32[]{:S(2)}) async-start(), calls=%async_computation.13 | async-start | bytes 7864320 | tf_op jit(solution)/shard_map/all_gather | solution.py:138
  13.5 122.0 %copy-start.21 = (f32[768,64]{1,0:T(8,128)}, f32[768,64]{1,0:T(8,128)S(1)}, u32[]{:S(2)}) copy-start(f32[768,64]{1,0:T(8,128)S(1)} %get-tuple-element.88) | copy-start | bytes 589828
  70.0 60.2 %copy-start.43 = (f32[1024]{0:T(1024)S(1)}, f32[1024]{0:T(1024)}, u32[]{:S(2)}) copy-start(f32[1024]{0:T(1024)} %param.24) | copy-start | bytes 12292
  141.0 256.9 %all-gather.12.cloned.1.call-start = ((), (), s32[]{:S(2)}) async-start(), calls=%async_computation.10 | async-start | bytes 7864320 | tf_op jit(solution)/shard_map/all_gather | solution.py:139
  175.8 275.5 %all-gather.20.cloned.1.call-start = ((), (), s32[]{:S(2)}) async-start(), calls=%async_computation.14 | async-start | bytes 4456448 | tf_op jit(solution)/shard_map/all_gather | solution.py:101
  176.4 435.3 %all-reduce.8.cloned.1.call-start = ((), (), s32[]{:S(2)}) async-start(), calls=%async_computation.15 | async-start | bytes 12582912 | tf_op jit(solution)/shard_map/psum | solution.py:156
  316.5 110.7 %copy-start.51 = (f32[8,768]{1,0:T(8,128)}, f32[8,768]{1,0:T(8,128)S(1)}, u32[]{:S(2)}) copy-start(f32[8,768]{1,0:T(8,128)S(1)} %get-tuple-element.94) | copy-start | bytes 73732
  460.1 280.9 %all-gather.22.cloned.1.call-start = ((), (), s32[]{:S(2)}) async-start(), calls=%async_computation.16 | async-start | bytes 17825792 | tf_op jit(solution)/shard_map/all_gather | solution.py:99
  460.9 407.6 %all-gather.24.cloned.1.call-start = ((), (), s32[]{:S(2)}) async-start(), calls=%async_computation.17 | async-start | bytes 17825792 | tf_op jit(solution)/shard_map/all_gather | solution.py:100
  461.6 537.6 %all-gather.26.cloned.1.call-start = ((), (), s32[]{:S(2)}) async-start(), calls=%async_computation.18 | async-start | bytes 17825792 | tf_op jit(solution)/shard_map/all_gather | solution.py:102
  462.2 153.5 %copy-start.33 = (f32[2048]{0:T(1024)S(1)}, f32[2048]{0:T(1024)}, u32[]{:S(2)}) copy-start(f32[2048]{0:T(1024)} %param.25) | copy-start | bytes 24580
  462.2 640.7 %all-reduce.10.cloned.1.call-start = ((), (), s32[]{:S(2)}) async-start(), calls=%async_computation.19 | async-start | bytes 6291456 | tf_op jit(solution)/shard_map/psum | solution.py:166
  619.0 249.5 %copy-start.25 = (bf16[768,2048]{1,0:T(8,128)(2,1)S(1)}, bf16[768,2048]{1,0:T(8,128)(2,1)}, u32[]{:S(2)}) copy-start(bf16[768,2048]{1,0:T(8,128)(2,1)} %fusion.27) | copy-start | bytes 9437188
  1018.8 86.9 %copy-start.2 = (bf16[768,2048]{1,0:T(8,128)(2,1)S(1)}, bf16[768,2048]{1,0:T(8,128)(2,1)}, u32[]{:S(2)}) copy-start(bf16[768,2048]{1,0:T(8,128)(2,1)} %param.27) | copy-start | bytes 9437188
  1018.8 86.9 %copy-start.49 = (f32[2048]{0:T(1024)S(1)}, f32[2048]{0:T(1024)}, u32[]{:S(2)}) copy-start(f32[2048]{0:T(1024)} %param.26) | copy-start | bytes 24580
  1018.8 312.9 %all-reduce.12.cloned.1.call-start = ((), (), s32[]{:S(2)}) async-start(), calls=%async_computation.20 | async-start | bytes 12582912 | tf_op jit(solution)/shard_map/psum | solution.py:185
  1105.8 233.1 %copy-start.45 = (f32[768]{0:T(1024)}, f32[768]{0:T(1024)S(1)}, u32[]{:S(2)}) copy-start(f32[768]{0:T(1024)S(1)} %add_rsqrt_fusion) | copy-start | bytes 9220
  1178.3 153.4 %copy-start.34 = (f32[2048]{0:T(1024)S(1)}, f32[2048]{0:T(1024)}, u32[]{:S(2)}) copy-start(f32[2048]{0:T(1024)} %param.25) | copy-start | bytes 24580
  1178.3 153.4 %copy-start.40 = (f32[768]{0:T(1024)S(1)}, f32[768]{0:T(1024)}, u32[]{:S(2)}) copy-start(f32[768]{0:T(1024)} %copy-done.39) | copy-start | bytes 9220
  1178.3 416.2 %reduce-scatter.20.cloned.1.call-start = ((), (), s32[]{:S(2)}) async-start(), calls=%async_computation.21 | async-start | bytes 7864320 | tf_op jit(solution)/shard_map/reduce_scatter | solution.py:221
  1483.6 224.5 %reduce-scatter.22.cloned.1.call-start = ((), (), s32[]{:S(2)}) async-start(), calls=%async_computation.22 | async-start | bytes 7864320 | tf_op jit(solution)/shard_map/reduce_scatter | solution.py:224
  1514.3 332.9 %reduce-scatter.34.cloned.1.call-start = ((), (), s32[]{:S(2)}) async-start(), calls=%async_computation.29 | async-start | bytes 4456448
  1529.0 381.2 %all-reduce.14.cloned.1.call-start = ((), (), s32[]{:S(2)}) async-start(), calls=%async_computation.23 | async-start | bytes 6291456 | tf_op jit(solution)/shard_map/psum | solution.py:252
  1719.6 335.7 %reduce-scatter.36.cloned.1.call-start = ((), (), s32[]{:S(2)}) async-start(), calls=%async_computation.30 | async-start | bytes 17825792
  1763.7 473.7 %reduce-scatter.26.cloned.1.call-start = ((), (), s32[]{:S(2)}) async-start(), calls=%async_computation.25 | async-start | bytes 17825792 | tf_op jit(solution)/shard_map/reduce_scatter | solution.py:266
  1783.7 636.0 %reduce-scatter.24.cloned.1.call-start = ((), (), s32[]{:S(2)}) async-start(), calls=%async_computation.24 | async-start | bytes 17825792 | tf_op jit(solution)/shard_map/reduce_scatter | solution.py:263
  1803.9 691.4 %reduce-scatter.32.cloned.1.call-start = ((), (), s32[]{:S(2)}) async-start(), calls=%async_computation.28 | async-start | bytes 4456448
  1818.2 752.8 %reduce-scatter.28.cloned.1.call-start = ((), (), s32[]{:S(2)}) async-start(), calls=%async_computation.26 | async-start | bytes 4456448
  1832.7 814.0 %reduce-scatter.30.cloned.1.call-start = ((), (), s32[]{:S(2)}) async-start(), calls=%async_computation.27 | async-start | bytes 4456448
  (49 other events, 498.6 us)
Sparse Core Ops, SparseCore 0:
  10.2 53.3 all-gather.15
  65.9 49.1 all-gather.13
  117.3 49.0 all-gather.9
  168.4 113.8 all-gather.17
  284.3 113.5 all-gather.11
  399.8 51.4 all-gather.19
  460.3 151.3 all-reduce.7
  614.1 126.8 all-gather.21
  743.5 124.9 all-gather.23
  870.6 128.5 all-gather.25
  1018.9 83.9 all-reduce.9
  1178.5 153.1 all-reduce.11
  1483.8 110.7 reduce-scatter.19
  1596.8 111.2 reduce-scatter.21
  1712.3 72.8 reduce-scatter.33
  1787.4 84.8 all-reduce.13
  1876.8 178.5 reduce-scatter.35
  2059.9 177.5 reduce-scatter.25
  2242.1 177.5 reduce-scatter.23
  2423.9 71.3 reduce-scatter.31
  2499.1 71.8 reduce-scatter.27
  2575.4 71.2 reduce-scatter.29
where the time goes:
time: 2670 us; the launch traced here: 2660 us
  waiting for transfers between devices  1890 us (71%)
  matrix products  465 us (17%)
  other arithmetic  131 us (5%)
  local copies, waits for them, and re-layouts  79.2 us (3%)
  blocking collectives  71.5 us (3%)
    unnamed x27, waiting for transfers between devices  361 us
    reduce_scatter x1, waiting for transfers between devices, body(): lax.psum_scatter(gate_grad.astype(jnp.bfloat16), ('dp', 'ctx'), scatter_d...  180 us
    reduce_scatter x1, waiting for transfers between devices, body(): lax.psum_scatter(up_grad.astype(jnp.bfloat16), ('dp', 'ctx'), scatter_dim...  179 us
    psum x1, waiting for transfers between devices, body(): lax.psum(contract_cols(grad_gate_low, full_gate) + contract_cols(grad_up_...  153 us
    psum x1, waiting for transfers between devices, body(): attn_rows = lax.psum(product(attended, full_out), 'tp')  149 us
    all_gather x1, waiting for transfers between devices, body(): lax.all_gather(shards[3], ('dp', 'ctx'), axis=0, tiled=True)  122 us
    all_gather x1, waiting for transfers between devices, body(): lax.all_gather(shards[4], ('dp', 'ctx'), axis=0, tiled=True)  107 us
    all_gather x1, waiting for transfers between devices, body(): lax.all_gather(shards[6], ('dp', 'ctx'), axis=1, tiled=True)  106 us
  transfers between devices with their start and end apart: 22, of which 20 were waited for; matrix products, arithmetic and copies ran while one was open for 15% of the time, Pallas kernels for 0%

commit v1 on v0

v1 whole, which is shorter than its diff:
```python
import functools
import math

import jax
import jax.numpy as jnp
from jax import lax
from jax.experimental import pallas as pl
from jax.experimental.pallas import tpu as pltpu
from jax.sharding import Mesh
from jax.sharding import PartitionSpec as P

HD = 128
EPSILON = 1e-06
ROPE_BASE = 500000.0
MASKED = -1e30
SCALING = HD**-0.5
LOG2E = math.log2(math.e)
BLOCK_K = 256
VMEM_LIMIT = 48 << 20
bf16 = jnp.bfloat16
f32 = jnp.float32


def cost(products, moved):
    return pl.CostEstimate(flops=products, bytes_accessed=moved // 2, transcendentals=0)


def dims(left, right, over):
    return lax.dot_general(left, right, (over, ((), ())), preferred_element_type=f32)


def product(left, right):
    return dims(left, right, ((1,), (0,)))


def contract_rows(left, right):
    return dims(left, right, ((0,), (0,)))


def contract_cols(left, right):
    return dims(left, right, ((1,), (1,)))


def key_steps(block, low, high, bk, per_block):
    end = block * per_block
    begin = jnp.minimum(low // bk, end)
    clear = jnp.minimum((high + bk - 1) // bk, end)
    return begin, clear, end


def diagonal(step, scores, start, first, bk):
    key = step * bk + lax.broadcasted_iota(jnp.int32, scores.shape, 0)
    place = step * bk + lax.broadcasted_iota(jnp.int32, scores.shape, 1)
    return jnp.where((key <= place) & (key + first >= start), scores, MASKED)


def attend_kernel(
    first_ref, low_ref, high_ref, start_ref, q_ref, k_ref, v_ref, o_ref, lse_ref, *, bk
):
    size = q_ref.shape[0]
    per_block = size // bk
    block = first_ref[0] + pl.program_id(2)
    sequence = pl.program_id(1)
    queries = q_ref[...]
    start = start_ref[0]

    def update(carry, scores, values):
        peak, total, acc = carry
        new_peak = jnp.maximum(peak, jnp.max(scores, axis=0, keepdims=True))
        weights = jnp.exp2(scores - new_peak)
        shrink = jnp.exp2(peak - new_peak)
        total = total * shrink + jnp.sum(weights, axis=0, keepdims=True)
        acc = acc * shrink + contract_rows(values, weights.astype(bf16))
        return new_peak, total, acc

    def clear_step(j, carry):
        rows = pl.ds(pl.multiple_of(j * bk, bk), bk)
        return update(carry, contract_cols(k_ref[rows, :], queries), v_ref[rows, :])

    def masked_step(j, carry):
        rows = pl.ds(pl.multiple_of(j * bk, bk), bk)
        scores = contract_cols(k_ref[rows, :], queries)
        key = j * bk + lax.broadcasted_iota(jnp.int32, (bk, 1), 0)
        return update(carry, jnp.where(key >= start, scores, MASKED), v_ref[rows, :])

    begin, clear, end = key_steps(
        block, low_ref[sequence, block], high_ref[sequence, block], bk, per_block
    )
    carry = (
        jnp.full((1, size), MASKED, f32),
        jnp.zeros((1, size), f32),
        jnp.zeros((HD, size), f32),
    )
    carry = lax.fori_loop(begin, clear, masked_step, carry)
    carry = lax.fori_loop(jnp.maximum(begin, clear), end, clear_step, carry)
    for step in range(per_block):
        cut = step * bk
        rows = pl.ds(pl.multiple_of(block * size + cut, bk), bk)
        scores = contract_cols(k_ref[rows, :], queries[cut:])
        scores = diagonal(step, scores, start[:, cut:], block * size, bk)
        right = update(tuple(part[:, cut:] for part in carry), scores, v_ref[rows, :])
        if cut:
            right = tuple(
                jnp.concatenate([part[:, :cut], new], axis=1) for part, new in zip(carry, right)
            )
        carry = right
    peak, total, acc = carry
    o_ref[...] = (acc / total).T.astype(bf16)
    lse_ref[0] = peak + jnp.log2(total)


def attend(first, starts, edges, heads, size, query, key, value):
    sequences, length = starts.shape
    slots = query[0].shape[0] // (sequences * size)
    rows = query[0].shape[0]

    def part(offset):
        return pl.BlockSpec((size, HD), lambda g, b, s, *refs: (b * slots + s, offset + g))

    def whole(offset):
        return pl.BlockSpec((length, HD), lambda g, b, s, *refs: (b, offset + g))

    return pl.pallas_call(
        functools.partial(attend_kernel, bk=min(BLOCK_K, size)),
        grid_spec=pltpu.PrefetchScalarGridSpec(
            num_scalar_prefetch=3,
            grid=(heads, sequences, slots),
            in_specs=[
                pl.BlockSpec((1, 1, size), lambda g, b, s, first, *refs: (b, 0, first[0] + s)),
                part(query[1]),
                whole(key[1]),
                whole(value[1]),
            ],
            out_specs=[
                part(0),
                pl.BlockSpec((1, 1, size), lambda g, b, s, *refs: (g, 0, b * slots + s)),
            ],
        ),
        out_shape=[
            jax.ShapeDtypeStruct((rows, heads * HD), bf16),
            jax.ShapeDtypeStruct((heads, 1, rows), f32),
        ],
        cost_estimate=cost(4 * HD * heads * rows * length, 0),
        compiler_params=pltpu.CompilerParams(vmem_limit_bytes=VMEM_LIMIT),
        name="attend",
    )(first, *edges, starts[:, None, :], query[0], key[0], value[0])


def attend_back_kernel(
    first_ref,
    low_ref,
    high_ref,
    start_ref,
    lse_ref,
    q_ref,
    o_ref,
    do_ref,
    k_ref,
    v_ref,
    dq_ref,
    dk_ref,
    dv_ref,
    dk_sum,
    dv_sum,
    *,
    bk,
):
    size = q_ref.shape[0]
    per_block = size // bk
    block = first_ref[0] + pl.program_id(2)
    sequence = pl.program_id(1)
    queries = q_ref[...]
    grads = do_ref[...]
    start = start_ref[0]
    lse = lse_ref[0]
    delta = jnp.sum((grads.astype(f32) * o_ref[...].astype(f32)).T, axis=0, keepdims=True)

    @pl.when(pl.program_id(2) == 0)
    def _():
        dk_sum[...] = jnp.zeros_like(dk_sum)
        dv_sum[...] = jnp.zeros_like(dv_sum)

    def update(dq, scores, rows, cut):
        probs = jnp.exp2(scores - lse[:, cut:])
        dv_sum[rows, :] += product(probs.astype(bf16), grads[cut:])
        dprobs = contract_cols(v_ref[rows, :], grads[cut:])
        dscores = (probs * (dprobs - delta[:, cut:])).astype(bf16)
        dk_sum[rows, :] += product(dscores, queries[cut:])
        return dq + contract_rows(k_ref[rows, :], dscores)

    def clear_step(j, dq):
        rows = pl.ds(pl.multiple_of(j * bk, bk), bk)
        return update(dq, contract_cols(k_ref[rows, :], queries), rows, 0)

    def masked_step(j, dq):
        rows = pl.ds(pl.multiple_of(j * bk, bk), bk)
        scores = contract_cols(k_ref[rows, :], queries)
        key = j * bk + lax.broadcasted_iota(jnp.int32, (bk, 1), 0)
        return update(dq, jnp.where(key >= start, scores, MASKED), rows, 0)

    begin, clear, end = key_steps(
        block, low_ref[sequence, block], high_ref[sequence, block], bk, per_block
    )
    dq = jnp.zeros((HD, size), f32)
    dq = lax.fori_loop(begin, clear, masked_step, dq)
    dq = lax.fori_loop(jnp.maximum(begin, clear), end, clear_step, dq)
    for step in range(per_block):
        cut = step * bk
        rows = pl.ds(pl.multiple_of(block * size + cut, bk), bk)
        scores = contract_cols(k_ref[rows, :], queries[cut:])
        scores = diagonal(step, scores, start[:, cut:], block * size, bk)
        right = update(dq[:, cut:], scores, rows, cut)
        dq = jnp.concatenate([dq[:, :cut], right], axis=1) if cut else right
    dq_ref[...] = (dq.T * SCALING).astype(bf16)

    @pl.when(pl.program_id(2) == pl.num_programs(2) - 1)
    def _():
        dk_ref[...] = (dk_sum[...] * (1.0 / LOG2E)).astype(bf16)
        dv_ref[...] = dv_sum[...].astype(bf16)


def attend_back(first, starts, edges, heads, size, lse, query, out, grad, key, value):
    sequences, length = starts.shape
    rows = query[0].shape[0]
    slots = rows // (sequences * size)

    def part(offset):
        return pl.BlockSpec((size, HD), lambda g, b, s, *refs: (b * slots + s, offset + g))

    def whole(offset):
        return pl.BlockSpec((length, HD), lambda g, b, s, *refs: (b, offset + g))

    return pl.pallas_call(
        functools.partial(attend_back_kernel, bk=min(BLOCK_K, size)),
        grid_spec=pltpu.PrefetchScalarGridSpec(
            num_scalar_prefetch=3,
            grid=(heads, sequences, slots),
            in_specs=[
                pl.BlockSpec((1, 1, size), lambda g, b, s, first, *refs: (b, 0, first[0] + s)),
                pl.BlockSpec((1, 1, size), lambda g, b, s, *refs: (g, 0, b * slots + s)),
                part(query[1]),
                part(0),
                part(0),
                whole(key[1]),
                whole(value[1]),
            ],
            out_specs=[part(0), whole(0), whole(0)],
            scratch_shapes=[pltpu.VMEM((length, HD), f32)] * 2,
        ),
        out_shape=[
            jax.ShapeDtypeStruct((rows, heads * HD), bf16),
            jax.ShapeDtypeStruct((sequences * length, heads * HD), bf16),
            jax.ShapeDtypeStruct((sequences * length, heads * HD), bf16),
        ],
        cost_estimate=cost(5 * HD * heads * rows * length, 0),
        compiler_params=pltpu.CompilerParams(vmem_limit_bytes=VMEM_LIMIT),
        name="attend_back",
    )(first, *edges, starts[:, None, :], lse, query[0], out, grad, key[0], value[0])


def turn_kernel(place_ref, raw_ref, scale_ref, gain_ref, cos_ref, sin_ref, out_ref, *, heads):
    for c in range(3):
        for h in range(heads):
            cols = slice((c * heads + h) * HD, (c * heads + h + 1) * HD)
            values = raw_ref[:, cols]
            if c < 2:
                values = values * scale_ref[c] * gain_ref[c, :, h * HD : (h + 1) * HD]
                values = values * cos_ref[...] + pltpu.roll(values, HD // 2, 1) * sin_ref[...]
            if c == 0:
                values = values * (SCALING * LOG2E)
            out_ref[:, cols] = values.astype(bf16)


def turn(place, raw, scales, gains, cosine, sine, heads):
    rows = raw.shape[0]
    size = rows // place.shape[0]
    return pl.pallas_call(
        functools.partial(turn_kernel, heads=heads),
        grid_spec=pltpu.PrefetchScalarGridSpec(
            num_scalar_prefetch=1,
            grid=(rows // size,),
            in_specs=[
                pl.BlockSpec((size, 3 * heads * HD), lambda i, place: (place[i], 0)),
                pl.BlockSpec((2, size, 1), lambda i, place: (0, i, 0)),
                pl.BlockSpec((2, 1, heads * HD), lambda i, place: (0, 0, 0)),
                pl.BlockSpec((size, HD), lambda i, place: (i, 0)),
                pl.BlockSpec((size, HD), lambda i, place: (i, 0)),
            ],
            out_specs=pl.BlockSpec((size, 3 * heads * HD), lambda i, place: (i, 0)),
        ),
        out_shape=jax.ShapeDtypeStruct(raw.shape, bf16),
        cost_estimate=cost(0, 20 * rows * heads * HD),
        compiler_params=pltpu.CompilerParams(vmem_limit_bytes=VMEM_LIMIT),
        name="turn",
    )(place, raw, scales, gains, cosine, sine)


def unturn_kernel(
    place_ref,
    dq_ref,
    dk_ref,
    raw_ref,
    scale_ref,
    gain_ref,
    cos_ref,
    sin_ref,
    out_ref,
    inner_ref,
    sum_ref,
    *,
    heads,
):
    @pl.when(pl.program_id(0) == 0)
    def _():
        sum_ref[...] = jnp.zeros_like(sum_ref)

    for c, grad_ref in enumerate((dq_ref, dk_ref)):
        inner = 0.0
        for h in range(heads):
            head = slice(h * HD, (h + 1) * HD)
            cols = slice((c * heads + h) * HD, (c * heads + h + 1) * HD)
            grad = grad_ref[:, head].astype(f32)
            normed = grad * cos_ref[...] - pltpu.roll(grad, HD // 2, 1) * sin_ref[...]
            unit = raw_ref[:, cols] * scale_ref[c]
            scaled = normed * gain_ref[c, :, head]
            out_ref[:, cols] = scaled
            inner = inner + jnp.sum(scaled * unit, axis=1, keepdims=True)
            sum_ref[c, :, head] += jnp.sum(normed * unit, axis=0, keepdims=True)
        inner_ref[c] = inner


def unturn(place, dq, dk, raw, scales, gains, cosine, sine, heads):
    rows = raw.shape[0]
    size = rows // place.shape[0]
    width = heads * HD
    return pl.pallas_call(
        functools.partial(unturn_kernel, heads=heads),
        grid_spec=pltpu.PrefetchScalarGridSpec(
            num_scalar_prefetch=1,
            grid=(rows // size,),
            in_specs=[
                pl.BlockSpec((size, width), lambda i, place: (i, 0)),
                pl.BlockSpec((size, width), lambda i, place: (i, 0)),
                pl.BlockSpec((size, 3 * width), lambda i, place: (place[i], 0)),
                pl.BlockSpec((2, size, 1), lambda i, place: (0, i, 0)),
                pl.BlockSpec((2, 1, width), lambda i, place: (0, 0, 0)),
                pl.BlockSpec((size, HD), lambda i, place: (i, 0)),
                pl.BlockSpec((size, HD), lambda i, place: (i, 0)),
            ],
            out_specs=[
                pl.BlockSpec((size, 2 * width), lambda i, place: (i, 0)),
                pl.BlockSpec((2, size, 1), lambda i, place: (0, i, 0)),
                pl.BlockSpec((2, 1, width), lambda i, place: (0, 0, 0)),
            ],
        ),
        out_shape=[
            jax.ShapeDtypeStruct((rows, 2 * width), f32),
            jax.ShapeDtypeStruct((2, rows, 1), f32),
            jax.ShapeDtypeStruct((2, 1, width), f32),
        ],
        cost_estimate=cost(0, 32 * rows * width),
        compiler_params=pltpu.CompilerParams(vmem_limit_bytes=VMEM_LIMIT),
        name="unturn",
    )(place, dq, dk, raw, scales, gains, cosine, sine)


def norm_back_kernel(
    place_ref, scaled_ref, raw_ref, scale_ref, inner_ref, dv_ref, out_ref, *, heads
):
    width = heads * HD
    for c in range(2):
        cols = slice(c * width, (c + 1) * width)
        unit = raw_ref[:, cols] * scale_ref[c]
        out_ref[:, cols] = (scale_ref[c] * (scaled_ref[:, cols] - unit * inner_ref[c])).astype(bf16)
    out_ref[:, 2 * width :] = dv_ref[...]


def norm_back(place, scaled, raw, scales, inner, dv, heads):
    rows = raw.shape[0]
    size = rows // place.shape[0]
    width = heads * HD
    return pl.pallas_call(
        functools.partial(norm_back_kernel, heads=heads),
        grid_spec=pltpu.PrefetchScalarGridSpec(
            num_scalar_prefetch=1,
            grid=(rows // size,),
            in_specs=[
                pl.BlockSpec((size, 2 * width), lambda i, place: (i, 0)),
                pl.BlockSpec((size, 3 * width), lambda i, place: (place[i], 0)),
                pl.BlockSpec((2, size, 1), lambda i, place: (0, i, 0)),
                pl.BlockSpec((2, size, 1), lambda i, place: (0, i, 0)),
                pl.BlockSpec((size, width), lambda i, place: (i, 0)),
            ],
            out_specs=pl.BlockSpec((size, 3 * width), lambda i, place: (place[i], 0)),
        ),
        out_shape=jax.ShapeDtypeStruct((rows, 3 * width), bf16),
        cost_estimate=cost(0, 24 * rows * width),
        compiler_params=pltpu.CompilerParams(vmem_limit_bytes=VMEM_LIMIT),
        name="norm_back",
    )(place, scaled, raw, scales, inner, dv)


def reorder_kernel(in_ref, out_ref, *, order):
    size = in_ref.shape[1] // len(order)
    for n, m in enumerate(order):
        out_ref[:, n * size : (n + 1) * size] = in_ref[:, m * size : (m + 1) * size]


def reorder(values, order):
    rows, width = values.shape
    size = math.gcd(rows, 192)
    spec = pl.BlockSpec((size, width), lambda i: (i, 0))
    return pl.pallas_call(
        functools.partial(reorder_kernel, order=order),
        grid=(rows // size,),
        in_specs=[spec],
        out_specs=spec,
        out_shape=jax.ShapeDtypeStruct(values.shape, values.dtype),
        cost_estimate=cost(0, 2 * values.size * values.dtype.itemsize),
        compiler_params=pltpu.CompilerParams(vmem_limit_bytes=VMEM_LIMIT),
        name="reorder",
    )(values)


def outer_kernel(left_a, left_b, right_a, right_b, out_ref):
    total = contract_rows(left_a[...], right_a[...]) + contract_rows(left_b[...], right_b[...])
    out_ref[...] = total.astype(bf16)


def outer(lefts, rights):
    rows, high = lefts[0].shape
    wide = rights[0].shape[1]
    tall, broad = math.gcd(high, 512), math.gcd(wide, 1024)
    left = pl.BlockSpec((rows, tall), lambda i, j: (0, i))
    right = pl.BlockSpec((rows, broad), lambda i, j: (0, j))
    return pl.pallas_call(
        outer_kernel,
        grid=(high // tall, wide // broad),
        in_specs=[left, left, right, right],
        out_specs=pl.BlockSpec((tall, broad), lambda i, j: (i, j)),
        out_shape=jax.ShapeDtypeStruct((high, wide), bf16),
        cost_estimate=cost(2 * rows * high * wide, 0),
        compiler_params=pltpu.CompilerParams(vmem_limit_bytes=VMEM_LIMIT),
        name="outer",
    )(*lefts, *rights)


def feed_kernel(hidden_ref, gate_ref, up_ref, gate_out, up_out, act_out):
    gate = product(hidden_ref[...], gate_ref[...])
    up = product(hidden_ref[...], up_ref[...])
    gate_out[...] = gate.astype(bf16)
    up_out[...] = up.astype(bf16)
    act_out[...] = (gate * jax.nn.sigmoid(gate) * up).astype(bf16)


def feed(hidden, gate_up):
    rows, width = hidden.shape
    units = gate_up.shape[1] // 2
    wide = math.gcd(units, 512)
    count = units // wide
    out = pl.BlockSpec((rows, wide), lambda j: (0, j))
    return pl.pallas_call(
        feed_kernel,
        grid=(count,),
        in_specs=[
            pl.BlockSpec((rows, width), lambda j: (0, 0)),
            pl.BlockSpec((width, wide), lambda j: (0, j)),
            pl.BlockSpec((width, wide), lambda j: (0, count + j)),
        ],
        out_specs=[out, out, out],
        out_shape=[jax.ShapeDtypeStruct((rows, units), bf16)] * 3,
        cost_estimate=cost(2 * rows * width * units, 0),
        compiler_params=pltpu.CompilerParams(vmem_limit_bytes=VMEM_LIMIT),
        name="feed",
    )(hidden, gate_up, gate_up)


def project_kernel(left_ref, right_ref, out_ref):
    out_ref[...] = contract_cols(left_ref[...], right_ref[...]).astype(bf16)


def project(left, right):
    rows, units = left.shape
    width = right.shape[0]
    wide = math.gcd(width, 512)
    return pl.pallas_call(
        project_kernel,
        grid=(width // wide,),
        in_specs=[
            pl.BlockSpec((rows, units), lambda j: (0, 0)),
            pl.BlockSpec((wide, units), lambda j: (j, 0)),
        ],
        out_specs=pl.BlockSpec((rows, wide), lambda j: (0, j)),
        out_shape=jax.ShapeDtypeStruct((rows, width), bf16),
        cost_estimate=cost(rows * units * width, 0),
        compiler_params=pltpu.CompilerParams(vmem_limit_bytes=VMEM_LIMIT),
        name="project",
    )(left, right)


def feed_back_kernel(grad_ref, down_ref, gate_ref, up_ref, gate_out, up_out):
    grad = product(grad_ref[...], down_ref[...])
    gate = gate_ref[...].astype(f32)
    sigmoid = jax.nn.sigmoid(gate)
    gate_out[...] = (
        grad * up_ref[...].astype(f32) * (sigmoid * (1.0 + gate * (1.0 - sigmoid)))
    ).astype(bf16)
    up_out[...] = (grad * (gate * sigmoid)).astype(bf16)


def feed_back(grad, down, gate, up):
    rows, width = grad.shape
    units = down.shape[1]
    wide = math.gcd(units, 512)
    part = pl.BlockSpec((rows, wide), lambda j: (0, j))
    return pl.pallas_call(
        feed_back_kernel,
        grid=(units // wide,),
        in_specs=[
            pl.BlockSpec((rows, width), lambda j: (0, 0)),
            pl.BlockSpec((width, wide), lambda j: (0, j)),
            part,
            part,
        ],
        out_specs=[part, part],
        out_shape=[jax.ShapeDtypeStruct((rows, units), bf16)] * 2,
        cost_estimate=cost(rows * width * units, 0),
        compiler_params=pltpu.CompilerParams(vmem_limit_bytes=VMEM_LIMIT),
        name="feed_back",
    )(grad, down, gate, up)


def project_both_kernel(gate_grad, up_grad, gate_ref, up_ref, out_ref):
    total = contract_cols(gate_grad[...], gate_ref[...]) + contract_cols(up_grad[...], up_ref[...])
    out_ref[...] = total.astype(bf16)


def project_both(gate_grad, up_grad, gate_up):
    rows, units = gate_grad.shape
    width = gate_up.shape[0]
    wide = math.gcd(width, 512)
    left = pl.BlockSpec((rows, units), lambda j: (0, 0))
    return pl.pallas_call(
        project_both_kernel,
        grid=(width // wide,),
        in_specs=[
            left,
            left,
            pl.BlockSpec((wide, units), lambda j: (j, 0)),
            pl.BlockSpec((wide, units), lambda j: (j, 1)),
        ],
        out_specs=pl.BlockSpec((rows, wide), lambda j: (0, j)),
        out_shape=jax.ShapeDtypeStruct((rows, width), bf16),
        cost_estimate=cost(2 * rows * units * width, 0),
        compiler_params=pltpu.CompilerParams(vmem_limit_bytes=VMEM_LIMIT),
        name="project_both",
    )(gate_grad, up_grad, gate_up, gate_up)


def tie_kernel(*refs):
    pass


def tie(values, *others):
    return pl.pallas_call(
        tie_kernel,
        in_specs=[pl.BlockSpec(memory_space=pl.ANY)] * (1 + len(others)),
        out_specs=pl.BlockSpec(memory_space=pl.ANY),
        out_shape=jax.ShapeDtypeStruct(values.shape, values.dtype),
        input_output_aliases={0: 0},
        cost_estimate=cost(0, 0),
        name="tie",
    )(values, *others)


def doc_starts(doc_ids):
    row_index = jnp.arange(doc_ids.shape[-1], dtype=jnp.int32)
    is_start = jnp.concatenate(
        [jnp.ones_like(doc_ids[:, :1], dtype=bool), doc_ids[:, 1:] != doc_ids[:, :-1]], axis=1
    )
    return lax.cummax(jnp.where(is_start, row_index[None, :], 0), axis=1)


def angles(places):
    frequency = ROPE_BASE ** (-(jnp.arange(HD // 2, dtype=f32) * 2.0 / HD))
    phases = places.astype(f32)[:, None] * frequency[None, :]
    cosine, sine = jnp.cos(phases), jnp.sin(phases)
    return (
        jnp.concatenate([cosine, cosine], axis=-1),
        jnp.concatenate([-sine, sine], axis=-1),
    )


def swap(values, axis):
    return lax.ppermute(values, axis, [(0, 1), (1, 0)])


def shift_ctx(values, steps, size):
    return lax.ppermute(values, "ctx", [(i, (i + steps) % size) for i in range(size)])


def by_source(received, me):
    size = len(received)
    turned = jnp.stack(received[::-1] + received[::-1])
    return lax.dynamic_slice_in_dim(turned, size - 1 - me, size, axis=0)


def in_order(index, mine, theirs):
    return jnp.where(index == 0, jnp.stack([mine, theirs]), jnp.stack([theirs, mine]))


def beside(index, mine, theirs):
    first = jnp.where(index == 0, mine, theirs)
    second = jnp.where(index == 0, theirs, mine)
    return jnp.concatenate([first, second], axis=1)


def lowered(values):
    return lax.reduce_precision(values, 8, 7).astype(bf16)


def body(
    tokens,
    segments,
    query_weight,
    key_weight,
    value_weight,
    out_weight,
    gate_weight,
    up_weight,
    down_weight,
    query_gain,
    key_gain,
    attn_gain,
    mlp_gain,
    cotangent,
    *,
    sizes,
):
    core = lax.axis_index("core")
    ctx = lax.axis_index("ctx")
    here_y = lax.axis_index("y")
    here_x = lax.axis_index("tp")
    n_ctx, n_tp = sizes["ctx"], sizes["tp"]
    rows, width = tokens.shape
    piece = query_weight.shape[0]
    local = query_weight.shape[1]
    att = local // 2
    half = width // 2
    short = rows // 2

    def column_half(values, index):
        size = values.shape[1] // 2
        return lax.dynamic_slice_in_dim(values, index * size, size, axis=1)

    def number(y, c, z):
        return (y * 2 + c) * n_ctx + z

    inward = [number(y, c, z) for y in range(2) for z in range(n_ctx) for c in range(2)]
    outward = [inward.index(n) for n in range(4 * n_ctx)]

    def gather(*shards, after=()):
        mine = jnp.concatenate([column_half(shard, core) for shard in shards], axis=1)
        theirs = jnp.concatenate([column_half(shard, 1 - core) for shard in shards], axis=1)
        pair = in_order(core, mine, swap(theirs, "core")).reshape(2 * piece, -1)
        if after:
            pair = tie(pair, *after)
        return lax.all_gather(pair, ("y", "ctx"), axis=0, tiled=True)

    def scatter(grad):
        return lax.psum_scatter(grad, ("y", "ctx"), scatter_dimension=0, tiled=True)

    def own_share(low):
        mine = lax.dynamic_slice_in_dim(low, core * piece, piece)
        theirs = swap(lax.dynamic_slice_in_dim(low, (1 - core) * piece, piece), "core")
        return beside(core, mine, theirs).astype(f32)

    def both(values):
        return jnp.concatenate([values, swap(values, "core")], axis=0)

    def open_sum(part):
        part = part.reshape(2, -1, width)
        total = part[0].astype(f32) + swap(part[1], "core").astype(f32)
        if n_tp == 2:
            low = lowered(total)
            return low, swap(low, "tp")
        low = lax.psum(total.astype(bf16), "tp")
        return low, jnp.zeros_like(low)

    def close_sum(low, other):
        return low.astype(f32) + other.astype(f32)

    def chunk(values, j):
        split = values.reshape(2, rows, -1)[:, j * short : (j + 1) * short]
        return split.reshape(2 * short, -1)

    def unchunk(parts):
        split = [part.reshape(2, short, -1) for part in parts]
        return jnp.concatenate(split, axis=1).reshape(2 * rows, -1)

    by_sequence = n_tp == 2 and (local // HD) % n_ctx == 0
    out_all = gather(out_weight.T)
    inner_tokens = reorder(tokens, inward)
    inner_cotangent = reorder(cotangent, inward)
    attn_gain, mlp_gain = (
        jnp.concatenate([gain[n * piece : (n + 1) * piece] for n in inward])
        for gain in (attn_gain, mlp_gain)
    )

    if by_sequence:
        heads = local // HD // n_ctx
        wide = heads * HD

        def shard_columns(index):
            return jnp.concatenate(
                [
                    lax.dynamic_slice_in_dim(shard, index * wide, wide, axis=1)
                    for shard in (query_weight, key_weight, value_weight)
                ],
                axis=1,
            )

        columns = [shard_columns(ctx)]
        for step in range(1, n_ctx):
            columns.append(shift_ctx(shard_columns(lax.rem(ctx + step, n_ctx)), step, n_ctx))
        weight = by_source(columns, ctx).reshape(n_ctx * piece, 3 * wide)
        weight = in_order(core, weight, swap(weight, "core")).reshape(half, 3 * wide)
        weight = in_order(here_y, weight, swap(weight, "y")).reshape(width, 3 * wide)

        sent = lax.dynamic_slice_in_dim(tokens, here_x * short, short)
        blocks = []
        for step in range(1, n_ctx):
            sent = shift_ctx(sent, 1, n_ctx)
            if step == 1:
                sent = tie(sent, *columns[1:])
            blocks.append(in_order(here_x, sent, swap(sent, "tp")).reshape(rows, width))
        blocks.append(tokens)
        raws = [product(block, weight) for block in blocks]
        raw = jnp.concatenate(raws)
        sums = [
            jnp.stack(
                [jnp.sum(jnp.square(r[:, c * wide : (c + 1) * wide]), axis=-1) for c in range(2)]
            )
            for r in raws
        ]
        squares = by_source([sums[-1]] + sums[:-1], ctx).swapaxes(0, 1).reshape(2, n_ctx * rows)
        size = math.gcd(rows, 384)
        order = jnp.arange(n_ctx * rows // size, dtype=jnp.int32)
        block_of, inside = order // (rows // size), order % (rows // size)
        place = lax.rem(ctx - block_of - 1 + n_ctx, n_ctx) * (rows // size) + inside
        place = place.astype(jnp.int32)

        starts = doc_starts(segments[None])
        places = jnp.arange(n_ctx * rows, dtype=jnp.int32) - starts[0]
        first_head = ctx * wide
        first_block = jnp.zeros((1,), jnp.int32)

        def sum_stats(stats):
            return lax.psum(stats, ("ctx", "tp"))

        ready = (sent,)
    else:
        heads = att // HD
        wide = att
        weight = gather(query_weight, key_weight, value_weight)
        raw = product(both(inner_tokens), weight)
        ready = ()
        squares = jnp.stack(
            [jnp.sum(jnp.square(raw[:, c * wide : (c + 1) * wide]), axis=-1) for c in range(2)]
        )
        place = jnp.arange(2 * rows // math.gcd(rows, 384), dtype=jnp.int32)
        starts = doc_starts(both(segments[None]))
        here = lax.dynamic_slice_in_dim(starts, ctx * rows, rows, axis=1)
        places = (ctx * rows + jnp.arange(rows, dtype=jnp.int32)[None, :] - here).reshape(-1)
        first_head = core * wide
        first_block = ctx.astype(jnp.int32)[None]

        def sum_stats(stats):
            split = stats.reshape(2, 2, rows)
            ordered = jnp.where(core == 0, split, split[:, ::-1])
            total = lax.psum(ordered, ("core", "tp"))
            return jnp.where(core == 0, total, total[:, ::-1]).reshape(stats.shape)

    gate_up_all = gather(gate_weight, up_weight, after=ready)
    down_all = gather(down_weight.T, after=ready)

    my_gains = jnp.stack(
        [
            lax.dynamic_slice_in_dim(query_gain, first_head, wide),
            lax.dynamic_slice_in_dim(key_gain, first_head, wide),
        ]
    )[:, None, :]
    cosine, sine = angles(places)
    edges = starts.reshape(starts.shape[0], n_ctx, rows)
    edges = (edges[:, :, 0], edges[:, :, -1])
    scales = lax.rsqrt(sum_stats(squares) / width + EPSILON)[:, :, None]
    turned = turn(place, raw, scales, my_gains, cosine, sine, heads)
    if by_sequence:
        keys, values = (turned, heads), (turned, 2 * heads)
    else:

        def whole_sequences(columns):
            line = lax.all_gather(columns.reshape(2, rows, wide), "ctx", axis=1, tiled=True)
            return line.reshape(-1, wide)

        keys = (whole_sequences(turned[:, wide : 2 * wide]), 0)
        values = (whole_sequences(turned[:, 2 * wide :]), 0)
    out_att, lse = attend(
        first_block, starts, edges, heads, rows, (turned, 0), keys, values
    )
    if by_sequence:
        received = []
        for step in range(n_ctx):
            start = lax.rem(ctx + step, n_ctx) * rows
            block = lax.dynamic_slice_in_dim(out_att, start, rows)
            received.append(shift_ctx(block, step, n_ctx) if step else block)
        twice = jnp.concatenate(received[::-1] + received[::-1], axis=1)
        own = lax.dynamic_slice_in_dim(twice, (n_ctx - 1 - ctx) * wide, local, axis=1)
        other = swap(lax.dynamic_slice_in_dim(own, (1 - core) * att, att, axis=1), "core")
        attended = jnp.concatenate([lax.dynamic_slice_in_dim(own, core * att, att, axis=1), other])
    else:
        attended = out_att

    spans = [slice(0, short), slice(short, rows)]
    attended = [chunk(attended, j) for j in range(2)]
    parts = [contract_cols(rows_part, out_all).astype(bf16) for rows_part in attended]
    attn_sums = [open_sum(part) for part in parts]

    def forward(j, attn_rows):
        attn_scale = lax.rsqrt(jnp.mean(attn_rows * attn_rows, axis=-1, keepdims=True) + EPSILON)
        attn_unit = attn_rows * attn_scale
        hidden_rows = inner_tokens[spans[j]].astype(f32) + attn_unit * attn_gain
        hidden_low = both(hidden_rows.astype(bf16))
        gate_rows, up_rows, act_low = feed(hidden_low, gate_up_all)
        part = project(act_low, down_all)
        return part, act_low, hidden_low, hidden_rows, attn_scale, attn_unit, gate_rows, up_rows

    def turn_norm(j, state, mlp_rows):
        hidden_rows = state[3]
        mlp_scale = lax.rsqrt(jnp.mean(mlp_rows * mlp_rows, axis=-1, keepdims=True) + EPSILON)
        mlp_unit = mlp_rows * mlp_scale
        output = (hidden_rows + mlp_unit * mlp_gain).astype(bf16)
        grad_out = inner_cotangent[spans[j]].astype(f32)
        gain_part = jnp.sum(grad_out * mlp_unit, axis=0)
        scaled_out = grad_out * mlp_gain
        inner_out = jnp.mean(scaled_out * mlp_unit, axis=-1, keepdims=True)
        grad_mlp_low = both((mlp_scale * (scaled_out - mlp_unit * inner_out)).astype(bf16))
        return grad_mlp_low, output, gain_part

    def turn_back(state, grad_mlp_low):
        gate_rows, up_rows = state[6:]
        grad_gate_low, grad_up_low = feed_back(grad_mlp_low, down_all, gate_rows, up_rows)
        back = project_both(grad_gate_low, grad_up_low, gate_up_all)
        return back, grad_gate_low, grad_up_low

    def close_back(j, state, back_rows):
        attn_scale, attn_unit = state[4], state[5]
        grad_hidden = inner_cotangent[spans[j]].astype(f32) + back_rows
        gain_part = jnp.sum(grad_hidden * attn_unit, axis=0)
        scaled_hidden = grad_hidden * attn_gain
        inner_hidden = jnp.mean(scaled_hidden * attn_unit, axis=-1, keepdims=True)
        grad_attn_low = both((attn_scale * (scaled_hidden - attn_unit * inner_hidden)).astype(bf16))
        grad_att = product(grad_attn_low, out_all).astype(bf16)
        return grad_att, grad_attn_low, grad_hidden, gain_part

    fore_a = forward(0, close_sum(*attn_sums[0]))
    mlp_a = open_sum(fore_a[0])
    fore_b = forward(1, close_sum(attn_sums[1][0], tie(attn_sums[1][1], fore_a[0])))
    mlp_b = open_sum(fore_b[0])
    norm_a = turn_norm(0, fore_a, close_sum(mlp_a[0], tie(mlp_a[1], fore_b[0])))
    back_a = turn_back(fore_a, norm_a[0])
    hid_a = open_sum(back_a[0])
    norm_b = turn_norm(1, fore_b, close_sum(mlp_b[0], tie(mlp_b[1], back_a[0])))
    down_grad = outer((norm_a[0], norm_b[0]), (fore_a[1], fore_b[1]))
    down_low = scatter(down_grad)
    back_b = turn_back(fore_b, tie(norm_b[0], down_grad))
    hid_b = open_sum(back_b[0])
    hiddens = (fore_a[2], fore_b[2])
    close_a = close_back(0, fore_a, close_sum(hid_a[0], tie(hid_a[1], back_b[0])))
    gate_grad = outer(hiddens, (back_a[1], back_b[1]))
    gate_low = scatter(gate_grad)
    close_b = close_back(1, fore_b, close_sum(hid_b[0], tie(hid_b[1], gate_grad)))
    up_low = scatter(outer(hiddens, (back_a[2], back_b[2])))
    out_theirs, out_mine = (
        outer(
            [
                lax.dynamic_slice_in_dim(close[1], index * half, half, axis=1)
                for close in (close_a, close_b)
            ],
            attended,
        )
        for index in (1 - here_y, here_y)
    )
    out_total = (out_mine.astype(f32) + swap(out_theirs, "y").astype(f32)).astype(bf16)
    out_sent = []
    for step in range(n_ctx):
        start = lax.rem(ctx + step, n_ctx) * 2 * piece
        block = lax.dynamic_slice_in_dim(out_total, start, 2 * piece)
        out_sent.append(shift_ctx(block, step, n_ctx) if step else block)
    out_low = sum(block.astype(f32) for block in out_sent).astype(bf16)
    grad_att = unchunk([close_a[0], close_b[0]])

    if by_sequence:
        own = beside(core, grad_att[:rows], swap(grad_att[rows:], "core"))
        received = []
        for step in range(n_ctx):
            start = lax.rem(ctx + step, n_ctx) * wide
            block = lax.dynamic_slice_in_dim(own, start, wide, axis=1)
            received.append(shift_ctx(block, step, n_ctx) if step else block)
        grad_att = by_source(received, ctx).reshape(n_ctx * rows, wide)
    dq, dk, dv = attend_back(
        first_block, starts, edges, heads, rows, lse, (turned, 0), out_att, grad_att, keys, values
    )
    if not by_sequence:

        def own_rows(grads):
            split = grads.reshape(2, n_ctx * rows, wide)
            low = lax.psum_scatter(split, "ctx", scatter_dimension=1, tiled=True)
            return low.reshape(2 * rows, wide)

        dk, dv = own_rows(dk), own_rows(dv)
    scaled, inner, gain_sums = unturn(
        place, dq, dk, raw, scales, my_gains, cosine, sine, heads
    )
    inner = sum_stats(inner[:, :, 0])[:, :, None] / width
    grad_qkv = norm_back(place, scaled, raw, scales, inner, dv, heads)

    if by_sequence:
        weight_halves = weight.reshape(2, half, 3 * wide)
        weight_mine = lax.dynamic_index_in_dim(weight_halves, here_x, 0, keepdims=False)
        weight_theirs = lax.dynamic_index_in_dim(weight_halves, 1 - here_x, 0, keepdims=False)
        grad_blocks = [grad_qkv[step * rows : (step + 1) * rows] for step in range(n_ctx)]
        others = [
            swap(contract_cols(block, weight_theirs).astype(bf16), "tp") for block in grad_blocks
        ]

        def y_half(index, after):
            tied = tie(grad_qkv, after)
            return sum(
                contract_rows(
                    lax.dynamic_slice_in_dim(block, index * half, half, axis=1),
                    tied[step * rows : (step + 1) * rows],
                )
                for step, block in enumerate(blocks)
            )

        terms = []
        for step in range(n_ctx):
            block = grad_blocks[step]
            if step == n_ctx - 1:
                block = tie(block, qkv_theirs)
            term = contract_cols(block, weight_mine) + others[step].astype(f32)
            if step < n_ctx - 1:
                low = term.astype(bf16)
                if step == 1:
                    qkv_theirs = y_half(1 - here_y, low).astype(bf16)
                term = shift_ctx(low, -1 - step, n_ctx).astype(f32)
            terms.append(term)
        dx = lowered(sum(terms))
        dx_rows = beside(here_x, dx, swap(dx, "tp")).astype(f32)

        qkv_total = y_half(here_y, qkv_theirs) + swap(qkv_theirs, "y").astype(f32)
        split = qkv_total.reshape(2, n_ctx * piece, 3 * wide)
        mine = lax.dynamic_index_in_dim(split, core, 0, keepdims=False)
        qkv_low = lax.dynamic_index_in_dim(split, 1 - core, 0, keepdims=False)
        qkv_low = (mine + swap(qkv_low.astype(bf16), "core").astype(f32)).astype(bf16)
        received = []
        for step in range(n_ctx):
            start = lax.rem(ctx + step, n_ctx) * piece
            block = lax.dynamic_slice_in_dim(qkv_low, start, piece)
            received.append(shift_ctx(block, step, n_ctx) if step else block)
        lines = by_source(received, ctx)
        qkv_shards = [
            jnp.concatenate([lines[n, :, c * wide : (c + 1) * wide] for n in range(n_ctx)], axis=1)
            .astype(f32)
            for c in range(3)
        ]
    else:
        grad_rows = [chunk(grad_qkv, j) for j in range(2)]
        token_rows = both(inner_tokens)
        token_rows = [chunk(token_rows, j) for j in range(2)]
        qkv_shards = [
            own_share(scatter(outer(token_rows, [r[:, c * wide : (c + 1) * wide] for r in grad_rows])))
            for c in range(3)
        ]
        sums = [open_sum(contract_cols(rows_part, weight).astype(bf16)) for rows_part in grad_rows]
        dx_rows = reorder(jnp.concatenate([close_sum(*parts) for parts in sums]), outward)
    grad_tokens = reorder(jnp.concatenate([close_a[2], close_b[2]]), outward) + dx_rows

    spread = jnp.zeros((2, local), f32)
    spread = lax.dynamic_update_slice(spread, gain_sums[:, 0], (jnp.int32(0), first_head))
    gains = jnp.concatenate([spread.reshape(-1), close_a[3] + close_b[3], norm_a[2] + norm_b[2]])
    if by_sequence:
        gains, down_low, gate_low, up_low = (
            tie(values, dx) for values in (gains, down_low, gate_low, up_low)
        )
    gains = lax.psum(gains, ("y", "core", "ctx"))
    cuts = [local, 2 * local, 2 * local + width]
    query_gain_grad, key_gain_grad, attn_gain_grad, mlp_gain_grad = jnp.split(gains, cuts)
    attn_gain_grad, mlp_gain_grad = (
        jnp.concatenate([gain[n * piece : (n + 1) * piece] for n in outward])
        for gain in (attn_gain_grad, mlp_gain_grad)
    )
    return (
        reorder(jnp.concatenate([norm_a[1], norm_b[1]]), outward),
        grad_tokens,
        *qkv_shards,
        own_share(out_low).T,
        own_share(gate_low),
        own_share(up_low),
        own_share(down_low).T,
        query_gain_grad,
        key_gain_grad,
        attn_gain_grad,
        mlp_gain_grad,
    )


def solution(mesh):
    sizes = {"y": mesh.shape["dp"] // 2, "core": 2, "ctx": mesh.shape["ctx"], "tp": mesh.shape["tp"]}
    split = Mesh(mesh.devices.reshape(tuple(sizes.values())), tuple(sizes))
    dp = ("y", "core")
    every = ("y", "core", "ctx")
    in_specs = (
        P(every, None),
        P(dp),
        P(every, "tp"),
        P(every, "tp"),
        P(every, "tp"),
        P("tp", every),
        P(every, "tp"),
        P(every, "tp"),
        P("tp", every),
        P("tp"),
        P("tp"),
        P(),
        P(),
        P(every, None),
    )
    out_specs = (
        P(every, None),
        P(every, None),
        P(every, "tp"),
        P(every, "tp"),
        P(every, "tp"),
        P("tp", every),
        P(every, "tp"),
        P(every, "tp"),
        P("tp", every),
        P("tp"),
        P("tp"),
        P(),
        P(),
    )
    return jax.shard_map(
        functools.partial(body, sizes=sizes),
        mesh=split,
        in_specs=in_specs,
        out_specs=out_specs,
        check_vma=False,
    )
```

time: 2670 us -> 1430 us (0.54)
  waiting for transfers between devices: 1890 us -> 602 us
  matrix products: 465 us -> 87.2 us
  Pallas kernels: 0 us -> 309 us
  blocking collectives: 71.5 us -> 130 us
  starting transfers between devices: 1.7 us -> 47.7 us
    all_gather x9 -> x3, waiting for transfers between devices: 663 us -> 0.01 us  [gather(): return lax.all_gather(pair, ('y', 'ctx'), axis=0, tiled=True)]
    ppermute x0 -> x61, waiting for transfers between devices: none -> 602 us  [the longest x21 344 us: shift_ctx(): lax.ppermute(values, 'ctx', [(i, (i + steps) % size) for i in range(size)])]
    reduce_scatter x4 -> x3, waiting for transfers between devices: 482 us -> 0.02 us  [scatter(): return lax.psum_scatter(grad, ('y', 'ctx'), scatter_dimension=0, tiled=True)]
    psum x4 -> x0, waiting for transfers between devices: 387 us -> none  [the longest x1 153 us: body(): lax.psum(contract_cols(grad_gate_low, full_gate) + contract_cols(grad_up_...]
    unnamed x27 -> x6, waiting for transfers between devices: 361 us -> 0.1 us
    dot_general x26 -> x24, matrix products: 431 us -> 87.2 us  [dims(): lax.dot_general(left, right, (over, ((), ())), preferred_element_type=f32)]
    pallas_call x0 -> x38, Pallas kernels: none -> 309 us  [the longest x5 64.4 us: outer(): pl.pallas_call(outer_kernel, grid=(high // tall, wide // broad), in_specs...]
    psum x3, blocking collectives: 71.5 us -> 130 us  [the longest x2 72.4 us: sum_stats(): return lax.psum(stats, ('ctx', 'tp'))]
  transfers between devices with their start and end apart: 22 -> 67, of which waited for: 20 -> 27; matrix products, arithmetic and copies ran while one was open for 15% -> 19% of each run, Pallas kernels for 0% -> 20%
where the time goes in v1:
time: 1430 us; the launch traced here: 1420 us
  waiting for transfers between devices  602 us (42%)
  Pallas kernels  309 us (22%)
  other arithmetic  152 us (11%)
  blocking collectives  130 us (9%)
  matrix products  87.2 us (6%)
  local copies, waits for them, and re-layouts  77.6 us (5%)
  starting transfers between devices  47.7 us (3%)
  between operations  16.5 us (1%)
    ppermute x21, waiting for transfers between devices, shift_ctx(): lax.ppermute(values, 'ctx', [(i, (i + steps) % size) for i in range(size)])  344 us
    ppermute x40, waiting for transfers between devices, swap(): return lax.ppermute(values, axis, [(0, 1), (1, 0)])  258 us
    dot_general x24, matrix products, dims(): lax.dot_general(left, right, (over, ((), ())), preferred_element_type=f32)  87.2 us
    psum x2, blocking collectives, sum_stats(): return lax.psum(stats, ('ctx', 'tp'))  72.4 us
    pallas_call x5, Pallas kernels, outer(): pl.pallas_call(outer_kernel, grid=(high // tall, wide // broad), in_specs...  64.4 us
    psum x1, blocking collectives, body(): gains = lax.psum(gains, ('y', 'core', 'ctx'))  57.9 us
    pallas_call x1, Pallas kernels, attend_back(): pl.pallas_call(functools.partial(attend_back_kernel, bk=min(BLOCK_K, size...  41.6 us
    pallas_call x2, Pallas kernels, feed(): pl.pallas_call(feed_kernel, grid=(count,), in_specs=[pl.BlockSpec((rows,...  38.2 us
  transfers between devices with their start and end apart: 67, of which 27 were waited for; matrix products, arithmetic and copies ran while one was open for 19% of the time, Pallas kernels for 20%

profile of v1, /device:TPU:0, one launch (start us, length us, event | category | flops | bytes accessed | tf_op | source)
XLA Modules:
  0.0 1421.8 jit_solution(10022053974745941006)
XLA Ops:
  26.9 35.0 %collective-permute-done.1.refs_1_ = bf16[128,768]{1,0:T(8,128)(2,1)S(1)} collective-permute-done((bf16[128,768]{1,0:T(8,128)(2,1)}, bf16[128,768]{1,0:T(8,128)(2,1)S(1)}, u32[]{:S(2)}, u32[]{:S(2)}) %collective-permute-start.1) | collective-permute-done | bytes 196640 | tf_op jit(solution)/shard_map/ppermute | solution.py:599
  75.2 51.6 %collective-permute-done.7 = bf16[384,2048]{1,0:T(8,128)(2,1)} collective-permute-done((bf16[384,2048]{1,0:T(8,128)(2,1)}, bf16[384,2048]{1,0:T(8,128)(2,1)}, u32[]{:S(2)}, u32[]{:S(2)}) %collective-permute-start.7) | collective-permute-done | bytes 1572896 | tf_op jit(solution)/shard_map/ppermute | solution.py:599
  131.7 31.8 %collective-permute-done.9.refs_1_ = bf16[384,2048]{1,0:T(8,128)(2,1)} collective-permute-done((bf16[384,2048]{1,0:T(8,128)(2,1)}, bf16[384,2048]{1,0:T(8,128)(2,1)}, u32[]{:S(2)}, u32[]{:S(2)}) %collective-permute-start.9) | collective-permute-done | bytes 1572896 | tf_op jit(solution)/shard_map/ppermute | solution.py:599
  186.0 43.9 %collective-permute-done.6 = bf16[1024,768]{1,0:T(8,128)(2,1)} collective-permute-done((bf16[1024,768]{1,0:T(8,128)(2,1)}, bf16[1024,768]{1,0:T(8,128)(2,1)}, u32[]{:S(2)}, u32[]{:S(2)}) %collective-permute-start.6) | collective-permute-done | bytes 1572896 | tf_op jit(solution)/shard_map/ppermute | solution.py:595
  252.0 19.0 %collective-permute-done.8 = bf16[384,2048]{1,0:T(8,128)(2,1)} collective-permute-done((bf16[384,2048]{1,0:T(8,128)(2,1)}, bf16[384,2048]{1,0:T(8,128)(2,1)}, u32[]{:S(2)}, u32[]{:S(2)}) %collective-permute-start.8) | collective-permute-done | bytes 1572896 | tf_op jit(solution)/shard_map/ppermute | solution.py:595
  285.6 17.3 %collective-permute-done.10 = bf16[384,2048]{1,0:T(8,128)(2,1)} collective-permute-done((bf16[384,2048]{1,0:T(8,128)(2,1)}, bf16[384,2048]{1,0:T(8,128)(2,1)}, u32[]{:S(2)}, u32[]{:S(2)}) %collective-permute-start.10) | collective-permute-done | bytes 1572896 | tf_op jit(solution)/shard_map/ppermute | solution.py:595
  317.0 38.0 %psum.21 = f32[2,3072]{1,0:T(2,128)S(1)} all-reduce(f32[2,3072]{1,0:T(2,128)S(1)} %bitcast.247), channel_id=1, replica_groups=mesh['y'=2,'core'=2,'ctx'=4,'tp'=2] {'ctx','tp'}, use_global_device_ids=true, to_apply=%region_10.11 | all-reduce | flops 6144 | bytes 49152 | tf_op jit(solution)/shard_map/psum | solution.py:759
  376.6 30.2 %attend.1 = (bf16[3072,256]{1,0:T(8,128)(2,1)S(1)}, f32[2,1,3072]{2,1,0:T(1,128)S(1)}) custom-call(s32[1]{0:T(128)} %constant.130.clone.1.first_ref, s32[1,4]{1,0:T(1,128)S(1)} %bitcast.212, s32[1,4]{1,0:T(1,128)S(1)} %bitcast.210, s32[1,1,3072]{2,1,0:T(1,128)S(1)} %reduce_window_max.36.start_ref, bf16[3072,768]{1,0:T(8,128)(2,1)} %turn.1.q_ref.k_ref.v_ref, ...), custom_call_target="tpu_custom_call" | custom-call | flops 9663676416 | tf_op jit(solution)/shard_map/attend/pallas_call | solution.py:123
  412.9 18.4 %collective-permute-done.11 = bf16[768,256]{1,0:T(8,128)(2,1)S(1)} collective-permute-done((bf16[768,256]{1,0:T(8,128)(2,1)}, bf16[768,256]{1,0:T(8,128)(2,1)S(1)}, u32[]{:S(2)}, u32[]{:S(2)}) %collective-permute-start.11) | collective-permute-done | bytes 393248 | tf_op jit(solution)/shard_map/ppermute | solution.py:599
  431.4 42.6 %collective-permute-done.12 = bf16[768,256]{1,0:T(8,128)(2,1)S(1)} collective-permute-done((bf16[768,256]{1,0:T(8,128)(2,1)S(1)}, bf16[768,256]{1,0:T(8,128)(2,1)S(1)}, u32[]{:S(2)}, u32[]{:S(2)}) %collective-permute-start.12) | collective-permute-done | bytes 393248 | tf_op jit(solution)/shard_map/ppermute | solution.py:599
  496.0 28.5 %collective-permute-done.17 = bf16[384,2048]{1,0:T(8,128)(2,1)} collective-permute-done((bf16[384,2048]{1,0:T(8,128)(2,1)}, bf16[384,2048]{1,0:T(8,128)(2,1)}, u32[]{:S(2)}, u32[]{:S(2)}) %collective-permute-start.17) | collective-permute-done | bytes 1572896 | tf_op jit(solution)/shard_map/ppermute | solution.py:595
  535.6 19.0 %feed.2 = (bf16[768,2048]{1,0:T(8,128)(2,1)S(1)}, bf16[768,2048]{1,0:T(8,128)(2,1)}, bf16[768,2048]{1,0:T(8,128)(2,1)}) custom-call(bf16[768,2048]{1,0:T(8,128)(2,1)} %pad_maximum_fusion.6.hidden_ref.left_a, bf16[2048,4096]{1,0:T(8,128)(2,1)} %all-gather.6.cloned.1.call-done.gate_ref.up_ref, bf16[2048,4096]{1,0:T(8,128)(2,1)} %all-gather.6.cloned.1.call-done.gate_ref.up_ref), custom_call_target="tpu_custom_call" | custom-call | flops 6442450944 | tf_op jit(solution)/shard_map/feed/pallas_call | solution.py:462
  583.2 19.2 %feed.3 = (bf16[768,2048]{1,0:T(8,128)(2,1)S(1)}, bf16[768,2048]{1,0:T(8,128)(2,1)}, bf16[768,2048]{1,0:T(8,128)(2,1)}) custom-call(bf16[768,2048]{1,0:T(8,128)(2,1)} %pad_maximum_fusion.7.hidden_ref.left_b, bf16[2048,4096]{1,0:T(8,128)(2,1)} %all-gather.6.cloned.1.call-done.gate_ref.up_ref, bf16[2048,4096]{1,0:T(8,128)(2,1)} %all-gather.6.cloned.1.call-done.gate_ref.up_ref), custom_call_target="tpu_custom_call" | custom-call | flops 6442450944 | tf_op jit(solution)/shard_map/feed/pallas_call | solution.py:462
  631.5 13.4 feed_back.2
  646.5 18.5 %project_both.2.refs_1_ = bf16[768,2048]{1,0:T(8,128)(2,1)S(1)} custom-call(bf16[768,2048]{1,0:T(8,128)(2,1)} %copy-done.21, bf16[768,2048]{1,0:T(8,128)(2,1)} %get-tuple-element.37.up_grad.right_a, bf16[2048,4096]{1,0:T(8,128)(2,1)} %all-gather.6.cloned.1.call-done.gate_ref.up_ref, bf16[2048,4096]{1,0:T(8,128)(2,1)} %all-gather.6.cloned.1.call-done.gate_ref.up_ref), custom_call_target="tpu_custom_call" | custom-call | flops 6442450944 | tf_op jit(solution)/shard_map/project_both/pallas_call | solution.py:543
  680.1 19.8 %outer.5.refs_1_ = bf16[2048,2048]{1,0:T(8,128)(2,1)} custom-call(bf16[768,2048]{1,0:T(8,128)(2,1)S(1)} %copy-done.15, bf16[768,2048]{1,0:T(8,128)(2,1)} %pad_maximum_fusion.10.left_b.refs_0_, bf16[768,2048]{1,0:T(8,128)(2,1)} %get-tuple-element.32.left_ref.right_a, bf16[768,2048]{1,0:T(8,128)(2,1)} %get-tuple-element.33.left_ref.right_b), custom_call_target="tpu_custom_call" | custom-call | flops 6442450944 | tf_op jit(solution)/shard_map/outer/pallas_call | solution.py:436
  700.0 13.5 feed_back.3
  715.2 20.0 %outer.9 = bf16[2048,2048]{1,0:T(8,128)(2,1)} custom-call(bf16[768,2048]{1,0:T(8,128)(2,1)S(1)} %copy-done.13, bf16[768,2048]{1,0:T(8,128)(2,1)} %pad_maximum_fusion.7.hidden_ref.left_b, bf16[768,2048]{1,0:T(8,128)(2,1)} %get-tuple-element.37.up_grad.right_a, bf16[768,2048]{1,0:T(8,128)(2,1)} %get-tuple-element.41.up_grad.right_b), custom_call_target="tpu_custom_call" | custom-call | flops 6442450944 | tf_op jit(solution)/shard_map/outer/pallas_call | solution.py:436
  737.1 18.5 %project_both.3.refs_1_ = bf16[768,2048]{1,0:T(8,128)(2,1)S(1)} custom-call(bf16[768,2048]{1,0:T(8,128)(2,1)} %copy-done.22, bf16[768,2048]{1,0:T(8,128)(2,1)} %get-tuple-element.41.up_grad.right_b, bf16[2048,4096]{1,0:T(8,128)(2,1)} %all-gather.6.cloned.1.call-done.gate_ref.up_ref, bf16[2048,4096]{1,0:T(8,128)(2,1)} %all-gather.6.cloned.1.call-done.gate_ref.up_ref), custom_call_target="tpu_custom_call" | custom-call | flops 6442450944 | tf_op jit(solution)/shard_map/project_both/pallas_call | solution.py:543
  764.3 20.0 %outer.6.refs_1_ = bf16[2048,2048]{1,0:T(8,128)(2,1)} custom-call(bf16[768,2048]{1,0:T(8,128)(2,1)S(1)} %copy-done.14, bf16[768,2048]{1,0:T(8,128)(2,1)} %pad_maximum_fusion.7.hidden_ref.left_b, bf16[768,2048]{1,0:T(8,128)(2,1)} %copy-done.21, bf16[768,2048]{1,0:T(8,128)(2,1)} %copy-done.22), custom_call_target="tpu_custom_call" | custom-call | flops 6442450944 | tf_op jit(solution)/shard_map/outer/pallas_call | solution.py:436
  784.4 13.6 collective-permute-done.30.refs_0_
  798.0 33.1 %collective-permute-done.33.refs_0_ = bf16[384,2048]{1,0:T(8,128)(2,1)} collective-permute-done((bf16[384,2048]{1,0:T(8,128)(2,1)}, bf16[384,2048]{1,0:T(8,128)(2,1)}, u32[]{:S(2)}, u32[]{:S(2)}) %collective-permute-start.33) | collective-permute-done | bytes 1572896 | tf_op jit(solution)/shard_map/ppermute | solution.py:595
  910.8 59.1 %collective-permute-done.38 = bf16[768,256]{1,0:T(8,128)(2,1)S(1)} collective-permute-done((bf16[768,256]{1,0:T(8,128)(2,1)S(1)}, bf16[768,256]{1,0:T(8,128)(2,1)S(1)}, u32[]{:S(2)}, u32[]{:S(2)}) %collective-permute-start.38) | collective-permute-done | bytes 393248 | tf_op jit(solution)/shard_map/ppermute | solution.py:599
  971.7 41.6 %attend_back.1 = (bf16[3072,256]{1,0:T(8,128)(2,1)S(1)}, bf16[3072,256]{1,0:T(8,128)(2,1)S(1)}, bf16[3072,256]{1,0:T(8,128)(2,1)S(1)}) custom-call(s32[1]{0:T(128)} %constant.130.clone.1.first_ref, s32[1,4]{1,0:T(1,128)S(1)} %bitcast.213, s32[1,4]{1,0:T(1,128)S(1)} %bitcast.211, s32[1,1,3072]{2,1,0:T(1,128)S(1)} %reduce_window_max.36.start_ref, ...), custom_call_target="tpu_custom_call" | custom-call | flops 12079595520 | tf_op jit(solution)/shard_map/attend_back/pallas_call | solution.py:233
  1014.4 13.2 unturn.1
  1030.6 34.4 %psum.22 = f32[2,3072]{1,0:T(2,128)S(1)} all-reduce(f32[2,3072]{1,0:T(2,128)S(1)} %reduce.4), channel_id=1, replica_groups=mesh['y'=2,'core'=2,'ctx'=4,'tp'=2] {'ctx','tp'}, use_global_device_ids=true, to_apply=%region_19.20 | all-reduce | flops 6144 | bytes 49152 | tf_op jit(solution)/shard_map/psum | solution.py:759
  1068.7 11.7 norm_back.1.refs_0_
  1101.4 20.5 %collective-permute-done.40 = bf16[768,1024]{1,0:T(8,128)(2,1)} collective-permute-done((bf16[768,1024]{1,0:T(8,128)(2,1)}, bf16[768,1024]{1,0:T(8,128)(2,1)}, u32[]{:S(2)}, u32[]{:S(2)}) %collective-permute-start.40) | collective-permute-done | bytes 1572896 | tf_op jit(solution)/shard_map/ppermute | solution.py:595
  1126.9 28.8 %collective-permute-done.42 = bf16[768,1024]{1,0:T(8,128)(2,1)} collective-permute-done((bf16[768,1024]{1,0:T(8,128)(2,1)}, bf16[768,1024]{1,0:T(8,128)(2,1)}, u32[]{:S(2)}, u32[]{:S(2)}) %collective-permute-start.42) | collective-permute-done | bytes 1572896 | tf_op jit(solution)/shard_map/ppermute | solution.py:595
  1159.7 29.7 %collective-permute-done.44 = bf16[768,1024]{1,0:T(8,128)(2,1)} collective-permute-done((bf16[768,1024]{1,0:T(8,128)(2,1)S(1)}, bf16[768,1024]{1,0:T(8,128)(2,1)}, u32[]{:S(2)}, u32[]{:S(2)}) %collective-permute-start.44) | collective-permute-done | bytes 1572896 | tf_op jit(solution)/shard_map/ppermute | solution.py:595
  1219.5 74.2 %collective-permute-done.43 = bf16[768,1024]{1,0:T(8,128)(2,1)} collective-permute-done((bf16[768,1024]{1,0:T(8,128)(2,1)}, bf16[768,1024]{1,0:T(8,128)(2,1)}, u32[]{:S(2)}, u32[]{:S(2)}) %collective-permute-start.43) | collective-permute-done | bytes 1572896 | tf_op jit(solution)/shard_map/ppermute | solution.py:599
  1308.8 57.9 %psum.23 = f32[6144]{0:T(1024)S(1)} all-reduce(f32[6144]{0:T(1024)S(1)} %copy-done.81), channel_id=1, replica_groups=mesh['y'=2,'core'=2,'ctx'=4,'tp'=2] {'y','core','ctx'}, use_global_device_ids=true, to_apply=%region_27.28 | all-reduce | flops 6144 | bytes 49152 | tf_op jit(solution)/shard_map/psum | solution.py:997
  (596 shorter events, 469.2 us)
Async XLA Ops:
  7.2 471.4 %all-gather.4.cloned.1.call-start = ((), (), s32[]{:S(2)}) async-start(), calls=%async_computation.3 | async-start | bytes 2359296 | tf_op jit(solution)/shard_map/all_gather | solution.py:668
  8.9 60.6 %collective-permute-start = (bf16[384,2048]{1,0:T(8,128)(2,1)S(1)}, bf16[384,2048]{1,0:T(8,128)(2,1)}, u32[]{:S(2)}, u32[]{:S(2)}) collective-permute-start(bf16[384,2048]{1,0:T(8,128)(2,1)S(1)} %constant_dynamic-slice_fusion.35), channel_id=1, source_target_pairs={{0,2},{2,4},{4,6},{6,0},{1,3},{3,5},{5,7},{7,1},{8,10},{10,12},{12... | collective-permute-start | bytes 4718600 | tf_op jit(solution)/shard_map/ppermute | solution.py:599
  14.0 47.9 %collective-permute-start.1 = (bf16[128,768]{1,0:T(8,128)(2,1)}, bf16[128,768]{1,0:T(8,128)(2,1)S(1)}, u32[]{:S(2)}, u32[]{:S(2)}) collective-permute-start(bf16[128,768]{1,0:T(8,128)(2,1)} %pad_maximum_fusion.20), channel_id=1, source_target_pairs={{0,2},{2,4},{4,6},{6,0},{1,3},{3,5},{5,7},{7,1},{8,10},{10,12},{12... | collective-permute-start | bytes 589832 | tf_op jit(solution)/shard_map/ppermute | solution.py:599
  18.7 50.8 %collective-permute-start.2 = (bf16[128,768]{1,0:T(8,128)(2,1)}, bf16[128,768]{1,0:T(8,128)(2,1)S(1)}, u32[]{:S(2)}, u32[]{:S(2)}) collective-permute-start(bf16[128,768]{1,0:T(8,128)(2,1)} %pad_maximum_fusion.21), channel_id=1, source_target_pairs={{0,4},{2,6},{4,0},{6,2},{1,5},{3,7},{5,1},{7,3},{8,12},{10,14},{12... | collective-permute-start | bytes 589832 | tf_op jit(solution)/shard_map/ppermute | solution.py:599
  21.3 48.2 %collective-permute-start.3 = (bf16[128,768]{1,0:T(8,128)(2,1)}, bf16[128,768]{1,0:T(8,128)(2,1)S(1)}, u32[]{:S(2)}, u32[]{:S(2)}) collective-permute-start(bf16[128,768]{1,0:T(8,128)(2,1)} %pad_maximum_fusion.22), channel_id=1, source_target_pairs={{0,6},{2,0},{4,2},{6,4},{1,7},{3,1},{5,3},{7,5},{8,14},{10,8},{12,... | collective-permute-start | bytes 589832 | tf_op jit(solution)/shard_map/ppermute | solution.py:599
  26.9 508.7 %all-gather.6.cloned.1.call-start = ((), (), s32[]{:S(2)}) async-start(), calls=%async_computation.4 | async-start | bytes 18874368 | tf_op jit(solution)/shard_map/all_gather | solution.py:668
  70.2 56.6 %collective-permute-start.7 = (bf16[384,2048]{1,0:T(8,128)(2,1)}, bf16[384,2048]{1,0:T(8,128)(2,1)}, u32[]{:S(2)}, u32[]{:S(2)}) collective-permute-start(bf16[384,2048]{1,0:T(8,128)(2,1)} %tie.16), channel_id=1, source_target_pairs={{0,2},{2,4},{4,6},{6,0},{1,3},{3,5},{5,7},{7,1},{8,10},{10,12},{12... | collective-permute-start | bytes 4718600 | tf_op jit(solution)/shard_map/ppermute | solution.py:599
  163.6 392.8 %all-gather.8.cloned.1.call-start = ((), (), s32[]{:S(2)}) async-start(), calls=%async_computation.5 | async-start | bytes 9437184 | tf_op jit(solution)/shard_map/all_gather | solution.py:668
  170.8 59.1 %collective-permute-start.6 = (bf16[1024,768]{1,0:T(8,128)(2,1)}, bf16[1024,768]{1,0:T(8,128)(2,1)}, u32[]{:S(2)}, u32[]{:S(2)}) collective-permute-start(bf16[1024,768]{1,0:T(8,128)(2,1)} %bitcast.15), channel_id=1, source_target_pairs={{0,16},{16,0},{1,17},{17,1},{2,18},{18,2},{3,19},{19,3},{4,20},{20... | collective-permute-start | bytes 4718600 | tf_op jit(solution)/shard_map/ppermute | solution.py:595
  179.4 58.5 %collective-permute-start.4 = (bf16[384,2048]{1,0:T(8,128)(2,1)}, bf16[384,2048]{1,0:T(8,128)(2,1)}, u32[]{:S(2)}, u32[]{:S(2)}) collective-permute-start(bf16[384,2048]{1,0:T(8,128)(2,1)} %tie.16), channel_id=1, source_target_pairs={{0,1},{1,0},{2,3},{3,2},{4,5},{5,4},{6,7},{7,6},{8,9},{9,8},{10,11... | collective-permute-start | bytes 4718600 | tf_op jit(solution)/shard_map/ppermute | solution.py:595
  241.4 61.5 %collective-permute-start.10 = (bf16[384,2048]{1,0:T(8,128)(2,1)}, bf16[384,2048]{1,0:T(8,128)(2,1)}, u32[]{:S(2)}, u32[]{:S(2)}) collective-permute-start(bf16[384,2048]{1,0:T(8,128)(2,1)} %collective-permute-done.9.refs_1_), channel_id=1, source_target_pairs={{0,1},{1,0},{2,3},{3,2},{4,5},{5,4},{6,7},{7,6},{8,9},{9,8},{10,11... | collective-permute-start | bytes 4718600 | tf_op jit(solution)/shard_map/ppermute | solution.py:595
  285.5 1106.4 %reduce-scatter.8.cloned.1.call-start = ((), (), s32[]{:S(2)}) async-start(), calls=%async_computation.8 | async-start | bytes 9437184 | tf_op jit(solution)/shard_map/reduce_scatter | solution.py:671
  408.3 65.6 %collective-permute-start.12 = (bf16[768,256]{1,0:T(8,128)(2,1)S(1)}, bf16[768,256]{1,0:T(8,128)(2,1)S(1)}, u32[]{:S(2)}, u32[]{:S(2)}) collective-permute-start(bf16[768,256]{1,0:T(8,128)(2,1)S(1)} %get-tuple-element.148), channel_id=1, source_target_pairs={{0,4},{2,6},{4,0},{6,2},{1,5},{3,7},{5,1},{7,3},{8,12},{10,14},{12... | collective-permute-start | bytes 1179656 | tf_op jit(solution)/shard_map/ppermute | solution.py:599
  410.9 63.1 %collective-permute-start.13 = (bf16[768,256]{1,0:T(8,128)(2,1)S(1)}, bf16[768,256]{1,0:T(8,128)(2,1)S(1)}, u32[]{:S(2)}, u32[]{:S(2)}) collective-permute-start(bf16[768,256]{1,0:T(8,128)(2,1)S(1)} %get-tuple-element.147), channel_id=1, source_target_pairs={{0,2},{2,4},{4,6},{6,0},{1,3},{3,5},{5,7},{7,1},{8,10},{10,12},{12... | collective-permute-start | bytes 1179656 | tf_op jit(solution)/shard_map/ppermute | solution.py:599
  627.8 38.9 %collective-permute-start.27 = (bf16[384,2048]{1,0:T(8,128)(2,1)S(1)}, bf16[384,2048]{1,0:T(8,128)(2,1)}, u32[]{:S(2)}, u32[]{:S(2)}) collective-permute-start(bf16[384,2048]{1,0:T(8,128)(2,1)S(1)} %reduce-precision_convert_fusion.3), channel_id=1, source_target_pairs={{0,1},{1,0},{2,3},{3,2},{4,5},{5,4},{6,7},{7,6},{8,9},{9,8},{10,11... | collective-permute-start | bytes 4718600 | tf_op jit(solution)/shard_map/ppermute | solution.py:595
  700.0 700.9 %reduce-scatter.6.cloned.1.call-start = ((), (), s32[]{:S(2)}) async-start(), calls=%async_computation.7 | async-start | bytes 9437184 | tf_op jit(solution)/shard_map/reduce_scatter | solution.py:671
  735.2 667.4 %reduce-scatter.4.cloned.1.call-start = ((), (), s32[]{:S(2)}) async-start(), calls=%async_computation.6 | async-start | bytes 9437184 | tf_op jit(solution)/shard_map/reduce_scatter | solution.py:671
  763.5 67.6 %collective-permute-start.33 = (bf16[384,2048]{1,0:T(8,128)(2,1)}, bf16[384,2048]{1,0:T(8,128)(2,1)}, u32[]{:S(2)}, u32[]{:S(2)}) collective-permute-start(bf16[384,2048]{1,0:T(8,128)(2,1)} %reduce-precision_convert_fusion.1), channel_id=1, source_target_pairs={{0,1},{1,0},{2,3},{3,2},{4,5},{5,4},{6,7},{7,6},{8,9},{9,8},{10,11... | collective-permute-start | bytes 4718600 | tf_op jit(solution)/shard_map/ppermute | solution.py:595
  884.4 85.4 %collective-permute-start.38 = (bf16[768,256]{1,0:T(8,128)(2,1)S(1)}, bf16[768,256]{1,0:T(8,128)(2,1)S(1)}, u32[]{:S(2)}, u32[]{:S(2)}) collective-permute-start(bf16[768,256]{1,0:T(8,128)(2,1)S(1)} %get-tuple-element.144), channel_id=1, source_target_pairs={{0,4},{2,6},{4,0},{6,2},{1,5},{3,7},{5,1},{7,3},{8,12},{10,14},{12... | collective-permute-start | bytes 1179656 | tf_op jit(solution)/shard_map/ppermute | solution.py:599
  886.3 83.7 %collective-permute-start.39 = (bf16[768,256]{1,0:T(8,128)(2,1)S(1)}, bf16[768,256]{1,0:T(8,128)(2,1)S(1)}, u32[]{:S(2)}, u32[]{:S(2)}) collective-permute-start(bf16[768,256]{1,0:T(8,128)(2,1)S(1)} %get-tuple-element.142), channel_id=1, source_target_pairs={{0,2},{2,4},{4,6},{6,0},{1,3},{3,5},{5,7},{7,1},{8,10},{10,12},{12... | collective-permute-start | bytes 1179656 | tf_op jit(solution)/shard_map/ppermute | solution.py:599
  901.3 191.6 %collective-permute-start.54 = (bf16[256,512]{1,0:T(8,128)(2,1)}, bf16[256,512]{1,0:T(8,128)(2,1)}, u32[]{:S(2)}, u32[]{:S(2)}) collective-permute-start(bf16[256,512]{1,0:T(8,128)(2,1)} %get-tuple-element.150), channel_id=1, source_target_pairs={{0,2},{2,4},{4,6},{6,0},{1,3},{3,5},{5,7},{7,1},{8,10},{10,12},{12... | collective-permute-start | bytes 786440 | tf_op jit(solution)/shard_map/ppermute | solution.py:599
  901.3 191.6 %collective-permute-start.55 = (bf16[256,512]{1,0:T(8,128)(2,1)}, bf16[256,512]{1,0:T(8,128)(2,1)}, u32[]{:S(2)}, u32[]{:S(2)}) collective-permute-start(bf16[256,512]{1,0:T(8,128)(2,1)} %get-tuple-element.152), channel_id=1, source_target_pairs={{0,4},{2,6},{4,0},{6,2},{1,5},{3,7},{5,1},{7,3},{8,12},{10,14},{12... | collective-permute-start | bytes 786440 | tf_op jit(solution)/shard_map/ppermute | solution.py:599
  910.7 182.2 %collective-permute-start.56 = (bf16[256,512]{1,0:T(8,128)(2,1)S(1)}, bf16[256,512]{1,0:T(8,128)(2,1)}, u32[]{:S(2)}, u32[]{:S(2)}) collective-permute-start(bf16[256,512]{1,0:T(8,128)(2,1)S(1)} %get-tuple-element.151), channel_id=1, source_target_pairs={{0,6},{2,0},{4,2},{6,4},{1,7},{3,1},{5,3},{7,5},{8,14},{10,8},{12,... | collective-permute-start | bytes 786440 | tf_op jit(solution)/shard_map/ppermute | solution.py:599
  1086.9 68.8 %collective-permute-start.42 = (bf16[768,1024]{1,0:T(8,128)(2,1)}, bf16[768,1024]{1,0:T(8,128)(2,1)}, u32[]{:S(2)}, u32[]{:S(2)}) collective-permute-start(bf16[768,1024]{1,0:T(8,128)(2,1)} %convolution_convert_fusion.4), channel_id=1, source_target_pairs={{0,1},{1,0},{2,3},{3,2},{4,5},{5,4},{6,7},{7,6},{8,9},{9,8},{10,11... | collective-permute-start | bytes 4718600 | tf_op jit(solution)/shard_map/ppermute | solution.py:595
  1092.9 96.5 %collective-permute-start.44 = (bf16[768,1024]{1,0:T(8,128)(2,1)S(1)}, bf16[768,1024]{1,0:T(8,128)(2,1)}, u32[]{:S(2)}, u32[]{:S(2)}) collective-permute-start(bf16[768,1024]{1,0:T(8,128)(2,1)S(1)} %convolution_convert_fusion.3), channel_id=1, source_target_pairs={{0,1},{1,0},{2,3},{3,2},{4,5},{5,4},{6,7},{7,6},{8,9},{9,8},{10,11... | collective-permute-start | bytes 4718600 | tf_op jit(solution)/shard_map/ppermute | solution.py:595
  1097.7 121.8 %collective-permute-start.46 = (bf16[768,1024]{1,0:T(8,128)(2,1)}, bf16[768,1024]{1,0:T(8,128)(2,1)}, u32[]{:S(2)}, u32[]{:S(2)}) collective-permute-start(bf16[768,1024]{1,0:T(8,128)(2,1)} %convolution_convert_fusion.2), channel_id=1, source_target_pairs={{0,1},{1,0},{2,3},{3,2},{4,5},{5,4},{6,7},{7,6},{8,9},{9,8},{10,11... | collective-permute-start | bytes 4718600 | tf_op jit(solution)/shard_map/ppermute | solution.py:595
  1126.9 92.6 %collective-permute-start.41 = (bf16[768,1024]{1,0:T(8,128)(2,1)}, bf16[768,1024]{1,0:T(8,128)(2,1)}, u32[]{:S(2)}, u32[]{:S(2)}) collective-permute-start(bf16[768,1024]{1,0:T(8,128)(2,1)} %add_convert_fusion.3), channel_id=1, source_target_pairs={{0,6},{2,0},{4,2},{6,4},{1,7},{3,1},{5,3},{7,5},{8,14},{10,8},{12,... | collective-permute-start | bytes 4718600 | tf_op jit(solution)/shard_map/ppermute | solution.py:599
  1159.7 134.1 %collective-permute-start.43 = (bf16[768,1024]{1,0:T(8,128)(2,1)}, bf16[768,1024]{1,0:T(8,128)(2,1)}, u32[]{:S(2)}, u32[]{:S(2)}) collective-permute-start(bf16[768,1024]{1,0:T(8,128)(2,1)} %add_convert_fusion.2.refs_1_), channel_id=1, source_target_pairs={{0,4},{2,6},{4,0},{6,2},{1,5},{3,7},{5,1},{7,3},{8,12},{10,14},{12... | collective-permute-start | bytes 4718600 | tf_op jit(solution)/shard_map/ppermute | solution.py:599
  1193.3 100.4 %collective-permute-start.45 = (bf16[768,1024]{1,0:T(8,128)(2,1)}, bf16[768,1024]{1,0:T(8,128)(2,1)}, u32[]{:S(2)}, u32[]{:S(2)}) collective-permute-start(bf16[768,1024]{1,0:T(8,128)(2,1)} %add_convert_fusion.1), channel_id=1, source_target_pairs={{0,2},{2,4},{4,6},{6,0},{1,3},{3,5},{5,7},{7,1},{8,10},{10,12},{12... | collective-permute-start | bytes 4718600 | tf_op jit(solution)/shard_map/ppermute | solution.py:599
  1207.1 93.8 %collective-permute-start.48 = (bf16[1024,768]{1,0:T(8,128)(2,1)S(1)}, bf16[1024,768]{1,0:T(8,128)(2,1)}, u32[]{:S(2)}, u32[]{:S(2)}) collective-permute-start(bf16[1024,768]{1,0:T(8,128)(2,1)S(1)} %copy-done.39), channel_id=1, source_target_pairs={{0,16},{16,0},{1,17},{17,1},{2,18},{18,2},{3,19},{19,3},{4,20},{20... | collective-permute-start | bytes 4718600 | tf_op jit(solution)/shard_map/ppermute | solution.py:595
  1299.4 90.5 %collective-permute-start.47 = (bf16[768,1024]{1,0:T(8,128)(2,1)}, bf16[768,1024]{1,0:T(8,128)(2,1)}, u32[]{:S(2)}, u32[]{:S(2)}) collective-permute-start(bf16[768,1024]{1,0:T(8,128)(2,1)} %reduce-precision_convert_fusion.refs_1_), channel_id=1, source_target_pairs={{0,1},{1,0},{2,3},{3,2},{4,5},{5,4},{6,7},{7,6},{8,9},{9,8},{10,11... | collective-permute-start | bytes 4718600 | tf_op jit(solution)/shard_map/ppermute | solution.py:595
  1308.8 58.7 %collective-permute-start.49 = (bf16[512,768]{1,0:T(8,128)(2,1)}, bf16[512,768]{1,0:T(8,128)(2,1)}, u32[]{:S(2)}, u32[]{:S(2)}) collective-permute-start(bf16[512,768]{1,0:T(8,128)(2,1)} %fusion.83), channel_id=1, source_target_pairs={{0,8},{8,0},{1,9},{9,1},{2,10},{10,2},{3,11},{11,3},{4,12},{12,4},... | collective-permute-start | bytes 2359304 | tf_op jit(solution)/shard_map/ppermute | solution.py:595
  (125 other events, 1991.8 us)
Sparse Core Ops, SparseCore 0:
  27.0 85.3 all-gather.3
  163.7 233.3 all-gather.5
  399.2 150.7 all-gather.7
  700.1 145.8 reduce-scatter.7
  849.9 194.3 reduce-scatter.5
  1047.7 237.7 reduce-scatter.3

commit v2 on v1

--- a/solution.py
+++ b/solution.py
@@ -453,49 +453,48 @@
     act_out[...] = (gate * jax.nn.sigmoid(gate) * up).astype(bf16)
 
 
-def feed(hidden, gate_up):
+def feed(hidden, gate, up_down):
     rows, width = hidden.shape
-    units = gate_up.shape[1] // 2
+    units = gate.shape[1]
     wide = math.gcd(units, 512)
-    count = units // wide
     out = pl.BlockSpec((rows, wide), lambda j: (0, j))
     return pl.pallas_call(
         feed_kernel,
-        grid=(count,),
+        grid=(units // wide,),
         in_specs=[
             pl.BlockSpec((rows, width), lambda j: (0, 0)),
             pl.BlockSpec((width, wide), lambda j: (0, j)),
-            pl.BlockSpec((width, wide), lambda j: (0, count + j)),
+            pl.BlockSpec((width, wide), lambda j: (0, j)),
         ],
         out_specs=[out, out, out],
         out_shape=[jax.ShapeDtypeStruct((rows, units), bf16)] * 3,
         cost_estimate=cost(2 * rows * width * units, 0),
         compiler_params=pltpu.CompilerParams(vmem_limit_bytes=VMEM_LIMIT),
         name="feed",
-    )(hidden, gate_up, gate_up)
+    )(hidden, gate, up_down)
 
 
 def project_kernel(left_ref, right_ref, out_ref):
     out_ref[...] = contract_cols(left_ref[...], right_ref[...]).astype(bf16)
 
 
-def project(left, right):
-    rows, units = left.shape
-    width = right.shape[0]
+def project(act, up_down):
+    rows, units = act.shape
+    width = up_down.shape[0]
     wide = math.gcd(width, 512)
     return pl.pallas_call(
         project_kernel,
         grid=(width // wide,),
         in_specs=[
             pl.BlockSpec((rows, units), lambda j: (0, 0)),
-            pl.BlockSpec((wide, units), lambda j: (j, 0)),
+            pl.BlockSpec((wide, units), lambda j: (j, 1)),
         ],
         out_specs=pl.BlockSpec((rows, wide), lambda j: (0, j)),
         out_shape=jax.ShapeDtypeStruct((rows, width), bf16),
         cost_estimate=cost(rows * units * width, 0),
         compiler_params=pltpu.CompilerParams(vmem_limit_bytes=VMEM_LIMIT),
         name="project",
-    )(left, right)
+    )(act, up_down)
 
 
 def feed_back_kernel(grad_ref, down_ref, gate_ref, up_ref, gate_out, up_out):
@@ -508,17 +507,18 @@
     up_out[...] = (grad * (gate * sigmoid)).astype(bf16)
 
 
-def feed_back(grad, down, gate, up):
+def feed_back(grad, up_down, gate, up):
     rows, width = grad.shape
-    units = down.shape[1]
+    units = gate.shape[1]
     wide = math.gcd(units, 512)
+    count = units // wide
     part = pl.BlockSpec((rows, wide), lambda j: (0, j))
     return pl.pallas_call(
         feed_back_kernel,
-        grid=(units // wide,),
+        grid=(count,),
         in_specs=[
             pl.BlockSpec((rows, width), lambda j: (0, 0)),
-            pl.BlockSpec((width, wide), lambda j: (0, j)),
+            pl.BlockSpec((width, wide), lambda j: (0, count + j)),
             part,
             part,
         ],
@@ -527,7 +527,7 @@
         cost_estimate=cost(rows * width * units, 0),
         compiler_params=pltpu.CompilerParams(vmem_limit_bytes=VMEM_LIMIT),
         name="feed_back",
-    )(grad, down, gate, up)
+    )(grad, up_down, gate, up)
 
 
 def project_both_kernel(gate_grad, up_grad, gate_ref, up_ref, out_ref):
@@ -535,9 +535,9 @@
     out_ref[...] = total.astype(bf16)
 
 
-def project_both(gate_grad, up_grad, gate_up):
+def project_both(gate_grad, up_grad, gate, up_down):
     rows, units = gate_grad.shape
-    width = gate_up.shape[0]
+    width = gate.shape[0]
     wide = math.gcd(width, 512)
     left = pl.BlockSpec((rows, units), lambda j: (0, 0))
     return pl.pallas_call(
@@ -547,14 +547,14 @@
             left,
             left,
             pl.BlockSpec((wide, units), lambda j: (j, 0)),
-            pl.BlockSpec((wide, units), lambda j: (j, 1)),
+            pl.BlockSpec((wide, units), lambda j: (j, 0)),
         ],
         out_specs=pl.BlockSpec((rows, wide), lambda j: (0, j)),
         out_shape=jax.ShapeDtypeStruct((rows, width), bf16),
         cost_estimate=cost(2 * rows * units * width, 0),
         compiler_params=pltpu.CompilerParams(vmem_limit_bytes=VMEM_LIMIT),
         name="project_both",
-    )(gate_grad, up_grad, gate_up, gate_up)
+    )(gate_grad, up_grad, gate, up_down)
 
 
 def tie_kernel(*refs):
@@ -659,13 +659,13 @@
     inward = [number(y, c, z) for y in range(2) for z in range(n_ctx) for c in range(2)]
     outward = [inward.index(n) for n in range(4 * n_ctx)]
 
-    def gather(*shards, after=()):
+    def gather(*shards, after=(), axes=("y", "ctx")):
         mine = jnp.concatenate([column_half(shard, core) for shard in shards], axis=1)
         theirs = jnp.concatenate([column_half(shard, 1 - core) for shard in shards], axis=1)
         pair = in_order(core, mine, swap(theirs, "core")).reshape(2 * piece, -1)
         if after:
             pair = tie(pair, *after)
-        return lax.all_gather(pair, ("y", "ctx"), axis=0, tiled=True)
+        return lax.all_gather(pair, axes, axis=0, tiled=True)
 
     def scatter(grad):
         return lax.psum_scatter(grad, ("y", "ctx"), scatter_dimension=0, tiled=True)
@@ -733,6 +733,8 @@
             sent = shift_ctx(sent, 1, n_ctx)
             if step == 1:
                 sent = tie(sent, *columns[1:])
+            elif step == 2:
+                sent = tie(sent, weight, blocks[0], out_all)
             blocks.append(in_order(here_x, sent, swap(sent, "tp")).reshape(rows, width))
         blocks.append(tokens)
         raws = [product(block, weight) for block in blocks]
@@ -758,7 +760,7 @@
         def sum_stats(stats):
             return lax.psum(stats, ("ctx", "tp"))
 
-        ready = (sent,)
+        ready = (sent, blocks[1])
     else:
         heads = att // HD
         wide = att
@@ -781,8 +783,10 @@
             total = lax.psum(ordered, ("core", "tp"))
             return jnp.where(core == 0, total, total[:, ::-1]).reshape(stats.shape)
 
-    gate_up_all = gather(gate_weight, up_weight, after=ready)
-    down_all = gather(down_weight.T, after=ready)
+    gate_line = gather(gate_weight, after=ready, axes="ctx")
+    gate_other = swap(gate_line, "y")
+    gate_all = in_order(here_y, gate_line, gate_other).reshape(width, -1)
+    up_down_all = gather(up_weight, down_weight.T, after=ready)
 
     my_gains = jnp.stack(
         [
@@ -814,6 +818,7 @@
             start = lax.rem(ctx + step, n_ctx) * rows
             block = lax.dynamic_slice_in_dim(out_att, start, rows)
             received.append(shift_ctx(block, step, n_ctx) if step else block)
+        received[-1] = tie(received[-1], gate_other)
         twice = jnp.concatenate(received[::-1] + received[::-1], axis=1)
         own = lax.dynamic_slice_in_dim(twice, (n_ctx - 1 - ctx) * wide, local, axis=1)
         other = swap(lax.dynamic_slice_in_dim(own, (1 - core) * att, att, axis=1), "core")
@@ -831,8 +836,8 @@
         attn_unit = attn_rows * attn_scale
         hidden_rows = inner_tokens[spans[j]].astype(f32) + attn_unit * attn_gain
         hidden_low = both(hidden_rows.astype(bf16))
-        gate_rows, up_rows, act_low = feed(hidden_low, gate_up_all)
-        part = project(act_low, down_all)
+        gate_rows, up_rows, act_low = feed(hidden_low, gate_all, up_down_all)
+        part = project(act_low, up_down_all)
         return part, act_low, hidden_low, hidden_rows, attn_scale, attn_unit, gate_rows, up_rows
 
     def turn_norm(j, state, mlp_rows):
@@ -849,8 +854,8 @@
 
     def turn_back(state, grad_mlp_low):
         gate_rows, up_rows = state[6:]
-        grad_gate_low, grad_up_low = feed_back(grad_mlp_low, down_all, gate_rows, up_rows)
-        back = project_both(grad_gate_low, grad_up_low, gate_up_all)
+        grad_gate_low, grad_up_low = feed_back(grad_mlp_low, up_down_all, gate_rows, up_rows)
+        back = project_both(grad_gate_low, grad_up_low, gate_all, up_down_all)
         return back, grad_gate_low, grad_up_low
 
     def close_back(j, state, back_rows):
@@ -871,7 +876,7 @@
     back_a = turn_back(fore_a, norm_a[0])
     hid_a = open_sum(back_a[0])
     norm_b = turn_norm(1, fore_b, close_sum(mlp_b[0], tie(mlp_b[1], back_a[0])))
-    down_grad = outer((norm_a[0], norm_b[0]), (fore_a[1], fore_b[1]))
+    down_grad = outer((norm_a[0], tie(norm_b[0], hid_a[0])), (fore_a[1], fore_b[1]))
     down_low = scatter(down_grad)
     back_b = turn_back(fore_b, tie(norm_b[0], down_grad))
     hid_b = open_sum(back_b[0])
@@ -880,25 +885,10 @@
     gate_grad = outer(hiddens, (back_a[1], back_b[1]))
     gate_low = scatter(gate_grad)
     close_b = close_back(1, fore_b, close_sum(hid_b[0], tie(hid_b[1], gate_grad)))
-    up_low = scatter(outer(hiddens, (back_a[2], back_b[2])))
-    out_theirs, out_mine = (
-        outer(
-            [
-                lax.dynamic_slice_in_dim(close[1], index * half, half, axis=1)
-                for close in (close_a, close_b)
-            ],
-            attended,
-        )
-        for index in (1 - here_y, here_y)
-    )
-    out_total = (out_mine.astype(f32) + swap(out_theirs, "y").astype(f32)).astype(bf16)
-    out_sent = []
-    for step in range(n_ctx):
-        start = lax.rem(ctx + step, n_ctx) * 2 * piece
-        block = lax.dynamic_slice_in_dim(out_total, start, 2 * piece)
-        out_sent.append(shift_ctx(block, step, n_ctx) if step else block)
-    out_low = sum(block.astype(f32) for block in out_sent).astype(bf16)
     grad_att = unchunk([close_a[0], close_b[0]])
+
+    def later(values):
+        return tie(values, own) if by_sequence else values
 
     if by_sequence:
         own = beside(core, grad_att[:rows], swap(grad_att[rows:], "core"))
@@ -908,6 +898,24 @@
             block = lax.dynamic_slice_in_dim(own, start, wide, axis=1)
             received.append(shift_ctx(block, step, n_ctx) if step else block)
         grad_att = by_source(received, ctx).reshape(n_ctx * rows, wide)
+    up_low = scatter(outer(hiddens, (back_a[2], tie(back_b[2], back_b[0]))))
+    out_theirs, out_mine = (
+        outer(
+            [
+                lax.dynamic_slice_in_dim(close[1], index * half, half, axis=1)
+                for close in (close_a, close_b)
+            ],
+            (attended[0], later(attended[1])),
+        )
+        for index in (1 - here_y, here_y)
+    )
+    out_total = (out_mine.astype(f32) + swap(out_theirs, "y").astype(f32)).astype(bf16)
+    out_sent = []
+    for step in range(n_ctx):
+        start = lax.rem(ctx + step, n_ctx) * 2 * piece
+        block = lax.dynamic_slice_in_dim(out_total, start, 2 * piece)
+        out_sent.append(shift_ctx(block, step, n_ctx) if step else block)
+    out_low = sum(block.astype(f32) for block in out_sent).astype(bf16)
     dq, dk, dv = attend_back(
         first_block, starts, edges, heads, rows, lse, (turned, 0), out_att, grad_att, keys, values
     )
@@ -925,6 +933,9 @@
     inner = sum_stats(inner[:, :, 0])[:, :, None] / width
     grad_qkv = norm_back(place, scaled, raw, scales, inner, dv, heads)
 
+    spread = jnp.zeros((2, local), f32)
+    spread = lax.dynamic_update_slice(spread, gain_sums[:, 0], (jnp.int32(0), first_head))
+    gains = jnp.concatenate([spread.reshape(-1), close_a[3] + close_b[3], norm_a[2] + norm_b[2]])
     if by_sequence:
         weight_halves = weight.reshape(2, half, 3 * wide)
         weight_mine = lax.dynamic_index_in_dim(weight_halves, here_x, 0, keepdims=False)
@@ -949,16 +960,14 @@
             block = grad_blocks[step]
             if step == n_ctx - 1:
                 block = tie(block, qkv_theirs)
-            term = contract_cols(block, weight_mine) + others[step].astype(f32)
+            other = tie(others[step], terms[0]) if step == 2 else others[step]
+            term = contract_cols(block, weight_mine) + other.astype(f32)
             if step < n_ctx - 1:
                 low = term.astype(bf16)
                 if step == 1:
                     qkv_theirs = y_half(1 - here_y, low).astype(bf16)
-                term = shift_ctx(low, -1 - step, n_ctx).astype(f32)
+                term = shift_ctx(low, -1 - step, n_ctx)
             terms.append(term)
-        dx = lowered(sum(terms))
-        dx_rows = beside(here_x, dx, swap(dx, "tp")).astype(f32)
-
         qkv_total = y_half(here_y, qkv_theirs) + swap(qkv_theirs, "y").astype(f32)
         split = qkv_total.reshape(2, n_ctx * piece, 3 * wide)
         mine = lax.dynamic_index_in_dim(split, core, 0, keepdims=False)
@@ -969,6 +978,11 @@
             start = lax.rem(ctx + step, n_ctx) * piece
             block = lax.dynamic_slice_in_dim(qkv_low, start, piece)
             received.append(shift_ctx(block, step, n_ctx) if step else block)
+        gains = lax.psum(tie(gains, low), ("y", "core", "ctx"))
+        terms[-1] = tie(terms[-1], gains, *received[1:])
+        dx = lowered(sum(term.astype(f32) for term in terms))
+        dx_rows = beside(here_x, dx, swap(dx, "tp")).astype(f32)
+        down_low, gate_low, up_low = (tie(values, dx) for values in (down_low, gate_low, up_low))
         lines = by_source(received, ctx)
         qkv_shards = [
             jnp.concatenate([lines[n, :, c * wide : (c + 1) * wide] for n in range(n_ctx)], axis=1)
@@ -976,6 +990,7 @@
             for c in range(3)
         ]
     else:
+        gains = lax.psum(gains, ("y", "core", "ctx"))
         grad_rows = [chunk(grad_qkv, j) for j in range(2)]
         token_rows = both(inner_tokens)
         token_rows = [chunk(token_rows, j) for j in range(2)]
@@ -985,16 +1000,8 @@
         ]
         sums = [open_sum(contract_cols(rows_part, weight).astype(bf16)) for rows_part in grad_rows]
         dx_rows = reorder(jnp.concatenate([close_sum(*parts) for parts in sums]), outward)
-    grad_tokens = reorder(jnp.concatenate([close_a[2], close_b[2]]), outward) + dx_rows
-
-    spread = jnp.zeros((2, local), f32)
-    spread = lax.dynamic_update_slice(spread, gain_sums[:, 0], (jnp.int32(0), first_head))
-    gains = jnp.concatenate([spread.reshape(-1), close_a[3] + close_b[3], norm_a[2] + norm_b[2]])
-    if by_sequence:
-        gains, down_low, gate_low, up_low = (
-            tie(values, dx) for values in (gains, down_low, gate_low, up_low)
-        )
-    gains = lax.psum(gains, ("y", "core", "ctx"))
+    grad_tokens = reorder(later(jnp.concatenate([close_a[2], close_b[2]])), outward) + dx_rows
+
     cuts = [local, 2 * local, 2 * local + width]
     query_gain_grad, key_gain_grad, attn_gain_grad, mlp_gain_grad = jnp.split(gains, cuts)
     attn_gain_grad, mlp_gain_grad = (
@@ -1002,7 +1009,7 @@
         for gain in (attn_gain_grad, mlp_gain_grad)
     )
     return (
-        reorder(jnp.concatenate([norm_a[1], norm_b[1]]), outward),
+        reorder(later(jnp.concatenate([norm_a[1], norm_b[1]])), outward),
         grad_tokens,
         *qkv_shards,
         own_share(out_low).T,

time: 1430 us -> 1480 us (1.035)
  waiting for transfers between devices: 602 us -> 469 us
  blocking collectives: 130 us -> 210 us
  starting transfers between devices: 47.7 us -> 107 us
  local copies, waits for them, and re-layouts: 77.6 us -> 127 us
    ppermute x21, waiting for transfers between devices: 344 us -> 226 us  [shift_ctx(): lax.ppermute(values, 'ctx', [(i, (i + steps) % size) for i in range(size)])]
    psum x1, blocking collectives: 57.9 us -> 138 us  [body(): gains = lax.psum(tie(gains, low), ('y', 'core', 'ctx'))]
    ppermute x21, starting transfers between devices: 26.9 us -> 84.4 us  [shift_ctx(): lax.ppermute(values, 'ctx', [(i, (i + steps) % size) for i in range(size)])]
    ppermute x40 -> x41, waiting for transfers between devices: 258 us -> 205 us  [swap(): return lax.ppermute(values, axis, [(0, 1), (1, 0)])]
    all_gather x3, waiting for transfers between devices: 0.01 us -> 37.7 us  [gather(): return lax.all_gather(pair, axes, axis=0, tiled=True)]
    unnamed x256 -> x309, local copies, waits for them, and re-layouts: 36.7 us -> 72.3 us
  transfers between devices with their start and end apart: 67 -> 68, of which waited for: 27 -> 33; matrix products, arithmetic and copies ran while one was open for 19% -> 19% of each run, Pallas kernels for 20% -> 20%
where the time goes in v2:
time: 1480 us; the launch traced here: 1470 us
  waiting for transfers between devices  469 us (32%)
  Pallas kernels  318 us (21%)
  blocking collectives  210 us (14%)
  other arithmetic  153 us (10%)
  local copies, waits for them, and re-layouts  127 us (9%)
  starting transfers between devices  107 us (7%)
  matrix products  72.7 us (5%)
  between operations  16.5 us (1%)
    ppermute x21, waiting for transfers between devices, shift_ctx(): lax.ppermute(values, 'ctx', [(i, (i + steps) % size) for i in range(size)])  226 us
    ppermute x41, waiting for transfers between devices, swap(): return lax.ppermute(values, axis, [(0, 1), (1, 0)])  205 us
    psum x1, blocking collectives, body(): gains = lax.psum(tie(gains, low), ('y', 'core', 'ctx'))  138 us
    ppermute x21, starting transfers between devices, shift_ctx(): lax.ppermute(values, 'ctx', [(i, (i + steps) % size) for i in range(size)])  84.4 us
    dot_general x24, matrix products, dims(): lax.dot_general(left, right, (over, ((), ())), preferred_element_type=f32)  72.7 us
    unnamed x309, local copies, waits for them, and re-layouts  72.3 us
    psum x2, blocking collectives, sum_stats(): return lax.psum(stats, ('ctx', 'tp'))  71.5 us
    pallas_call x5, Pallas kernels, outer(): pl.pallas_call(outer_kernel, grid=(high // tall, wide // broad), in_specs...  65.9 us
  transfers between devices with their start and end apart: 68, of which 33 were waited for; matrix products, arithmetic and copies ran while one was open for 19% of the time, Pallas kernels for 20%

profile of v2, /device:TPU:0, one launch (start us, length us, event | category | flops | bytes accessed | tf_op | source)
XLA Modules:
  0.0 1472.9 jit_solution(15400120454083989192)
XLA Ops:
  39.7 32.0 %collective-permute-done.refs_0_ = bf16[384,2048]{1,0:T(8,128)(2,1)S(1)} collective-permute-done((bf16[384,2048]{1,0:T(8,128)(2,1)}, bf16[384,2048]{1,0:T(8,128)(2,1)S(1)}, u32[]{:S(2)}, u32[]{:S(2)}) %collective-permute-start) | collective-permute-done | bytes 1572896 | tf_op jit(solution)/shard_map/ppermute | solution.py:599
  74.3 14.5 collective-permute-start.7
  92.6 16.1 %collective-permute-done.4 = bf16[384,2048]{1,0:T(8,128)(2,1)} collective-permute-done((bf16[384,2048]{1,0:T(8,128)(2,1)}, bf16[384,2048]{1,0:T(8,128)(2,1)}, u32[]{:S(2)}, u32[]{:S(2)}) %collective-permute-start.4) | collective-permute-done | bytes 1572896 | tf_op jit(solution)/shard_map/ppermute | solution.py:595
  112.4 20.6 %collective-permute-done.7.refs_0_ = bf16[384,2048]{1,0:T(8,128)(2,1)S(1)} collective-permute-done((bf16[384,2048]{1,0:T(8,128)(2,1)}, bf16[384,2048]{1,0:T(8,128)(2,1)S(1)}, u32[]{:S(2)}, u32[]{:S(2)}) %collective-permute-start.7) | collective-permute-done | bytes 1572896 | tf_op jit(solution)/shard_map/ppermute | solution.py:599
  144.3 25.9 %collective-permute-done.9 = bf16[384,2048]{1,0:T(8,128)(2,1)S(1)} collective-permute-done((bf16[384,2048]{1,0:T(8,128)(2,1)}, bf16[384,2048]{1,0:T(8,128)(2,1)S(1)}, u32[]{:S(2)}, u32[]{:S(2)}) %collective-permute-start.9) | collective-permute-done | bytes 1572896 | tf_op jit(solution)/shard_map/ppermute | solution.py:595
  204.7 14.3 copy.79
  227.6 27.7 %all-gather.6.cloned.1.call-done = bf16[1024,2048]{1,0:T(8,128)(2,1)} async-done(((bf16[256,2048]{1,0:T(8,128)(2,1)}), bf16[1024,2048]{1,0:T(8,128)(2,1)}) %all-gather.6.cloned.1.call-update) | async-done | bytes 4194320 | tf_op jit(solution)/shard_map/all_gather | solution.py:668
  273.9 35.7 %psum.21 = f32[2,3072]{1,0:T(2,128)S(1)} all-reduce(f32[2,3072]{1,0:T(2,128)S(1)} %bitcast.267), channel_id=1, replica_groups=mesh['y'=2,'core'=2,'ctx'=4,'tp'=2] {'ctx','tp'}, use_global_device_ids=true, to_apply=%region_10.11 | all-reduce | flops 6144 | bytes 49152 | tf_op jit(solution)/shard_map/psum | solution.py:761
  331.2 33.7 %attend.1 = (bf16[3072,256]{1,0:T(8,128)(2,1)S(1)}, f32[2,1,3072]{2,1,0:T(1,128)S(1)}) custom-call(s32[1]{0:T(128)} %constant.130.clone.1.first_ref, s32[1,4]{1,0:T(1,128)S(1)} %bitcast.216, s32[1,4]{1,0:T(1,128)S(1)} %bitcast.214, s32[1,1,3072]{2,1,0:T(1,128)S(1)} %reduce_window_max.36.start_ref, bf16[3072,768]{1,0:T(8,128)(2,1)} %turn.1.q_ref.k_ref.v_ref, ...), custom_call_target="tpu_custom_call" | custom-call | flops 9663676416 | tf_op jit(solution)/shard_map/attend/pallas_call | solution.py:123
  368.1 23.5 %collective-permute-done.12.refs_0_ = bf16[768,256]{1,0:T(8,128)(2,1)S(1)} collective-permute-done((bf16[768,256]{1,0:T(8,128)(2,1)}, bf16[768,256]{1,0:T(8,128)(2,1)S(1)}, u32[]{:S(2)}, u32[]{:S(2)}) %collective-permute-start.12) | collective-permute-done | bytes 393248 | tf_op jit(solution)/shard_map/ppermute | solution.py:599
  393.5 50.4 %collective-permute-done.15 = bf16[768,256]{1,0:T(8,128)(2,1)S(1)} collective-permute-done((bf16[768,256]{1,0:T(8,128)(2,1)}, bf16[768,256]{1,0:T(8,128)(2,1)S(1)}, u32[]{:S(2)}, u32[]{:S(2)}) %collective-permute-start.15) | collective-permute-done | bytes 393248 | tf_op jit(solution)/shard_map/ppermute | solution.py:599
  466.9 29.6 %collective-permute-done.19 = bf16[384,2048]{1,0:T(8,128)(2,1)S(1)} collective-permute-done((bf16[384,2048]{1,0:T(8,128)(2,1)S(1)}, bf16[384,2048]{1,0:T(8,128)(2,1)S(1)}, u32[]{:S(2)}, u32[]{:S(2)}) %collective-permute-start.19) | collective-permute-done | bytes 1572896 | tf_op jit(solution)/shard_map/ppermute | solution.py:595
  522.3 19.0 %feed.2 = (bf16[768,2048]{1,0:T(8,128)(2,1)S(1)}, bf16[768,2048]{1,0:T(8,128)(2,1)}, bf16[768,2048]{1,0:T(8,128)(2,1)}) custom-call(bf16[768,2048]{1,0:T(8,128)(2,1)} %pad_maximum_fusion.6.hidden_ref.left_a, bf16[2048,2048]{1,0:T(8,128)(2,1)} %bitcast.218, bf16[2048,4096]{1,0:T(8,128)(2,1)} %all-gather.8.cloned.1.call-done.up_ref.right_ref.down_ref), custom_call_target="tpu_custom_call" | custom-call | flops 6442450944 | tf_op jit(solution)/shard_map/feed/pallas_call | solution.py:461
  571.9 19.0 %feed.3 = (bf16[768,2048]{1,0:T(8,128)(2,1)S(1)}, bf16[768,2048]{1,0:T(8,128)(2,1)}, bf16[768,2048]{1,0:T(8,128)(2,1)}) custom-call(bf16[768,2048]{1,0:T(8,128)(2,1)} %pad_maximum_fusion.7.hidden_ref.left_b, bf16[2048,2048]{1,0:T(8,128)(2,1)} %bitcast.219, bf16[2048,4096]{1,0:T(8,128)(2,1)} %all-gather.8.cloned.1.call-done.up_ref.right_ref.down_ref), custom_call_target="tpu_custom_call" | custom-call | flops 6442450944 | tf_op jit(solution)/shard_map/feed/pallas_call | solution.py:461
  619.4 13.3 feed_back.2
  634.5 18.3 %project_both.2.refs_1_ = bf16[768,2048]{1,0:T(8,128)(2,1)S(1)} custom-call(bf16[768,2048]{1,0:T(8,128)(2,1)} %copy-done.30, bf16[768,2048]{1,0:T(8,128)(2,1)} %get-tuple-element.37.up_grad.right_a, bf16[2048,2048]{1,0:T(8,128)(2,1)} %bitcast.220, bf16[2048,4096]{1,0:T(8,128)(2,1)} %all-gather.8.cloned.1.call-done.up_ref.right_ref.down_ref), custom_call_target="tpu_custom_call" | custom-call | flops 6442450944 | tf_op jit(solution)/shard_map/project_both/pallas_call | solution.py:543
  672.7 19.9 %outer.5.refs_1_ = bf16[2048,2048]{1,0:T(8,128)(2,1)} custom-call(bf16[768,2048]{1,0:T(8,128)(2,1)S(1)} %copy-done.19, bf16[768,2048]{1,0:T(8,128)(2,1)} %tie.33.left_b, bf16[768,2048]{1,0:T(8,128)(2,1)} %get-tuple-element.32.left_ref.right_a, bf16[768,2048]{1,0:T(8,128)(2,1)} %get-tuple-element.33.left_ref.right_b), custom_call_target="tpu_custom_call" | custom-call | flops 6442450944 | tf_op jit(solution)/shard_map/outer/pallas_call | solution.py:436
  692.6 13.5 feed_back.3
  707.8 18.1 %project_both.3.refs_1_ = bf16[768,2048]{1,0:T(8,128)(2,1)S(1)} custom-call(bf16[768,2048]{1,0:T(8,128)(2,1)} %copy-done.32, bf16[768,2048]{1,0:T(8,128)(2,1)} %get-tuple-element.41.up_grad.refs_0_, bf16[2048,2048]{1,0:T(8,128)(2,1)} %bitcast.221, bf16[2048,4096]{1,0:T(8,128)(2,1)} %all-gather.8.cloned.1.call-done.up_ref.right_ref.down_ref), custom_call_target="tpu_custom_call" | custom-call | flops 6442450944 | tf_op jit(solution)/shard_map/project_both/pallas_call | solution.py:543
  729.8 20.1 %outer.9 = bf16[2048,2048]{1,0:T(8,128)(2,1)} custom-call(bf16[768,2048]{1,0:T(8,128)(2,1)S(1)} %copy-done.17, bf16[768,2048]{1,0:T(8,128)(2,1)} %pad_maximum_fusion.7.hidden_ref.left_b, bf16[768,2048]{1,0:T(8,128)(2,1)} %get-tuple-element.37.up_grad.right_a, bf16[768,2048]{1,0:T(8,128)(2,1)} %tie.47.right_b), custom_call_target="tpu_custom_call" | custom-call | flops 6442450944 | tf_op jit(solution)/shard_map/outer/pallas_call | solution.py:436
  758.8 20.3 %outer.6.refs_1_ = bf16[2048,2048]{1,0:T(8,128)(2,1)} custom-call(bf16[768,2048]{1,0:T(8,128)(2,1)S(1)} %copy-done.18, bf16[768,2048]{1,0:T(8,128)(2,1)} %pad_maximum_fusion.7.hidden_ref.left_b, bf16[768,2048]{1,0:T(8,128)(2,1)} %copy-done.30, bf16[768,2048]{1,0:T(8,128)(2,1)} %copy-done.32), custom_call_target="tpu_custom_call" | custom-call | flops 6442450944 | tf_op jit(solution)/shard_map/outer/pallas_call | solution.py:436
  789.8 33.0 %collective-permute-done.35.refs_0_ = bf16[384,2048]{1,0:T(8,128)(2,1)} collective-permute-done((bf16[384,2048]{1,0:T(8,128)(2,1)}, bf16[384,2048]{1,0:T(8,128)(2,1)}, u32[]{:S(2)}, u32[]{:S(2)}) %collective-permute-start.35) | collective-permute-done | bytes 1572896 | tf_op jit(solution)/shard_map/ppermute | solution.py:595
  869.3 12.4 collective-permute-done.38
  882.7 49.2 %collective-permute-done.39 = bf16[768,256]{1,0:T(8,128)(2,1)} collective-permute-done((bf16[768,256]{1,0:T(8,128)(2,1)}, bf16[768,256]{1,0:T(8,128)(2,1)}, u32[]{:S(2)}, u32[]{:S(2)}) %collective-permute-start.39) | collective-permute-done | bytes 393248 | tf_op jit(solution)/shard_map/ppermute | solution.py:599
  938.7 45.7 %attend_back.1 = (bf16[3072,256]{1,0:T(8,128)(2,1)S(1)}, bf16[3072,256]{1,0:T(8,128)(2,1)S(1)}, bf16[3072,256]{1,0:T(8,128)(2,1)S(1)}) custom-call(s32[1]{0:T(128)} %constant.130.clone.1.first_ref, s32[1,4]{1,0:T(1,128)S(1)} %bitcast.217, s32[1,4]{1,0:T(1,128)S(1)} %bitcast.215, s32[1,1,3072]{2,1,0:T(1,128)S(1)} %reduce_window_max.36.start_ref, ...), custom_call_target="tpu_custom_call" | custom-call | flops 12079595520 | tf_op jit(solution)/shard_map/attend_back/pallas_call | solution.py:233
  985.6 13.5 unturn.1
  1002.1 35.7 %psum.22 = f32[2,3072]{1,0:T(2,128)S(1)} all-reduce(f32[2,3072]{1,0:T(2,128)S(1)} %reduce.4), channel_id=1, replica_groups=mesh['y'=2,'core'=2,'ctx'=4,'tp'=2] {'ctx','tp'}, use_global_device_ids=true, to_apply=%region_19.20 | all-reduce | flops 6144 | bytes 49152 | tf_op jit(solution)/shard_map/psum | solution.py:761
  1041.5 11.5 norm_back.1.refs_0_
  1130.6 31.6 %collective-permute-done.43 = bf16[768,1024]{1,0:T(8,128)(2,1)} collective-permute-done((bf16[768,1024]{1,0:T(8,128)(2,1)}, bf16[768,1024]{1,0:T(8,128)(2,1)}, u32[]{:S(2)}, u32[]{:S(2)}) %collective-permute-start.43) | collective-permute-done | bytes 1572896 | tf_op jit(solution)/shard_map/ppermute | solution.py:595
  1183.0 46.4 %collective-permute-start.46 = (bf16[768,1024]{1,0:T(8,128)(2,1)}, bf16[768,1024]{1,0:T(8,128)(2,1)}, u32[]{:S(2)}, u32[]{:S(2)}) collective-permute-start(bf16[768,1024]{1,0:T(8,128)(2,1)} %add_convert_fusion.1.refs_1_), channel_id=1, source_target_pairs={{0,2},{2,4},{4,6},{6,0},{1,3},{3,5},{5,7},{7,1},{8,10},{10,12},{12... | collective-permute-start | bytes 4718600 | tf_op jit(solution)/shard_map/ppermute | solution.py:599
  1229.3 138.1 %psum.23.refs_1_ = f32[6144]{0:T(1024)S(1)} all-reduce(f32[6144]{0:T(1024)} %tie.42), channel_id=1, replica_groups=mesh['y'=2,'core'=2,'ctx'=4,'tp'=2] {'y','core','ctx'}, use_global_device_ids=true, to_apply=%region_24.25 | all-reduce | flops 6144 | bytes 49152 | tf_op jit(solution)/shard_map/psum | solution.py:981
  1410.4 32.5 %collective-permute-done.53 = bf16[768,1024]{1,0:T(8,128)(2,1)S(1)} collective-permute-done((bf16[768,1024]{1,0:T(8,128)(2,1)S(1)}, bf16[768,1024]{1,0:T(8,128)(2,1)S(1)}, u32[]{:S(2)}, u32[]{:S(2)}) %collective-permute-start.53) | collective-permute-done | bytes 1572896 | tf_op jit(solution)/shard_map/ppermute | solution.py:595
  (666 shorter events, 521.1 us)
Async XLA Ops:
  7.2 125.8 %all-gather.4.cloned.1.call-start = ((), (), s32[]{:S(2)}) async-start(), calls=%async_computation.3 | async-start | bytes 2359296 | tf_op jit(solution)/shard_map/all_gather | solution.py:668
  22.1 49.6 %collective-permute-start = (bf16[384,2048]{1,0:T(8,128)(2,1)}, bf16[384,2048]{1,0:T(8,128)(2,1)S(1)}, u32[]{:S(2)}, u32[]{:S(2)}) collective-permute-start(bf16[384,2048]{1,0:T(8,128)(2,1)} %constant_dynamic-slice_fusion.32), channel_id=1, source_target_pairs={{0,2},{2,4},{4,6},{6,0},{1,3},{3,5},{5,7},{7,1},{8,10},{10,12},{12... | collective-permute-start | bytes 4718600 | tf_op jit(solution)/shard_map/ppermute | solution.py:599
  24.8 230.5 %all-gather.6.cloned.1.call-start = ((), (), s32[]{:S(2)}) async-start(), calls=%async_computation.4 | async-start | bytes 5242880 | tf_op jit(solution)/shard_map/all_gather | solution.py:668
  37.8 51.0 %collective-permute-start.6 = (bf16[1024,768]{1,0:T(8,128)(2,1)S(1)}, bf16[1024,768]{1,0:T(8,128)(2,1)}, u32[]{:S(2)}, u32[]{:S(2)}) collective-permute-start(bf16[1024,768]{1,0:T(8,128)(2,1)S(1)} %bitcast.249), channel_id=1, source_target_pairs={{0,16},{16,0},{1,17},{17,1},{2,18},{18,2},{3,19},{19,3},{4,20},{20... | collective-permute-start | bytes 4718600 | tf_op jit(solution)/shard_map/ppermute | solution.py:595
  74.3 58.7 %collective-permute-start.7 = (bf16[384,2048]{1,0:T(8,128)(2,1)}, bf16[384,2048]{1,0:T(8,128)(2,1)S(1)}, u32[]{:S(2)}, u32[]{:S(2)}) collective-permute-start(bf16[384,2048]{1,0:T(8,128)(2,1)} %tie.25), channel_id=1, source_target_pairs={{0,2},{2,4},{4,6},{6,0},{1,3},{3,5},{5,7},{7,1},{8,10},{10,12},{12... | collective-permute-start | bytes 4718600 | tf_op jit(solution)/shard_map/ppermute | solution.py:599
  134.2 36.1 %collective-permute-start.9 = (bf16[384,2048]{1,0:T(8,128)(2,1)}, bf16[384,2048]{1,0:T(8,128)(2,1)S(1)}, u32[]{:S(2)}, u32[]{:S(2)}) collective-permute-start(bf16[384,2048]{1,0:T(8,128)(2,1)} %tie.26), channel_id=1, source_target_pairs={{0,1},{1,0},{2,3},{3,2},{4,5},{5,4},{6,7},{7,6},{8,9},{9,8},{10,11... | collective-permute-start | bytes 4718600 | tf_op jit(solution)/shard_map/ppermute | solution.py:595
  135.2 38.5 %collective-permute-start.10 = (bf16[384,2048]{1,0:T(8,128)(2,1)}, bf16[384,2048]{1,0:T(8,128)(2,1)}, u32[]{:S(2)}, u32[]{:S(2)}) collective-permute-start(bf16[384,2048]{1,0:T(8,128)(2,1)} %tie.26), channel_id=1, source_target_pairs={{0,2},{2,4},{4,6},{6,0},{1,3},{3,5},{5,7},{7,1},{8,10},{10,12},{12... | collective-permute-start | bytes 4718600 | tf_op jit(solution)/shard_map/ppermute | solution.py:599
  173.7 348.6 %all-gather.8.cloned.1.call-start = ((), (), s32[]{:S(2)}) async-start(), calls=%async_computation.5 | async-start | bytes 18874368 | tf_op jit(solution)/shard_map/all_gather | solution.py:668
  183.6 1259.6 %reduce-scatter.8.cloned.1.call-start = ((), (), s32[]{:S(2)}) async-start(), calls=%async_computation.8 | async-start | bytes 9437184 | tf_op jit(solution)/shard_map/reduce_scatter | solution.py:671
  200.0 59.8 %collective-permute-start.11 = (bf16[384,2048]{1,0:T(8,128)(2,1)}, bf16[384,2048]{1,0:T(8,128)(2,1)}, u32[]{:S(2)}, u32[]{:S(2)}) collective-permute-start(bf16[384,2048]{1,0:T(8,128)(2,1)} %collective-permute-done.10.refs_1_), channel_id=1, source_target_pairs={{0,1},{1,0},{2,3},{3,2},{4,5},{5,4},{6,7},{7,6},{8,9},{9,8},{10,11... | collective-permute-start | bytes 4718600 | tf_op jit(solution)/shard_map/ppermute | solution.py:595
  255.3 136.3 %collective-permute-start.14 = (bf16[1024,2048]{1,0:T(8,128)(2,1)}, bf16[1024,2048]{1,0:T(8,128)(2,1)}, u32[]{:S(2)}, u32[]{:S(2)}) collective-permute-start(bf16[1024,2048]{1,0:T(8,128)(2,1)} %all-gather.6.cloned.1.call-done), channel_id=1, source_target_pairs={{0,16},{16,0},{1,17},{17,1},{2,18},{18,2},{3,19},{19,3},{4,20},{20... | collective-permute-start | bytes 12582920 | tf_op jit(solution)/shard_map/ppermute | solution.py:595
  366.0 77.9 %collective-permute-start.15 = (bf16[768,256]{1,0:T(8,128)(2,1)}, bf16[768,256]{1,0:T(8,128)(2,1)S(1)}, u32[]{:S(2)}, u32[]{:S(2)}) collective-permute-start(bf16[768,256]{1,0:T(8,128)(2,1)} %get-tuple-element.148), channel_id=1, source_target_pairs={{0,4},{2,6},{4,0},{6,2},{1,5},{3,7},{5,1},{7,3},{8,12},{10,14},{12... | collective-permute-start | bytes 1179656 | tf_op jit(solution)/shard_map/ppermute | solution.py:599
  366.1 77.9 %collective-permute-start.16 = (bf16[768,256]{1,0:T(8,128)(2,1)S(1)}, bf16[768,256]{1,0:T(8,128)(2,1)S(1)}, u32[]{:S(2)}, u32[]{:S(2)}) collective-permute-start(bf16[768,256]{1,0:T(8,128)(2,1)S(1)} %get-tuple-element.147), channel_id=1, source_target_pairs={{0,2},{2,4},{4,6},{6,0},{1,3},{3,5},{5,7},{7,1},{8,10},{10,12},{12... | collective-permute-start | bytes 1179656 | tf_op jit(solution)/shard_map/ppermute | solution.py:599
  460.0 36.5 %collective-permute-start.19 = (bf16[384,2048]{1,0:T(8,128)(2,1)S(1)}, bf16[384,2048]{1,0:T(8,128)(2,1)S(1)}, u32[]{:S(2)}, u32[]{:S(2)}) collective-permute-start(bf16[384,2048]{1,0:T(8,128)(2,1)S(1)} %reduce-precision_convert_fusion.6), channel_id=1, source_target_pairs={{0,1},{1,0},{2,3},{3,2},{4,5},{5,4},{6,7},{7,6},{8,9},{9,8},{10,11... | collective-permute-start | bytes 4718600 | tf_op jit(solution)/shard_map/ppermute | solution.py:595
  501.8 54.2 %collective-permute-start.25 = (bf16[384,2048]{1,0:T(8,128)(2,1)}, bf16[384,2048]{1,0:T(8,128)(2,1)}, u32[]{:S(2)}, u32[]{:S(2)}) collective-permute-start(bf16[384,2048]{1,0:T(8,128)(2,1)} %reduce-precision_convert_fusion.4), channel_id=1, source_target_pairs={{0,1},{1,0},{2,3},{3,2},{4,5},{5,4},{6,7},{7,6},{8,9},{9,8},{10,11... | collective-permute-start | bytes 4718600 | tf_op jit(solution)/shard_map/ppermute | solution.py:595
  568.3 37.5 %collective-permute-start.23 = (bf16[384,2048]{1,0:T(8,128)(2,1)S(1)}, bf16[384,2048]{1,0:T(8,128)(2,1)}, u32[]{:S(2)}, u32[]{:S(2)}) collective-permute-start(bf16[384,2048]{1,0:T(8,128)(2,1)S(1)} %reduce-precision_convert_fusion.5), channel_id=1, source_target_pairs={{0,1},{1,0},{2,3},{3,2},{4,5},{5,4},{6,7},{7,6},{8,9},{9,8},{10,11... | collective-permute-start | bytes 4718600 | tf_op jit(solution)/shard_map/ppermute | solution.py:595
  616.4 38.1 %collective-permute-start.28 = (bf16[384,2048]{1,0:T(8,128)(2,1)S(1)}, bf16[384,2048]{1,0:T(8,128)(2,1)}, u32[]{:S(2)}, u32[]{:S(2)}) collective-permute-start(bf16[384,2048]{1,0:T(8,128)(2,1)S(1)} %reduce-precision_convert_fusion.3), channel_id=1, source_target_pairs={{0,1},{1,0},{2,3},{3,2},{4,5},{5,4},{6,7},{7,6},{8,9},{9,8},{10,11... | collective-permute-start | bytes 4718600 | tf_op jit(solution)/shard_map/ppermute | solution.py:595
  692.6 759.4 %reduce-scatter.6.cloned.1.call-start = ((), (), s32[]{:S(2)}) async-start(), calls=%async_computation.7 | async-start | bytes 9437184 | tf_op jit(solution)/shard_map/reduce_scatter | solution.py:671
  749.9 703.9 %reduce-scatter.4.cloned.1.call-start = ((), (), s32[]{:S(2)}) async-start(), calls=%async_computation.6 | async-start | bytes 9437184 | tf_op jit(solution)/shard_map/reduce_scatter | solution.py:671
  752.2 37.5 %collective-permute-start.31 = (bf16[384,2048]{1,0:T(8,128)(2,1)}, bf16[384,2048]{1,0:T(8,128)(2,1)}, u32[]{:S(2)}, u32[]{:S(2)}) collective-permute-start(bf16[384,2048]{1,0:T(8,128)(2,1)} %reduce-precision_convert_fusion.2.refs_1_), channel_id=1, source_target_pairs={{0,1},{1,0},{2,3},{3,2},{4,5},{5,4},{6,7},{7,6},{8,9},{9,8},{10,11... | collective-permute-start | bytes 4718600 | tf_op jit(solution)/shard_map/ppermute | solution.py:595
  757.2 65.6 %collective-permute-start.35 = (bf16[384,2048]{1,0:T(8,128)(2,1)}, bf16[384,2048]{1,0:T(8,128)(2,1)}, u32[]{:S(2)}, u32[]{:S(2)}) collective-permute-start(bf16[384,2048]{1,0:T(8,128)(2,1)} %reduce-precision_convert_fusion.1), channel_id=1, source_target_pairs={{0,1},{1,0},{2,3},{3,2},{4,5},{5,4},{6,7},{7,6},{8,9},{9,8},{10,11... | collective-permute-start | bytes 4718600 | tf_op jit(solution)/shard_map/ppermute | solution.py:595
  859.2 72.7 %collective-permute-start.39 = (bf16[768,256]{1,0:T(8,128)(2,1)}, bf16[768,256]{1,0:T(8,128)(2,1)}, u32[]{:S(2)}, u32[]{:S(2)}) collective-permute-start(bf16[768,256]{1,0:T(8,128)(2,1)} %get-tuple-element.144), channel_id=1, source_target_pairs={{0,4},{2,6},{4,0},{6,2},{1,5},{3,7},{5,1},{7,3},{8,12},{10,14},{12... | collective-permute-start | bytes 1179656 | tf_op jit(solution)/shard_map/ppermute | solution.py:599
  860.6 72.3 %collective-permute-start.40 = (bf16[768,256]{1,0:T(8,128)(2,1)}, bf16[768,256]{1,0:T(8,128)(2,1)}, u32[]{:S(2)}, u32[]{:S(2)}) collective-permute-start(bf16[768,256]{1,0:T(8,128)(2,1)} %get-tuple-element.142), channel_id=1, source_target_pairs={{0,2},{2,4},{4,6},{6,0},{1,3},{3,5},{5,7},{7,1},{8,10},{10,12},{12... | collective-permute-start | bytes 1179656 | tf_op jit(solution)/shard_map/ppermute | solution.py:599
  867.6 217.2 %collective-permute-start.54 = (bf16[1024,512]{1,0:T(8,128)(2,1)}, bf16[1024,512]{1,0:T(8,128)(2,1)}, u32[]{:S(2)}, u32[]{:S(2)}) collective-permute-start(bf16[1024,512]{1,0:T(8,128)(2,1)} %outer.8), channel_id=1, source_target_pairs={{0,16},{16,0},{1,17},{17,1},{2,18},{18,2},{3,19},{19,3},{4,20},{20... | collective-permute-start | bytes 3145736 | tf_op jit(solution)/shard_map/ppermute | solution.py:595
  1057.1 37.6 %collective-permute-start.41 = (bf16[768,1024]{1,0:T(8,128)(2,1)}, bf16[768,1024]{1,0:T(8,128)(2,1)}, u32[]{:S(2)}, u32[]{:S(2)}) collective-permute-start(bf16[768,1024]{1,0:T(8,128)(2,1)} %convolution_convert_fusion.5), channel_id=1, source_target_pairs={{0,1},{1,0},{2,3},{3,2},{4,5},{5,4},{6,7},{7,6},{8,9},{9,8},{10,11... | collective-permute-start | bytes 4718600 | tf_op jit(solution)/shard_map/ppermute | solution.py:595
  1080.2 86.4 %collective-permute-start.45 = (bf16[768,1024]{1,0:T(8,128)(2,1)}, bf16[768,1024]{1,0:T(8,128)(2,1)}, u32[]{:S(2)}, u32[]{:S(2)}) collective-permute-start(bf16[768,1024]{1,0:T(8,128)(2,1)} %convolution_convert_fusion.3), channel_id=1, source_target_pairs={{0,1},{1,0},{2,3},{3,2},{4,5},{5,4},{6,7},{7,6},{8,9},{9,8},{10,11... | collective-permute-start | bytes 4718600 | tf_op jit(solution)/shard_map/ppermute | solution.py:595
  1084.7 77.5 %collective-permute-start.43 = (bf16[768,1024]{1,0:T(8,128)(2,1)}, bf16[768,1024]{1,0:T(8,128)(2,1)}, u32[]{:S(2)}, u32[]{:S(2)}) collective-permute-start(bf16[768,1024]{1,0:T(8,128)(2,1)} %convolution_convert_fusion.4), channel_id=1, source_target_pairs={{0,1},{1,0},{2,3},{3,2},{4,5},{5,4},{6,7},{7,6},{8,9},{9,8},{10,11... | collective-permute-start | bytes 4718600 | tf_op jit(solution)/shard_map/ppermute | solution.py:595
  1103.3 63.3 %collective-permute-start.42 = (bf16[768,1024]{1,0:T(8,128)(2,1)}, bf16[768,1024]{1,0:T(8,128)(2,1)}, u32[]{:S(2)}, u32[]{:S(2)}) collective-permute-start(bf16[768,1024]{1,0:T(8,128)(2,1)} %add_convert_fusion.3), channel_id=1, source_target_pairs={{0,6},{2,0},{4,2},{6,4},{1,7},{3,1},{5,3},{7,5},{8,14},{10,8},{12,... | collective-permute-start | bytes 4718600 | tf_op jit(solution)/shard_map/ppermute | solution.py:599
  1125.1 254.3 %collective-permute-start.47 = (bf16[768,1024]{1,0:T(8,128)(2,1)}, bf16[768,1024]{1,0:T(8,128)(2,1)}, u32[]{:S(2)}, u32[]{:S(2)}) collective-permute-start(bf16[768,1024]{1,0:T(8,128)(2,1)} %convolution_convert_fusion.2), channel_id=1, source_target_pairs={{0,1},{1,0},{2,3},{3,2},{4,5},{5,4},{6,7},{7,6},{8,9},{9,8},{10,11... | collective-permute-start | bytes 4718600 | tf_op jit(solution)/shard_map/ppermute | solution.py:595
  1166.5 236.1 %collective-permute-start.44 = (bf16[768,1024]{1,0:T(8,128)(2,1)}, bf16[768,1024]{1,0:T(8,128)(2,1)}, u32[]{:S(2)}, u32[]{:S(2)}) collective-permute-start(bf16[768,1024]{1,0:T(8,128)(2,1)} %add_convert_fusion.2.refs_1_), channel_id=1, source_target_pairs={{0,4},{2,6},{4,0},{6,2},{1,5},{3,7},{5,1},{7,3},{8,12},{10,14},{12... | collective-permute-start | bytes 4718600 | tf_op jit(solution)/shard_map/ppermute | solution.py:599
  1183.0 192.0 %collective-permute-start.48 = (bf16[1024,768]{1,0:T(8,128)(2,1)}, bf16[1024,768]{1,0:T(8,128)(2,1)}, u32[]{:S(2)}, u32[]{:S(2)}) collective-permute-start(bf16[1024,768]{1,0:T(8,128)(2,1)} %add_convert_fusion.refs_1_), channel_id=1, source_target_pairs={{0,16},{16,0},{1,17},{17,1},{2,18},{18,2},{3,19},{19,3},{4,20},{20... | collective-permute-start | bytes 4718600 | tf_op jit(solution)/shard_map/ppermute | solution.py:595
  1183.0 219.7 %collective-permute-start.46 = (bf16[768,1024]{1,0:T(8,128)(2,1)}, bf16[768,1024]{1,0:T(8,128)(2,1)}, u32[]{:S(2)}, u32[]{:S(2)}) collective-permute-start(bf16[768,1024]{1,0:T(8,128)(2,1)} %add_convert_fusion.1.refs_1_), channel_id=1, source_target_pairs={{0,2},{2,4},{4,6},{6,0},{1,3},{3,5},{5,7},{7,1},{8,10},{10,12},{12... | collective-permute-start | bytes 4718600 | tf_op jit(solution)/shard_map/ppermute | solution.py:599
  (152 other events, 1737.0 us)
Sparse Core Ops, SparseCore 0:
  24.9 94.5 all-gather.3
  173.8 81.4 all-gather.5
  258.0 264.2 all-gather.7
  692.7 147.5 reduce-scatter.7
  844.3 183.1 reduce-scatter.5
  1030.9 284.7 reduce-scatter.3

commit v3 on v2

--- a/solution.py
+++ b/solution.py
@@ -422,27 +422,36 @@
     )(values)
 
 
-def outer_kernel(left_a, left_b, right_a, right_b, out_ref):
+def outer_kernel(part_ref, left_a, left_b, right_a, right_b, *refs):
     total = contract_rows(left_a[...], right_a[...]) + contract_rows(left_b[...], right_b[...])
-    out_ref[...] = total.astype(bf16)
-
-
-def outer(lefts, rights):
+    if len(refs) == 2:
+        total = total + refs[0][...].astype(f32)
+    refs[-1][...] = total.astype(bf16)
+
+
+def outer(lefts, rights, part, parts=2, add=None):
     rows, high = lefts[0].shape
+    high = high // parts
     wide = rights[0].shape[1]
     tall, broad = math.gcd(high, 512), math.gcd(wide, 1024)
-    left = pl.BlockSpec((rows, tall), lambda i, j: (0, i))
-    right = pl.BlockSpec((rows, broad), lambda i, j: (0, j))
+    count = high // tall
+    left = pl.BlockSpec((rows, tall), lambda i, j, part: (0, part[0] * count + i))
+    right = pl.BlockSpec((rows, broad), lambda i, j, part: (0, j))
+    out = pl.BlockSpec((tall, broad), lambda i, j, part: (i, j))
+    more = () if add is None else (add,)
     return pl.pallas_call(
         outer_kernel,
-        grid=(high // tall, wide // broad),
-        in_specs=[left, left, right, right],
-        out_specs=pl.BlockSpec((tall, broad), lambda i, j: (i, j)),
+        grid_spec=pltpu.PrefetchScalarGridSpec(
+            num_scalar_prefetch=1,
+            grid=(count, wide // broad),
+            in_specs=[left, left, right, right] + [out] * len(more),
+            out_specs=out,
+        ),
         out_shape=jax.ShapeDtypeStruct((high, wide), bf16),
         cost_estimate=cost(2 * rows * high * wide, 0),
         compiler_params=pltpu.CompilerParams(vmem_limit_bytes=VMEM_LIMIT),
         name="outer",
-    )(*lefts, *rights)
+    )(part.astype(jnp.int32)[None], *lefts, *rights, *more)
 
 
 def feed_kernel(hidden_ref, gate_ref, up_ref, gate_out, up_out, act_out):
@@ -667,8 +676,8 @@
             pair = tie(pair, *after)
         return lax.all_gather(pair, axes, axis=0, tiled=True)
 
-    def scatter(grad):
-        return lax.psum_scatter(grad, ("y", "ctx"), scatter_dimension=0, tiled=True)
+    def scatter(grad, axes="ctx"):
+        return lax.psum_scatter(grad, axes, scatter_dimension=0, tiled=True)
 
     def own_share(low):
         mine = lax.dynamic_slice_in_dim(low, core * piece, piece)
@@ -876,15 +885,22 @@
     back_a = turn_back(fore_a, norm_a[0])
     hid_a = open_sum(back_a[0])
     norm_b = turn_norm(1, fore_b, close_sum(mlp_b[0], tie(mlp_b[1], back_a[0])))
-    down_grad = outer((norm_a[0], tie(norm_b[0], hid_a[0])), (fore_a[1], fore_b[1]))
-    down_low = scatter(down_grad)
-    back_b = turn_back(fore_b, tie(norm_b[0], down_grad))
+    down_pairs = ((norm_a[0], tie(norm_b[0], hid_a[0])), (fore_a[1], fore_b[1]))
+    down_theirs = outer(*down_pairs, 1 - here_y)
+    down_other = swap(down_theirs, "y")
+    back_b = turn_back(fore_b, tie(norm_b[0], down_theirs))
     hid_b = open_sum(back_b[0])
     hiddens = (fore_a[2], fore_b[2])
-    close_a = close_back(0, fore_a, close_sum(hid_a[0], tie(hid_a[1], back_b[0])))
-    gate_grad = outer(hiddens, (back_a[1], back_b[1]))
-    gate_low = scatter(gate_grad)
-    close_b = close_back(1, fore_b, close_sum(hid_b[0], tie(hid_b[1], gate_grad)))
+    gate_pairs = (hiddens, (back_a[1], tie(back_b[1], back_b[0])))
+    up_pairs = (hiddens, (back_a[2], tie(back_b[2], back_b[0])))
+    gate_theirs = outer(*gate_pairs, 1 - here_y)
+    close_a = close_back(0, fore_a, close_sum(hid_a[0], tie(hid_a[1], gate_theirs)))
+    up_pairs = (hiddens, (back_a[2], tie(back_b[2], close_a[1])))
+    up_theirs = outer(*up_pairs, 1 - here_y)
+    gate_other, up_other = swap(gate_theirs, "y"), swap(up_theirs, "y")
+    down_total = outer(*down_pairs, here_y, add=down_other)
+    down_low = scatter(down_total)
+    close_b = close_back(1, fore_b, close_sum(hid_b[0], tie(hid_b[1], close_a[0], down_total, up_theirs)))
     grad_att = unchunk([close_a[0], close_b[0]])
 
     def later(values):
@@ -898,24 +914,11 @@
             block = lax.dynamic_slice_in_dim(own, start, wide, axis=1)
             received.append(shift_ctx(block, step, n_ctx) if step else block)
         grad_att = by_source(received, ctx).reshape(n_ctx * rows, wide)
-    up_low = scatter(outer(hiddens, (back_a[2], tie(back_b[2], back_b[0]))))
-    out_theirs, out_mine = (
-        outer(
-            [
-                lax.dynamic_slice_in_dim(close[1], index * half, half, axis=1)
-                for close in (close_a, close_b)
-            ],
-            (attended[0], later(attended[1])),
-        )
-        for index in (1 - here_y, here_y)
-    )
-    out_total = (out_mine.astype(f32) + swap(out_theirs, "y").astype(f32)).astype(bf16)
-    out_sent = []
-    for step in range(n_ctx):
-        start = lax.rem(ctx + step, n_ctx) * 2 * piece
-        block = lax.dynamic_slice_in_dim(out_total, start, 2 * piece)
-        out_sent.append(shift_ctx(block, step, n_ctx) if step else block)
-    out_low = sum(block.astype(f32) for block in out_sent).astype(bf16)
+    out_pairs = ((close_a[1], close_b[1]), (attended[0], later(attended[1])))
+    out_low = scatter(outer(*out_pairs, jnp.int32(0), parts=1), ("y", "ctx"))
+    gate_total = outer(hiddens, (back_a[1], later(gate_pairs[1][1])), here_y, add=gate_other)
+    gate_low = scatter(gate_total)
+    grad_att = tie(grad_att, gate_total)
     dq, dk, dv = attend_back(
         first_block, starts, edges, heads, rows, lse, (turned, 0), out_att, grad_att, keys, values
     )
@@ -927,26 +930,28 @@
             return low.reshape(2 * rows, wide)
 
         dk, dv = own_rows(dk), own_rows(dv)
+    up_total = outer(*up_pairs, here_y, add=up_other)
+    up_low = scatter(up_total)
+    dq = tie(dq, down_low, up_other)
     scaled, inner, gain_sums = unturn(
         place, dq, dk, raw, scales, my_gains, cosine, sine, heads
     )
-    inner = sum_stats(inner[:, :, 0])[:, :, None] / width
-    grad_qkv = norm_back(place, scaled, raw, scales, inner, dv, heads)
-
     spread = jnp.zeros((2, local), f32)
     spread = lax.dynamic_update_slice(spread, gain_sums[:, 0], (jnp.int32(0), first_head))
     gains = jnp.concatenate([spread.reshape(-1), close_a[3] + close_b[3], norm_a[2] + norm_b[2]])
+    inner = sum_stats(inner[:, :, 0])
+    inner = tie(inner, up_total)[:, :, None] / width
+    grad_qkv = norm_back(place, scaled, raw, scales, inner, dv, heads)
     if by_sequence:
         weight_halves = weight.reshape(2, half, 3 * wide)
         weight_mine = lax.dynamic_index_in_dim(weight_halves, here_x, 0, keepdims=False)
         weight_theirs = lax.dynamic_index_in_dim(weight_halves, 1 - here_x, 0, keepdims=False)
         grad_blocks = [grad_qkv[step * rows : (step + 1) * rows] for step in range(n_ctx)]
-        others = [
-            swap(contract_cols(block, weight_theirs).astype(bf16), "tp") for block in grad_blocks
-        ]
-
-        def y_half(index, after):
-            tied = tie(grad_qkv, after)
+        theirs = [contract_cols(block, weight_theirs).astype(bf16) for block in grad_blocks]
+        others = [swap(block, "tp") for block in theirs]
+
+        def y_half(index, *after):
+            tied = tie(grad_qkv, *after)
             return sum(
                 contract_rows(
                     lax.dynamic_slice_in_dim(block, index * half, half, axis=1),
@@ -959,16 +964,15 @@
         for step in range(n_ctx):
             block = grad_blocks[step]
             if step == n_ctx - 1:
-                block = tie(block, qkv_theirs)
-            other = tie(others[step], terms[0]) if step == 2 else others[step]
-            term = contract_cols(block, weight_mine) + other.astype(f32)
+                block = tie(block, qkv_theirs, gate_low)
+            term = contract_cols(block, weight_mine) + others[step].astype(f32)
             if step < n_ctx - 1:
                 low = term.astype(bf16)
-                if step == 1:
-                    qkv_theirs = y_half(1 - here_y, low).astype(bf16)
                 term = shift_ctx(low, -1 - step, n_ctx)
+                if step == n_ctx - 2:
+                    qkv_theirs = y_half(1 - here_y, low, terms[0]).astype(bf16)
             terms.append(term)
-        qkv_total = y_half(here_y, qkv_theirs) + swap(qkv_theirs, "y").astype(f32)
+        qkv_total = y_half(here_y, qkv_theirs, terms[1]) + swap(qkv_theirs, "y").astype(f32)
         split = qkv_total.reshape(2, n_ctx * piece, 3 * wide)
         mine = lax.dynamic_index_in_dim(split, core, 0, keepdims=False)
         qkv_low = lax.dynamic_index_in_dim(split, 1 - core, 0, keepdims=False)
@@ -978,11 +982,13 @@
             start = lax.rem(ctx + step, n_ctx) * piece
             block = lax.dynamic_slice_in_dim(qkv_low, start, piece)
             received.append(shift_ctx(block, step, n_ctx) if step else block)
-        gains = lax.psum(tie(gains, low), ("y", "core", "ctx"))
-        terms[-1] = tie(terms[-1], gains, *received[1:])
+        terms[-1] = tie(terms[-1], up_low, qkv_low)
         dx = lowered(sum(term.astype(f32) for term in terms))
         dx_rows = beside(here_x, dx, swap(dx, "tp")).astype(f32)
-        down_low, gate_low, up_low = (tie(values, dx) for values in (down_low, gate_low, up_low))
+        down_low, gate_low, up_low, out_low = (
+            tie(values, dx) for values in (down_low, gate_low, up_low, out_low)
+        )
+        gains = tie(gains, dx, *received[1:])
         lines = by_source(received, ctx)
         qkv_shards = [
             jnp.concatenate([lines[n, :, c * wide : (c + 1) * wide] for n in range(n_ctx)], axis=1)
@@ -990,18 +996,31 @@
             for c in range(3)
         ]
     else:
-        gains = lax.psum(gains, ("y", "core", "ctx"))
         grad_rows = [chunk(grad_qkv, j) for j in range(2)]
         token_rows = both(inner_tokens)
         token_rows = [chunk(token_rows, j) for j in range(2)]
         qkv_shards = [
-            own_share(scatter(outer(token_rows, [r[:, c * wide : (c + 1) * wide] for r in grad_rows])))
+            own_share(
+                scatter(
+                    outer(
+                        token_rows,
+                        [r[:, c * wide : (c + 1) * wide] for r in grad_rows],
+                        jnp.int32(0),
+                        parts=1,
+                    ),
+                    ("y", "ctx"),
+                )
+            )
             for c in range(3)
         ]
         sums = [open_sum(contract_cols(rows_part, weight).astype(bf16)) for rows_part in grad_rows]
         dx_rows = reorder(jnp.concatenate([close_sum(*parts) for parts in sums]), outward)
-    grad_tokens = reorder(later(jnp.concatenate([close_a[2], close_b[2]])), outward) + dx_rows
-
+    def late(values):
+        return tie(values, theirs[-1]) if by_sequence else values
+
+    grad_tokens = reorder(late(jnp.concatenate([close_a[2], close_b[2]])), outward) + dx_rows
+
+    gains = lax.psum(gains, ("y", "core", "ctx"))
     cuts = [local, 2 * local, 2 * local + width]
     query_gain_grad, key_gain_grad, attn_gain_grad, mlp_gain_grad = jnp.split(gains, cuts)
     attn_gain_grad, mlp_gain_grad = (
@@ -1009,7 +1028,7 @@
         for gain in (attn_gain_grad, mlp_gain_grad)
     )
     return (
-        reorder(later(jnp.concatenate([norm_a[1], norm_b[1]])), outward),
+        reorder(late(jnp.concatenate([norm_a[1], norm_b[1]])), outward),
         grad_tokens,
         *qkv_shards,
         own_share(out_low).T,

time: 1480 us -> 1480 us (level)
  waiting for transfers between devices: 469 us -> 551 us
  blocking collectives: 210 us -> 132 us
  starting transfers between devices: 107 us -> 60.3 us
  other arithmetic: 153 us -> 178 us
    psum x1, blocking collectives: 138 us -> 60.9 us  [body(): gains = lax.psum(gains, ('y', 'core', 'ctx'))]
    ppermute x21 -> x18, starting transfers between devices: 84.4 us -> 38.2 us  [shift_ctx(): lax.ppermute(values, 'ctx', [(i, (i + steps) % size) for i in range(size)])]
    ppermute x41 -> x43, waiting for transfers between devices: 205 us -> 251 us  [swap(): return lax.ppermute(values, axis, [(0, 1), (1, 0)])]
    ppermute x21 -> x18, waiting for transfers between devices: 226 us -> 251 us  [shift_ctx(): lax.ppermute(values, 'ctx', [(i, (i + steps) % size) for i in range(size)])]
    unnamed x309 -> x311, local copies, waits for them, and re-layouts: 72.3 us -> 85.9 us
    pallas_call x5 -> x7, Pallas kernels: 65.9 us -> 76.8 us  [outer(): pl.pallas_call(outer_kernel, grid_spec=pltpu.PrefetchScalarGridSpec(num_s...]
  transfers between devices with their start and end apart: 68 -> 68, of which waited for: 33 -> 31; matrix products, arithmetic and copies ran while one was open for 19% -> 21% of each run, Pallas kernels for 20% -> 22%
where the time goes in v3:
time: 1480 us; the launch traced here: 1470 us
  waiting for transfers between devices  551 us (37%)
  Pallas kernels  328 us (22%)
  other arithmetic  178 us (12%)
  local copies, waits for them, and re-layouts  137 us (9%)
  blocking collectives  132 us (9%)
  matrix products  70.3 us (5%)
  starting transfers between devices  60.3 us (4%)
  between operations  16.5 us (1%)
    ppermute x18, waiting for transfers between devices, shift_ctx(): lax.ppermute(values, 'ctx', [(i, (i + steps) % size) for i in range(size)])  251 us
    ppermute x43, waiting for transfers between devices, swap(): return lax.ppermute(values, axis, [(0, 1), (1, 0)])  251 us
    unnamed x311, local copies, waits for them, and re-layouts  85.9 us
    pallas_call x7, Pallas kernels, outer(): pl.pallas_call(outer_kernel, grid_spec=pltpu.PrefetchScalarGridSpec(num_s...  76.8 us
    psum x2, blocking collectives, sum_stats(): return lax.psum(stats, ('ctx', 'tp'))  70.9 us
    dot_general x24, matrix products, dims(): lax.dot_general(left, right, (over, ((), ())), preferred_element_type=f32)  70.3 us
    psum x1, blocking collectives, body(): gains = lax.psum(gains, ('y', 'core', 'ctx'))  60.9 us
    all_gather x3, waiting for transfers between devices, gather(): return lax.all_gather(pair, axes, axis=0, tiled=True)  48.6 us
  transfers between devices with their start and end apart: 68, of which 31 were waited for; matrix products, arithmetic and copies ran while one was open for 21% of the time, Pallas kernels for 22%

profile of v3, /device:TPU:0, one launch (start us, length us, event | category | flops | bytes accessed | tf_op | source)
XLA Modules:
  0.0 1473.5 jit_solution(18088807525756976189)
XLA Ops:
  39.7 32.0 %collective-permute-done.refs_0_ = bf16[384,2048]{1,0:T(8,128)(2,1)S(1)} collective-permute-done((bf16[384,2048]{1,0:T(8,128)(2,1)}, bf16[384,2048]{1,0:T(8,128)(2,1)S(1)}, u32[]{:S(2)}, u32[]{:S(2)}) %collective-permute-start) | collective-permute-done | bytes 1572896 | tf_op jit(solution)/shard_map/ppermute | solution.py:608
  74.3 14.5 collective-permute-start.7
  92.5 16.1 %collective-permute-done.4 = bf16[384,2048]{1,0:T(8,128)(2,1)} collective-permute-done((bf16[384,2048]{1,0:T(8,128)(2,1)}, bf16[384,2048]{1,0:T(8,128)(2,1)}, u32[]{:S(2)}, u32[]{:S(2)}) %collective-permute-start.4) | collective-permute-done | bytes 1572896 | tf_op jit(solution)/shard_map/ppermute | solution.py:604
  112.4 20.6 %collective-permute-done.7.refs_0_ = bf16[384,2048]{1,0:T(8,128)(2,1)S(1)} collective-permute-done((bf16[384,2048]{1,0:T(8,128)(2,1)}, bf16[384,2048]{1,0:T(8,128)(2,1)S(1)}, u32[]{:S(2)}, u32[]{:S(2)}) %collective-permute-start.7) | collective-permute-done | bytes 1572896 | tf_op jit(solution)/shard_map/ppermute | solution.py:608
  144.3 25.9 %collective-permute-done.9 = bf16[384,2048]{1,0:T(8,128)(2,1)S(1)} collective-permute-done((bf16[384,2048]{1,0:T(8,128)(2,1)}, bf16[384,2048]{1,0:T(8,128)(2,1)S(1)}, u32[]{:S(2)}, u32[]{:S(2)}) %collective-permute-start.9) | collective-permute-done | bytes 1572896 | tf_op jit(solution)/shard_map/ppermute | solution.py:604
  216.6 38.7 %all-gather.6.cloned.1.call-done = bf16[1024,2048]{1,0:T(8,128)(2,1)} async-done(((bf16[256,2048]{1,0:T(8,128)(2,1)}), bf16[1024,2048]{1,0:T(8,128)(2,1)}) %all-gather.6.cloned.1.call-update) | async-done | bytes 4194320 | tf_op jit(solution)/shard_map/all_gather | solution.py:677
  273.6 35.9 %psum.21 = f32[2,3072]{1,0:T(2,128)S(1)} all-reduce(f32[2,3072]{1,0:T(2,128)S(1)} %bitcast.264), channel_id=1, replica_groups=mesh['y'=2,'core'=2,'ctx'=4,'tp'=2] {'ctx','tp'}, use_global_device_ids=true, to_apply=%region_10.11 | all-reduce | flops 6144 | bytes 49152 | tf_op jit(solution)/shard_map/psum | solution.py:770
  331.1 33.7 %attend.1 = (bf16[3072,256]{1,0:T(8,128)(2,1)S(1)}, f32[2,1,3072]{2,1,0:T(1,128)S(1)}) custom-call(s32[1]{0:T(128)} %constant.126.clone.1.first_ref.part_ref, s32[1,4]{1,0:T(1,128)S(1)} %bitcast.215, s32[1,4]{1,0:T(1,128)S(1)} %bitcast.213, s32[1,1,3072]{2,1,0:T(1,128)S(1)} %reduce_window_max.36.start_ref, bf16[3072,768]{1,0:T(8,128)(2,1)} %turn.1.q_ref.k_ref.v_ref, ...), custom_call_target="tpu_custom_call" | custom-call | flops 9663676416 | tf_op jit(solution)/shard_map/attend/pallas_call | solution.py:123
  368.0 23.4 %collective-permute-done.12.refs_0_ = bf16[768,256]{1,0:T(8,128)(2,1)S(1)} collective-permute-done((bf16[768,256]{1,0:T(8,128)(2,1)}, bf16[768,256]{1,0:T(8,128)(2,1)S(1)}, u32[]{:S(2)}, u32[]{:S(2)}) %collective-permute-start.12) | collective-permute-done | bytes 393248 | tf_op jit(solution)/shard_map/ppermute | solution.py:608
  393.3 50.6 %collective-permute-done.15 = bf16[768,256]{1,0:T(8,128)(2,1)S(1)} collective-permute-done((bf16[768,256]{1,0:T(8,128)(2,1)}, bf16[768,256]{1,0:T(8,128)(2,1)S(1)}, u32[]{:S(2)}, u32[]{:S(2)}) %collective-permute-start.15) | collective-permute-done | bytes 393248 | tf_op jit(solution)/shard_map/ppermute | solution.py:608
  466.6 29.9 %collective-permute-done.19 = bf16[384,2048]{1,0:T(8,128)(2,1)S(1)} collective-permute-done((bf16[384,2048]{1,0:T(8,128)(2,1)S(1)}, bf16[384,2048]{1,0:T(8,128)(2,1)S(1)}, u32[]{:S(2)}, u32[]{:S(2)}) %collective-permute-start.19) | collective-permute-done | bytes 1572896 | tf_op jit(solution)/shard_map/ppermute | solution.py:604
  522.3 19.0 %feed.2 = (bf16[768,2048]{1,0:T(8,128)(2,1)S(1)}, bf16[768,2048]{1,0:T(8,128)(2,1)}, bf16[768,2048]{1,0:T(8,128)(2,1)}) custom-call(bf16[768,2048]{1,0:T(8,128)(2,1)} %pad_maximum_fusion.2.hidden_ref.left_a, bf16[2048,2048]{1,0:T(8,128)(2,1)} %bitcast.217, bf16[2048,4096]{1,0:T(8,128)(2,1)} %all-gather.8.cloned.1.call-done.up_ref.right_ref.down_ref), custom_call_target="tpu_custom_call" | custom-call | flops 6442450944 | tf_op jit(solution)/shard_map/feed/pallas_call | solution.py:470
  571.8 19.0 %feed.3 = (bf16[768,2048]{1,0:T(8,128)(2,1)S(1)}, bf16[768,2048]{1,0:T(8,128)(2,1)}, bf16[768,2048]{1,0:T(8,128)(2,1)}) custom-call(bf16[768,2048]{1,0:T(8,128)(2,1)} %pad_maximum_fusion.3.hidden_ref.left_b, bf16[2048,2048]{1,0:T(8,128)(2,1)} %bitcast.218, bf16[2048,4096]{1,0:T(8,128)(2,1)} %all-gather.8.cloned.1.call-done.up_ref.right_ref.down_ref), custom_call_target="tpu_custom_call" | custom-call | flops 6442450944 | tf_op jit(solution)/shard_map/feed/pallas_call | solution.py:470
  620.1 13.4 feed_back.2
  635.2 18.7 %project_both.2.refs_1_ = bf16[768,2048]{1,0:T(8,128)(2,1)S(1)} custom-call(bf16[768,2048]{1,0:T(8,128)(2,1)} %copy-done.11, bf16[768,2048]{1,0:T(8,128)(2,1)} %get-tuple-element.37.up_grad.right_a, bf16[2048,2048]{1,0:T(8,128)(2,1)} %bitcast.219, bf16[2048,4096]{1,0:T(8,128)(2,1)} %all-gather.8.cloned.1.call-done.up_ref.right_ref.down_ref), custom_call_target="tpu_custom_call" | custom-call | flops 6442450944 | tf_op jit(solution)/shard_map/project_both/pallas_call | solution.py:552
  692.8 13.4 feed_back.3
  707.8 18.1 %project_both.3.refs_1_ = bf16[768,2048]{1,0:T(8,128)(2,1)S(1)} custom-call(bf16[768,2048]{1,0:T(8,128)(2,1)} %copy-done.1, bf16[768,2048]{1,0:T(8,128)(2,1)} %get-tuple-element.42.up_grad.refs_0_, bf16[2048,2048]{1,0:T(8,128)(2,1)} %bitcast.220, bf16[2048,4096]{1,0:T(8,128)(2,1)} %all-gather.8.cloned.1.call-done.up_ref.right_ref.down_ref), custom_call_target="tpu_custom_call" | custom-call | flops 6442450944 | tf_op jit(solution)/shard_map/project_both/pallas_call | solution.py:552
  748.8 34.6 %collective-permute-done.36.refs_0_ = bf16[1024,2048]{1,0:T(8,128)(2,1)} collective-permute-done((bf16[1024,2048]{1,0:T(8,128)(2,1)}, bf16[1024,2048]{1,0:T(8,128)(2,1)}, u32[]{:S(2)}, u32[]{:S(2)}) %collective-permute-start.36) | collective-permute-done | bytes 4194336 | tf_op jit(solution)/shard_map/ppermute | solution.py:604
  783.5 11.9 outer.9.refs_2_
  822.8 17.1 %collective-permute-done.35.refs_0_ = bf16[384,2048]{1,0:T(8,128)(2,1)} collective-permute-done((bf16[384,2048]{1,0:T(8,128)(2,1)}, bf16[384,2048]{1,0:T(8,128)(2,1)}, u32[]{:S(2)}, u32[]{:S(2)}) %collective-permute-start.35) | collective-permute-done | bytes 1572896 | tf_op jit(solution)/shard_map/ppermute | solution.py:604
  864.7 32.1 %collective-permute-done.42.refs_0_ = bf16[1024,2048]{1,0:T(8,128)(2,1)} collective-permute-done((bf16[1024,2048]{1,0:T(8,128)(2,1)}, bf16[1024,2048]{1,0:T(8,128)(2,1)}, u32[]{:S(2)}, u32[]{:S(2)}) %collective-permute-start.42) | collective-permute-done | bytes 4194336 | tf_op jit(solution)/shard_map/ppermute | solution.py:604
  914.8 27.0 %collective-permute-done.39 = bf16[768,256]{1,0:T(8,128)(2,1)} collective-permute-done((bf16[768,256]{1,0:T(8,128)(2,1)}, bf16[768,256]{1,0:T(8,128)(2,1)}, u32[]{:S(2)}, u32[]{:S(2)}) %collective-permute-start.39) | collective-permute-done | bytes 393248 | tf_op jit(solution)/shard_map/ppermute | solution.py:608
  943.5 38.6 %collective-permute-done.40 = bf16[768,256]{1,0:T(8,128)(2,1)} collective-permute-done((bf16[768,256]{1,0:T(8,128)(2,1)}, bf16[768,256]{1,0:T(8,128)(2,1)}, u32[]{:S(2)}, u32[]{:S(2)}) %collective-permute-start.40) | collective-permute-done | bytes 393248 | tf_op jit(solution)/shard_map/ppermute | solution.py:608
  1000.6 12.3 outer.12.refs_1_
  1019.3 45.7 %attend_back.1 = (bf16[3072,256]{1,0:T(8,128)(2,1)S(1)}, bf16[3072,256]{1,0:T(8,128)(2,1)S(1)}, bf16[3072,256]{1,0:T(8,128)(2,1)S(1)}) custom-call(s32[1]{0:T(128)} %constant.126.clone.1.first_ref.part_ref, s32[1,4]{1,0:T(1,128)S(1)} %bitcast.216, s32[1,4]{1,0:T(1,128)S(1)} %bitcast.214, s32[1,1,3072]{2,1,0:T(1,128)S(1)} %reduce_window_max.36.start_ref, ...), custom_call_target="tpu_custom_call" | custom-call | flops 12079595520 | tf_op jit(solution)/shard_map/attend_back/pallas_call | solution.py:233
  1070.1 13.2 unturn.1
  1086.1 35.1 %psum.22.refs_0_ = f32[2,3072]{1,0:T(2,128)} all-reduce(f32[2,3072]{1,0:T(2,128)S(1)} %reduce.4), channel_id=1, replica_groups=mesh['y'=2,'core'=2,'ctx'=4,'tp'=2] {'ctx','tp'}, use_global_device_ids=true, to_apply=%region_20.21 | all-reduce | flops 6144 | bytes 49152 | tf_op jit(solution)/shard_map/psum | solution.py:770
  1151.1 27.6 %collective-permute-done.44 = bf16[768,1024]{1,0:T(8,128)(2,1)} collective-permute-done((bf16[768,1024]{1,0:T(8,128)(2,1)}, bf16[768,1024]{1,0:T(8,128)(2,1)}, u32[]{:S(2)}, u32[]{:S(2)}) %collective-permute-start.44) | collective-permute-done | bytes 1572896 | tf_op jit(solution)/shard_map/ppermute | solution.py:604
  1198.7 13.8 collective-permute-done.46
  1216.5 20.8 %collective-permute-done.48 = bf16[768,1024]{1,0:T(8,128)(2,1)S(1)} collective-permute-done((bf16[768,1024]{1,0:T(8,128)(2,1)}, bf16[768,1024]{1,0:T(8,128)(2,1)S(1)}, u32[]{:S(2)}, u32[]{:S(2)}) %collective-permute-start.48) | collective-permute-done | bytes 1572896 | tf_op jit(solution)/shard_map/ppermute | solution.py:604
  1267.4 53.0 %collective-permute-done.47.refs_2_ = bf16[768,1024]{1,0:T(8,128)(2,1)} collective-permute-done((bf16[768,1024]{1,0:T(8,128)(2,1)}, bf16[768,1024]{1,0:T(8,128)(2,1)}, u32[]{:S(2)}, u32[]{:S(2)}) %collective-permute-start.47) | collective-permute-done | bytes 1572896 | tf_op jit(solution)/shard_map/ppermute | solution.py:608
  1374.3 60.9 %psum.23 = f32[6144]{0:T(1024)S(1)} all-reduce(f32[6144]{0:T(1024)} %tie.59), channel_id=1, replica_groups=mesh['y'=2,'core'=2,'ctx'=4,'tp'=2] {'y','core','ctx'}, use_global_device_ids=true, to_apply=%region_28.29 | all-reduce | flops 6144 | bytes 49152 | tf_op jit(solution)/shard_map/psum | solution.py:1023
  (674 shorter events, 590.5 us)
Async XLA Ops:
  7.2 125.8 %all-gather.4.cloned.1.call-start = ((), (), s32[]{:S(2)}) async-start(), calls=%async_computation.4 | async-start | bytes 2359296 | tf_op jit(solution)/shard_map/all_gather | solution.py:677
  24.8 230.5 %all-gather.6.cloned.1.call-start = ((), (), s32[]{:S(2)}) async-start(), calls=%async_computation.5 | async-start | bytes 5242880 | tf_op jit(solution)/shard_map/all_gather | solution.py:677
  37.8 51.0 %collective-permute-start.6 = (bf16[1024,768]{1,0:T(8,128)(2,1)S(1)}, bf16[1024,768]{1,0:T(8,128)(2,1)}, u32[]{:S(2)}, u32[]{:S(2)}) collective-permute-start(bf16[1024,768]{1,0:T(8,128)(2,1)S(1)} %bitcast.246), channel_id=1, source_target_pairs={{0,16},{16,0},{1,17},{17,1},{2,18},{18,2},{3,19},{19,3},{4,20},{20... | collective-permute-start | bytes 4718600 | tf_op jit(solution)/shard_map/ppermute | solution.py:604
  74.3 58.7 %collective-permute-start.7 = (bf16[384,2048]{1,0:T(8,128)(2,1)}, bf16[384,2048]{1,0:T(8,128)(2,1)S(1)}, u32[]{:S(2)}, u32[]{:S(2)}) collective-permute-start(bf16[384,2048]{1,0:T(8,128)(2,1)} %tie.30), channel_id=1, source_target_pairs={{0,2},{2,4},{4,6},{6,0},{1,3},{3,5},{5,7},{7,1},{8,10},{10,12},{12... | collective-permute-start | bytes 4718600 | tf_op jit(solution)/shard_map/ppermute | solution.py:608
  173.7 348.6 %all-gather.8.cloned.1.call-start = ((), (), s32[]{:S(2)}) async-start(), calls=%async_computation.6 | async-start | bytes 18874368 | tf_op jit(solution)/shard_map/all_gather | solution.py:677
  183.5 883.8 %reduce-scatter.5.cloned.1.call-start = ((), (), s32[]{:S(2)}) async-start(), calls=%async_computation.7 | async-start | bytes 5242880 | tf_op jit(solution)/shard_map/reduce_scatter | solution.py:680
  199.8 60.1 %collective-permute-start.11 = (bf16[384,2048]{1,0:T(8,128)(2,1)}, bf16[384,2048]{1,0:T(8,128)(2,1)}, u32[]{:S(2)}, u32[]{:S(2)}) collective-permute-start(bf16[384,2048]{1,0:T(8,128)(2,1)} %collective-permute-done.10.refs_1_), channel_id=1, source_target_pairs={{0,1},{1,0},{2,3},{3,2},{4,5},{5,4},{6,7},{7,6},{8,9},{9,8},{10,11... | collective-permute-start | bytes 4718600 | tf_op jit(solution)/shard_map/ppermute | solution.py:604
  255.2 136.2 %collective-permute-start.14 = (bf16[1024,2048]{1,0:T(8,128)(2,1)}, bf16[1024,2048]{1,0:T(8,128)(2,1)}, u32[]{:S(2)}, u32[]{:S(2)}) collective-permute-start(bf16[1024,2048]{1,0:T(8,128)(2,1)} %all-gather.6.cloned.1.call-done), channel_id=1, source_target_pairs={{0,16},{16,0},{1,17},{17,1},{2,18},{18,2},{3,19},{19,3},{4,20},{20... | collective-permute-start | bytes 12582920 | tf_op jit(solution)/shard_map/ppermute | solution.py:604
  365.9 78.0 %collective-permute-start.15 = (bf16[768,256]{1,0:T(8,128)(2,1)}, bf16[768,256]{1,0:T(8,128)(2,1)S(1)}, u32[]{:S(2)}, u32[]{:S(2)}) collective-permute-start(bf16[768,256]{1,0:T(8,128)(2,1)} %get-tuple-element.141), channel_id=1, source_target_pairs={{0,4},{2,6},{4,0},{6,2},{1,5},{3,7},{5,1},{7,3},{8,12},{10,14},{12... | collective-permute-start | bytes 1179656 | tf_op jit(solution)/shard_map/ppermute | solution.py:608
  366.0 78.0 %collective-permute-start.16 = (bf16[768,256]{1,0:T(8,128)(2,1)S(1)}, bf16[768,256]{1,0:T(8,128)(2,1)S(1)}, u32[]{:S(2)}, u32[]{:S(2)}) collective-permute-start(bf16[768,256]{1,0:T(8,128)(2,1)S(1)} %get-tuple-element.140), channel_id=1, source_target_pairs={{0,2},{2,4},{4,6},{6,0},{1,3},{3,5},{5,7},{7,1},{8,10},{10,12},{12... | collective-permute-start | bytes 1179656 | tf_op jit(solution)/shard_map/ppermute | solution.py:608
  501.8 54.2 %collective-permute-start.25 = (bf16[384,2048]{1,0:T(8,128)(2,1)}, bf16[384,2048]{1,0:T(8,128)(2,1)}, u32[]{:S(2)}, u32[]{:S(2)}) collective-permute-start(bf16[384,2048]{1,0:T(8,128)(2,1)} %reduce-precision_convert_fusion.4), channel_id=1, source_target_pairs={{0,1},{1,0},{2,3},{3,2},{4,5},{5,4},{6,7},{7,6},{8,9},{9,8},{10,11... | collective-permute-start | bytes 4718600 | tf_op jit(solution)/shard_map/ppermute | solution.py:604
  690.3 93.2 %collective-permute-start.36 = (bf16[1024,2048]{1,0:T(8,128)(2,1)}, bf16[1024,2048]{1,0:T(8,128)(2,1)}, u32[]{:S(2)}, u32[]{:S(2)}) collective-permute-start(bf16[1024,2048]{1,0:T(8,128)(2,1)} %outer.7.refs_1_), channel_id=1, source_target_pairs={{0,16},{16,0},{1,17},{17,1},{2,18},{18,2},{3,19},{19,3},{4,20},{20... | collective-permute-start | bytes 12582920 | tf_op jit(solution)/shard_map/ppermute | solution.py:604
  691.8 50.0 %collective-permute-start.31 = (bf16[384,2048]{1,0:T(8,128)(2,1)}, bf16[384,2048]{1,0:T(8,128)(2,1)}, u32[]{:S(2)}, u32[]{:S(2)}) collective-permute-start(bf16[384,2048]{1,0:T(8,128)(2,1)} %reduce-precision_convert_fusion.2.refs_1_), channel_id=1, source_target_pairs={{0,1},{1,0},{2,3},{3,2},{4,5},{5,4},{6,7},{7,6},{8,9},{9,8},{10,11... | collective-permute-start | bytes 4718600 | tf_op jit(solution)/shard_map/ppermute | solution.py:604
  730.5 69.0 %collective-permute-start.34 = (bf16[384,2048]{1,0:T(8,128)(2,1)}, bf16[384,2048]{1,0:T(8,128)(2,1)}, u32[]{:S(2)}, u32[]{:S(2)}) collective-permute-start(bf16[384,2048]{1,0:T(8,128)(2,1)} %slice.564), channel_id=1, source_target_pairs={{0,8},{8,0},{1,9},{9,1},{2,10},{10,2},{3,11},{11,3},{4,12},{12,4},... | collective-permute-start | bytes 4718600 | tf_op jit(solution)/shard_map/ppermute | solution.py:604
  795.4 550.5 %reduce-scatter.7.cloned.1.call-start = ((), (), s32[]{:S(2)}) async-start(), calls=%async_computation.8 | async-start | bytes 5242880 | tf_op jit(solution)/shard_map/reduce_scatter | solution.py:680
  804.2 92.7 %collective-permute-start.42 = (bf16[1024,2048]{1,0:T(8,128)(2,1)}, bf16[1024,2048]{1,0:T(8,128)(2,1)}, u32[]{:S(2)}, u32[]{:S(2)}) collective-permute-start(bf16[1024,2048]{1,0:T(8,128)(2,1)} %outer.8.refs_1_), channel_id=1, source_target_pairs={{0,16},{16,0},{1,17},{17,1},{2,18},{18,2},{3,19},{19,3},{4,20},{20... | collective-permute-start | bytes 12582920 | tf_op jit(solution)/shard_map/ppermute | solution.py:604
  908.7 447.6 %reduce-scatter.9.cloned.1.call-start = ((), (), s32[]{:S(2)}) async-start(), calls=%async_computation.9 | async-start | bytes 5242880 | tf_op jit(solution)/shard_map/reduce_scatter | solution.py:680
  908.8 91.9 %collective-permute-start.43 = (bf16[1024,2048]{1,0:T(8,128)(2,1)}, bf16[1024,2048]{1,0:T(8,128)(2,1)}, u32[]{:S(2)}, u32[]{:S(2)}) collective-permute-start(bf16[1024,2048]{1,0:T(8,128)(2,1)} %outer.10.refs_3_), channel_id=1, source_target_pairs={{0,16},{16,0},{1,17},{17,1},{2,18},{18,2},{3,19},{19,3},{4,20},{20... | collective-permute-start | bytes 12582920 | tf_op jit(solution)/shard_map/ppermute | solution.py:604
  913.6 68.5 %collective-permute-start.40 = (bf16[768,256]{1,0:T(8,128)(2,1)}, bf16[768,256]{1,0:T(8,128)(2,1)}, u32[]{:S(2)}, u32[]{:S(2)}) collective-permute-start(bf16[768,256]{1,0:T(8,128)(2,1)} %get-tuple-element.137), channel_id=1, source_target_pairs={{0,4},{2,6},{4,0},{6,2},{1,5},{3,7},{5,1},{7,3},{8,12},{10,14},{12... | collective-permute-start | bytes 1179656 | tf_op jit(solution)/shard_map/ppermute | solution.py:608
  913.6 70.3 %collective-permute-start.41 = (bf16[768,256]{1,0:T(8,128)(2,1)}, bf16[768,256]{1,0:T(8,128)(2,1)S(1)}, u32[]{:S(2)}, u32[]{:S(2)}) collective-permute-start(bf16[768,256]{1,0:T(8,128)(2,1)} %get-tuple-element.135), channel_id=1, source_target_pairs={{0,2},{2,4},{4,6},{6,0},{1,3},{3,5},{5,7},{7,1},{8,10},{10,12},{12... | collective-permute-start | bytes 1179656 | tf_op jit(solution)/shard_map/ppermute | solution.py:608
  1013.0 353.0 %reduce-scatter.11.cloned.1.call-start = ((), (), s32[]{:S(2)}) async-start(), calls=%async_computation.10 | async-start | bytes 2359296 | tf_op jit(solution)/shard_map/reduce_scatter | solution.py:680
  1145.1 67.3 %collective-permute-start.46 = (bf16[768,1024]{1,0:T(8,128)(2,1)}, bf16[768,1024]{1,0:T(8,128)(2,1)}, u32[]{:S(2)}, u32[]{:S(2)}) collective-permute-start(bf16[768,1024]{1,0:T(8,128)(2,1)} %convolution_convert_fusion.3), channel_id=1, source_target_pairs={{0,1},{1,0},{2,3},{3,2},{4,5},{5,4},{6,7},{7,6},{8,9},{9,8},{10,11... | collective-permute-start | bytes 4718600 | tf_op jit(solution)/shard_map/ppermute | solution.py:604
  1151.0 86.3 %collective-permute-start.48 = (bf16[768,1024]{1,0:T(8,128)(2,1)}, bf16[768,1024]{1,0:T(8,128)(2,1)S(1)}, u32[]{:S(2)}, u32[]{:S(2)}) collective-permute-start(bf16[768,1024]{1,0:T(8,128)(2,1)} %convolution_convert_fusion.2), channel_id=1, source_target_pairs={{0,1},{1,0},{2,3},{3,2},{4,5},{5,4},{6,7},{7,6},{8,9},{9,8},{10,11... | collective-permute-start | bytes 4718600 | tf_op jit(solution)/shard_map/ppermute | solution.py:604
  1183.2 56.7 %collective-permute-start.45 = (bf16[768,1024]{1,0:T(8,128)(2,1)}, bf16[768,1024]{1,0:T(8,128)(2,1)}, u32[]{:S(2)}, u32[]{:S(2)}) collective-permute-start(bf16[768,1024]{1,0:T(8,128)(2,1)} %add_convert_fusion.3), channel_id=1, source_target_pairs={{0,6},{2,0},{4,2},{6,4},{1,7},{3,1},{5,3},{7,5},{8,14},{10,8},{12,... | collective-permute-start | bytes 4718600 | tf_op jit(solution)/shard_map/ppermute | solution.py:608
  1216.5 103.8 %collective-permute-start.47 = (bf16[768,1024]{1,0:T(8,128)(2,1)}, bf16[768,1024]{1,0:T(8,128)(2,1)}, u32[]{:S(2)}, u32[]{:S(2)}) collective-permute-start(bf16[768,1024]{1,0:T(8,128)(2,1)} %add_convert_fusion.2), channel_id=1, source_target_pairs={{0,4},{2,6},{4,0},{6,2},{1,5},{3,7},{5,1},{7,3},{8,12},{10,14},{12... | collective-permute-start | bytes 4718600 | tf_op jit(solution)/shard_map/ppermute | solution.py:608
  1251.9 77.5 %collective-permute-start.51 = (bf16[1024,768]{1,0:T(8,128)(2,1)}, bf16[1024,768]{1,0:T(8,128)(2,1)}, u32[]{:S(2)}, u32[]{:S(2)}) collective-permute-start(bf16[1024,768]{1,0:T(8,128)(2,1)} %add_convert_fusion.refs_1_), channel_id=1, source_target_pairs={{0,16},{16,0},{1,17},{17,1},{2,18},{18,2},{3,19},{19,3},{4,20},{20... | collective-permute-start | bytes 4718600 | tf_op jit(solution)/shard_map/ppermute | solution.py:604
  1262.0 83.9 %collective-permute-start.50 = (bf16[768,1024]{1,0:T(8,128)(2,1)}, bf16[768,1024]{1,0:T(8,128)(2,1)}, u32[]{:S(2)}, u32[]{:S(2)}) collective-permute-start(bf16[768,1024]{1,0:T(8,128)(2,1)} %convolution_convert_fusion.5.refs_1_), channel_id=1, source_target_pairs={{0,1},{1,0},{2,3},{3,2},{4,5},{5,4},{6,7},{7,6},{8,9},{9,8},{10,11... | collective-permute-start | bytes 4718600 | tf_op jit(solution)/shard_map/ppermute | solution.py:604
  1262.3 94.0 %collective-permute-start.49 = (bf16[768,1024]{1,0:T(8,128)(2,1)}, bf16[768,1024]{1,0:T(8,128)(2,1)}, u32[]{:S(2)}, u32[]{:S(2)}) collective-permute-start(bf16[768,1024]{1,0:T(8,128)(2,1)} %add_convert_fusion.1.refs_1_), channel_id=1, source_target_pairs={{0,2},{2,4},{4,6},{6,0},{1,3},{3,5},{5,7},{7,1},{8,10},{10,12},{12... | collective-permute-start | bytes 4718600 | tf_op jit(solution)/shard_map/ppermute | solution.py:608
  1360.8 97.0 %collective-permute-start.53 = (bf16[768,1024]{1,0:T(8,128)(2,1)S(1)}, bf16[768,1024]{1,0:T(8,128)(2,1)}, u32[]{:S(2)}, u32[]{:S(2)}) collective-permute-start(bf16[768,1024]{1,0:T(8,128)(2,1)S(1)} %reduce-precision_convert_fusion.refs_1_), channel_id=1, source_target_pairs={{0,1},{1,0},{2,3},{3,2},{4,5},{5,4},{6,7},{7,6},{8,9},{9,8},{10,11... | collective-permute-start | bytes 4718600 | tf_op jit(solution)/shard_map/ppermute | solution.py:604
  1369.4 75.1 %collective-permute-start.60 = (bf16[128,2048]{1,0:T(8,128)(2,1)}, bf16[128,2048]{1,0:T(8,128)(2,1)}, u32[]{:S(2)}, u32[]{:S(2)}) collective-permute-start(bf16[128,2048]{1,0:T(8,128)(2,1)} %constant_dynamic-slice_fusion), channel_id=1, source_target_pairs={{0,8},{8,0},{1,9},{9,1},{2,10},{10,2},{3,11},{11,3},{4,12},{12,4},... | collective-permute-start | bytes 1572872 | tf_op jit(solution)/shard_map/ppermute | solution.py:604
  1373.8 73.5 %collective-permute-start.59 = (bf16[128,2048]{1,0:T(8,128)(2,1)}, bf16[128,2048]{1,0:T(8,128)(2,1)}, u32[]{:S(2)}, u32[]{:S(2)}) collective-permute-start(bf16[128,2048]{1,0:T(8,128)(2,1)} %constant_dynamic-slice_fusion.1), channel_id=1, source_target_pairs={{0,8},{8,0},{1,9},{9,1},{2,10},{10,2},{3,11},{11,3},{4,12},{12,4},... | collective-permute-start | bytes 1572872 | tf_op jit(solution)/shard_map/ppermute | solution.py:604
  1373.9 78.5 %collective-permute-start.58 = (bf16[128,2048]{1,0:T(8,128)(2,1)}, bf16[128,2048]{1,0:T(8,128)(2,1)}, u32[]{:S(2)}, u32[]{:S(2)}) collective-permute-start(bf16[128,2048]{1,0:T(8,128)(2,1)} %constant_dynamic-slice_fusion.2), channel_id=1, source_target_pairs={{0,8},{8,0},{1,9},{9,1},{2,10},{10,2},{3,11},{11,3},{4,12},{12,4},... | collective-permute-start | bytes 1572872 | tf_op jit(solution)/shard_map/ppermute | solution.py:604
  (153 other events, 1958.7 us)
Sparse Core Ops, SparseCore 0:
  24.9 94.5 all-gather.3
  173.8 81.4 all-gather.5
  258.0 264.2 all-gather.7
  795.5 74.9 reduce-scatter.4
  908.8 99.3 reduce-scatter.6
  1013.1 80.5 reduce-scatter.8
  1262.1 92.3 reduce-scatter.10

commit v4 on v2

--- a/solution.py
+++ b/solution.py
@@ -941,9 +941,8 @@
         weight_mine = lax.dynamic_index_in_dim(weight_halves, here_x, 0, keepdims=False)
         weight_theirs = lax.dynamic_index_in_dim(weight_halves, 1 - here_x, 0, keepdims=False)
         grad_blocks = [grad_qkv[step * rows : (step + 1) * rows] for step in range(n_ctx)]
-        others = [
-            swap(contract_cols(block, weight_theirs).astype(bf16), "tp") for block in grad_blocks
-        ]
+        theirs = [contract_cols(block, weight_theirs).astype(bf16) for block in grad_blocks]
+        others = [swap(block, "tp") for block in theirs]
 
         def y_half(index, after):
             tied = tie(grad_qkv, after)
@@ -978,11 +977,11 @@
             start = lax.rem(ctx + step, n_ctx) * piece
             block = lax.dynamic_slice_in_dim(qkv_low, start, piece)
             received.append(shift_ctx(block, step, n_ctx) if step else block)
-        gains = lax.psum(tie(gains, low), ("y", "core", "ctx"))
-        terms[-1] = tie(terms[-1], gains, *received[1:])
+        terms[-1] = tie(terms[-1], qkv_low)
         dx = lowered(sum(term.astype(f32) for term in terms))
         dx_rows = beside(here_x, dx, swap(dx, "tp")).astype(f32)
         down_low, gate_low, up_low = (tie(values, dx) for values in (down_low, gate_low, up_low))
+        gains = lax.psum(tie(gains, dx, *received[1:]), ("y", "core", "ctx"))
         lines = by_source(received, ctx)
         qkv_shards = [
             jnp.concatenate([lines[n, :, c * wide : (c + 1) * wide] for n in range(n_ctx)], axis=1)
@@ -1000,7 +999,10 @@
         ]
         sums = [open_sum(contract_cols(rows_part, weight).astype(bf16)) for rows_part in grad_rows]
         dx_rows = reorder(jnp.concatenate([close_sum(*parts) for parts in sums]), outward)
-    grad_tokens = reorder(later(jnp.concatenate([close_a[2], close_b[2]])), outward) + dx_rows
+    def late(values):
+        return tie(values, theirs[-1]) if by_sequence else values
+
+    grad_tokens = reorder(late(jnp.concatenate([close_a[2], close_b[2]])), outward) + dx_rows
 
     cuts = [local, 2 * local, 2 * local + width]
     query_gain_grad, key_gain_grad, attn_gain_grad, mlp_gain_grad = jnp.split(gains, cuts)
@@ -1009,7 +1011,7 @@
         for gain in (attn_gain_grad, mlp_gain_grad)
     )
     return (
-        reorder(later(jnp.concatenate([norm_a[1], norm_b[1]])), outward),
+        reorder(late(jnp.concatenate([norm_a[1], norm_b[1]])), outward),
         grad_tokens,
         *qkv_shards,
         own_share(out_low).T,

time: 1480 us -> 1450 us (0.980)
  waiting for transfers between devices: 469 us -> 556 us
  blocking collectives: 210 us -> 130 us
  starting transfers between devices: 107 us -> 82.2 us
    psum x1, blocking collectives: 138 us -> 58.2 us  [body(): gains = lax.psum(tie(gains, dx, *received[1:]), ('y', 'core', 'ctx'))]
    ppermute x21, waiting for transfers between devices: 226 us -> 296 us  [shift_ctx(): lax.ppermute(values, 'ctx', [(i, (i + steps) % size) for i in range(size)])]
    ppermute x21, starting transfers between devices: 84.4 us -> 57.5 us  [shift_ctx(): lax.ppermute(values, 'ctx', [(i, (i + steps) % size) for i in range(size)])]
    unnamed x309 -> x303, local copies, waits for them, and re-layouts: 72.3 us -> 76.9 us
  transfers between devices with their start and end apart: 68 -> 68, of which waited for: 33 -> 34; matrix products, arithmetic and copies ran while one was open for 19% -> 19% of each run, Pallas kernels for 20% -> 20%
where the time goes in v4:
time: 1450 us
  waiting for transfers between devices  556 us (38%)
  Pallas kernels  308 us (21%)
  other arithmetic  158 us (11%)
  blocking collectives  130 us (9%)
  local copies, waits for them, and re-layouts  123 us (8%)
  starting transfers between devices  82.2 us (6%)
  matrix products  71.5 us (5%)
  between operations  16.4 us (1%)
    ppermute x21, waiting for transfers between devices, shift_ctx(): lax.ppermute(values, 'ctx', [(i, (i + steps) % size) for i in range(size)])  296 us
    ppermute x41, waiting for transfers between devices, swap(): return lax.ppermute(values, axis, [(0, 1), (1, 0)])  209 us
    unnamed x303, local copies, waits for them, and re-layouts  76.9 us
    psum x2, blocking collectives, sum_stats(): return lax.psum(stats, ('ctx', 'tp'))  71.7 us
    dot_general x24, matrix products, dims(): lax.dot_general(left, right, (over, ((), ())), preferred_element_type=f32)  71.5 us
    pallas_call x5, Pallas kernels, outer(): pl.pallas_call(outer_kernel, grid=(high // tall, wide // broad), in_specs...  64.7 us
    psum x1, blocking collectives, body(): gains = lax.psum(tie(gains, dx, *received[1:]), ('y', 'core', 'ctx'))  58.2 us
    ppermute x21, starting transfers between devices, shift_ctx(): lax.ppermute(values, 'ctx', [(i, (i + steps) % size) for i in range(size)])  57.5 us
  transfers between devices with their start and end apart: 68, of which 34 were waited for; matrix products, arithmetic and copies ran while one was open for 19% of the time, Pallas kernels for 20%

profile of v4, /device:TPU:0, one launch (start us, length us, event | category | flops | bytes accessed | tf_op | source)
XLA Modules:
  0.0 1445.5 jit_solution(15936516948799840339)
XLA Ops:
  39.7 32.0 %collective-permute-done.refs_0_ = bf16[384,2048]{1,0:T(8,128)(2,1)S(1)} collective-permute-done((bf16[384,2048]{1,0:T(8,128)(2,1)}, bf16[384,2048]{1,0:T(8,128)(2,1)S(1)}, u32[]{:S(2)}, u32[]{:S(2)}) %collective-permute-start) | collective-permute-done | bytes 1572896 | tf_op jit(solution)/shard_map/ppermute | solution.py:599
  74.3 14.5 %collective-permute-start.7 = (bf16[384,2048]{1,0:T(8,128)(2,1)}, bf16[384,2048]{1,0:T(8,128)(2,1)S(1)}, u32[]{:S(2)}, u32[]{:S(2)}) collective-permute-start(bf16[384,2048]{1,0:T(8,128)(2,1)} %tie.25), channel_id=1, source_target_pairs={{0,2},{2,4},{4,6},{6,0},{1,3},{3,5},{5,7},{7,1},{8,10},{10,12},{12... | collective-permute-start | bytes 4718600 | tf_op jit(solution)/shard_map/ppermute | solution.py:599
  92.6 16.1 %collective-permute-done.4 = bf16[384,2048]{1,0:T(8,128)(2,1)} collective-permute-done((bf16[384,2048]{1,0:T(8,128)(2,1)}, bf16[384,2048]{1,0:T(8,128)(2,1)}, u32[]{:S(2)}, u32[]{:S(2)}) %collective-permute-start.4) | collective-permute-done | bytes 1572896 | tf_op jit(solution)/shard_map/ppermute | solution.py:595
  112.4 20.6 %collective-permute-done.7.refs_0_ = bf16[384,2048]{1,0:T(8,128)(2,1)S(1)} collective-permute-done((bf16[384,2048]{1,0:T(8,128)(2,1)}, bf16[384,2048]{1,0:T(8,128)(2,1)S(1)}, u32[]{:S(2)}, u32[]{:S(2)}) %collective-permute-start.7) | collective-permute-done | bytes 1572896 | tf_op jit(solution)/shard_map/ppermute | solution.py:599
  144.3 26.0 %collective-permute-done.9 = bf16[384,2048]{1,0:T(8,128)(2,1)S(1)} collective-permute-done((bf16[384,2048]{1,0:T(8,128)(2,1)}, bf16[384,2048]{1,0:T(8,128)(2,1)S(1)}, u32[]{:S(2)}, u32[]{:S(2)}) %collective-permute-start.9) | collective-permute-done | bytes 1572896 | tf_op jit(solution)/shard_map/ppermute | solution.py:595
  216.7 38.6 %all-gather.6.cloned.1.call-done = bf16[1024,2048]{1,0:T(8,128)(2,1)} async-done(((bf16[256,2048]{1,0:T(8,128)(2,1)}), bf16[1024,2048]{1,0:T(8,128)(2,1)}) %all-gather.6.cloned.1.call-update) | async-done | bytes 4194320 | tf_op jit(solution)/shard_map/all_gather | solution.py:668
  273.9 35.8 %psum.21 = f32[2,3072]{1,0:T(2,128)S(1)} all-reduce(f32[2,3072]{1,0:T(2,128)S(1)} %bitcast.265), channel_id=1, replica_groups=mesh['y'=2,'core'=2,'ctx'=4,'tp'=2] {'ctx','tp'}, use_global_device_ids=true, to_apply=%region_10.11 | all-reduce | flops 6144 | bytes 49152 | tf_op jit(solution)/shard_map/psum | solution.py:761
  331.2 30.3 %attend.1 = (bf16[3072,256]{1,0:T(8,128)(2,1)S(1)}, f32[2,1,3072]{2,1,0:T(1,128)S(1)}) custom-call(s32[1]{0:T(128)} %constant.130.clone.1.first_ref, s32[1,4]{1,0:T(1,128)S(1)} %bitcast.216, s32[1,4]{1,0:T(1,128)S(1)} %bitcast.214, s32[1,1,3072]{2,1,0:T(1,128)S(1)} %reduce_window_max.36.start_ref, bf16[3072,768]{1,0:T(8,128)(2,1)} %turn.1.q_ref.k_ref.v_ref, ...), custom_call_target="tpu_custom_call" | custom-call | flops 9663676416 | tf_op jit(solution)/shard_map/attend/pallas_call | solution.py:123
  364.7 24.5 %collective-permute-done.12.refs_0_ = bf16[768,256]{1,0:T(8,128)(2,1)S(1)} collective-permute-done((bf16[768,256]{1,0:T(8,128)(2,1)}, bf16[768,256]{1,0:T(8,128)(2,1)S(1)}, u32[]{:S(2)}, u32[]{:S(2)}) %collective-permute-start.12) | collective-permute-done | bytes 393248 | tf_op jit(solution)/shard_map/ppermute | solution.py:599
  391.1 51.0 %collective-permute-done.15 = bf16[768,256]{1,0:T(8,128)(2,1)S(1)} collective-permute-done((bf16[768,256]{1,0:T(8,128)(2,1)}, bf16[768,256]{1,0:T(8,128)(2,1)S(1)}, u32[]{:S(2)}, u32[]{:S(2)}) %collective-permute-start.15) | collective-permute-done | bytes 393248 | tf_op jit(solution)/shard_map/ppermute | solution.py:599
  465.0 29.8 %collective-permute-done.19 = bf16[384,2048]{1,0:T(8,128)(2,1)S(1)} collective-permute-done((bf16[384,2048]{1,0:T(8,128)(2,1)S(1)}, bf16[384,2048]{1,0:T(8,128)(2,1)S(1)}, u32[]{:S(2)}, u32[]{:S(2)}) %collective-permute-start.19) | collective-permute-done | bytes 1572896 | tf_op jit(solution)/shard_map/ppermute | solution.py:595
  522.2 19.0 %feed.2 = (bf16[768,2048]{1,0:T(8,128)(2,1)S(1)}, bf16[768,2048]{1,0:T(8,128)(2,1)}, bf16[768,2048]{1,0:T(8,128)(2,1)}) custom-call(bf16[768,2048]{1,0:T(8,128)(2,1)} %pad_maximum_fusion.6.hidden_ref.left_a, bf16[2048,2048]{1,0:T(8,128)(2,1)} %bitcast.218, bf16[2048,4096]{1,0:T(8,128)(2,1)} %all-gather.8.cloned.1.call-done.up_ref.right_ref.down_ref), custom_call_target="tpu_custom_call" | custom-call | flops 6442450944 | tf_op jit(solution)/shard_map/feed/pallas_call | solution.py:461
  571.9 19.0 %feed.3 = (bf16[768,2048]{1,0:T(8,128)(2,1)S(1)}, bf16[768,2048]{1,0:T(8,128)(2,1)}, bf16[768,2048]{1,0:T(8,128)(2,1)}) custom-call(bf16[768,2048]{1,0:T(8,128)(2,1)} %pad_maximum_fusion.7.hidden_ref.left_b, bf16[2048,2048]{1,0:T(8,128)(2,1)} %bitcast.219, bf16[2048,4096]{1,0:T(8,128)(2,1)} %all-gather.8.cloned.1.call-done.up_ref.right_ref.down_ref), custom_call_target="tpu_custom_call" | custom-call | flops 6442450944 | tf_op jit(solution)/shard_map/feed/pallas_call | solution.py:461
  619.5 13.4 feed_back.2
  634.6 18.5 %project_both.2.refs_1_ = bf16[768,2048]{1,0:T(8,128)(2,1)S(1)} custom-call(bf16[768,2048]{1,0:T(8,128)(2,1)} %copy-done.28, bf16[768,2048]{1,0:T(8,128)(2,1)} %get-tuple-element.37.up_grad.right_a, bf16[2048,2048]{1,0:T(8,128)(2,1)} %bitcast.220, bf16[2048,4096]{1,0:T(8,128)(2,1)} %all-gather.8.cloned.1.call-done.up_ref.right_ref.down_ref), custom_call_target="tpu_custom_call" | custom-call | flops 6442450944 | tf_op jit(solution)/shard_map/project_both/pallas_call | solution.py:543
  673.1 19.9 %outer.5.refs_1_ = bf16[2048,2048]{1,0:T(8,128)(2,1)} custom-call(bf16[768,2048]{1,0:T(8,128)(2,1)S(1)} %copy-done.19, bf16[768,2048]{1,0:T(8,128)(2,1)} %tie.33.left_b, bf16[768,2048]{1,0:T(8,128)(2,1)} %get-tuple-element.32.left_ref.right_a, bf16[768,2048]{1,0:T(8,128)(2,1)} %get-tuple-element.33.left_ref.right_b), custom_call_target="tpu_custom_call" | custom-call | flops 6442450944 | tf_op jit(solution)/shard_map/outer/pallas_call | solution.py:436
  693.0 13.5 feed_back.3
  708.2 18.1 %project_both.3.refs_1_ = bf16[768,2048]{1,0:T(8,128)(2,1)S(1)} custom-call(bf16[768,2048]{1,0:T(8,128)(2,1)} %copy-done.30, bf16[768,2048]{1,0:T(8,128)(2,1)} %get-tuple-element.42.up_grad.refs_0_, bf16[2048,2048]{1,0:T(8,128)(2,1)} %bitcast.221, bf16[2048,4096]{1,0:T(8,128)(2,1)} %all-gather.8.cloned.1.call-done.up_ref.right_ref.down_ref), custom_call_target="tpu_custom_call" | custom-call | flops 6442450944 | tf_op jit(solution)/shard_map/project_both/pallas_call | solution.py:543
  730.1 20.2 %outer.9 = bf16[2048,2048]{1,0:T(8,128)(2,1)} custom-call(bf16[768,2048]{1,0:T(8,128)(2,1)S(1)} %copy-done.17, bf16[768,2048]{1,0:T(8,128)(2,1)} %pad_maximum_fusion.7.hidden_ref.left_b, bf16[768,2048]{1,0:T(8,128)(2,1)} %get-tuple-element.37.up_grad.right_a, bf16[768,2048]{1,0:T(8,128)(2,1)} %tie.46.right_b), custom_call_target="tpu_custom_call" | custom-call | flops 6442450944 | tf_op jit(solution)/shard_map/outer/pallas_call | solution.py:436
  759.2 20.1 %outer.6.refs_1_ = bf16[2048,2048]{1,0:T(8,128)(2,1)} custom-call(bf16[768,2048]{1,0:T(8,128)(2,1)S(1)} %copy-done.18, bf16[768,2048]{1,0:T(8,128)(2,1)} %pad_maximum_fusion.7.hidden_ref.left_b, bf16[768,2048]{1,0:T(8,128)(2,1)} %copy-done.28, bf16[768,2048]{1,0:T(8,128)(2,1)} %copy-done.30), custom_call_target="tpu_custom_call" | custom-call | flops 6442450944 | tf_op jit(solution)/shard_map/outer/pallas_call | solution.py:436
  790.2 33.1 %collective-permute-done.35.refs_0_ = bf16[384,2048]{1,0:T(8,128)(2,1)} collective-permute-done((bf16[384,2048]{1,0:T(8,128)(2,1)}, bf16[384,2048]{1,0:T(8,128)(2,1)}, u32[]{:S(2)}, u32[]{:S(2)}) %collective-permute-start.35) | collective-permute-done | bytes 1572896 | tf_op jit(solution)/shard_map/ppermute | solution.py:595
  854.6 25.1 %collective-permute-done.38 = bf16[768,256]{1,0:T(8,128)(2,1)S(1)} collective-permute-done((bf16[768,256]{1,0:T(8,128)(2,1)}, bf16[768,256]{1,0:T(8,128)(2,1)S(1)}, u32[]{:S(2)}, u32[]{:S(2)}) %collective-permute-start.38) | collective-permute-done | bytes 393248 | tf_op jit(solution)/shard_map/ppermute | solution.py:599
  879.7 47.2 %collective-permute-done.39 = bf16[768,256]{1,0:T(8,128)(2,1)S(1)} collective-permute-done((bf16[768,256]{1,0:T(8,128)(2,1)S(1)}, bf16[768,256]{1,0:T(8,128)(2,1)S(1)}, u32[]{:S(2)}, u32[]{:S(2)}) %collective-permute-start.39) | collective-permute-done | bytes 393248 | tf_op jit(solution)/shard_map/ppermute | solution.py:599
  928.8 41.3 %attend_back.1 = (bf16[3072,256]{1,0:T(8,128)(2,1)S(1)}, bf16[3072,256]{1,0:T(8,128)(2,1)S(1)}, bf16[3072,256]{1,0:T(8,128)(2,1)S(1)}) custom-call(s32[1]{0:T(128)} %constant.130.clone.1.first_ref, s32[1,4]{1,0:T(1,128)S(1)} %bitcast.217, s32[1,4]{1,0:T(1,128)S(1)} %bitcast.215, s32[1,1,3072]{2,1,0:T(1,128)S(1)} %reduce_window_max.36.start_ref, ...), custom_call_target="tpu_custom_call" | custom-call | flops 12079595520 | tf_op jit(solution)/shard_map/attend_back/pallas_call | solution.py:233
  971.2 13.2 unturn.1
  987.4 36.0 %psum.22 = f32[2,3072]{1,0:T(2,128)S(1)} all-reduce(f32[2,3072]{1,0:T(2,128)S(1)} %reduce.4), channel_id=1, replica_groups=mesh['y'=2,'core'=2,'ctx'=4,'tp'=2] {'ctx','tp'}, use_global_device_ids=true, to_apply=%region_19.20 | all-reduce | flops 6144 | bytes 49152 | tf_op jit(solution)/shard_map/psum | solution.py:761
  1117.6 29.7 %collective-permute-done.45.refs_0_ = bf16[768,1024]{1,0:T(8,128)(2,1)} collective-permute-done((bf16[768,1024]{1,0:T(8,128)(2,1)}, bf16[768,1024]{1,0:T(8,128)(2,1)}, u32[]{:S(2)}, u32[]{:S(2)}) %collective-permute-start.45) | collective-permute-done | bytes 1572896 | tf_op jit(solution)/shard_map/ppermute | solution.py:595
  1147.7 16.8 %collective-permute-done.42.refs_1_ = bf16[768,1024]{1,0:T(8,128)(2,1)} collective-permute-done((bf16[768,1024]{1,0:T(8,128)(2,1)}, bf16[768,1024]{1,0:T(8,128)(2,1)}, u32[]{:S(2)}, u32[]{:S(2)}) %collective-permute-start.42) | collective-permute-done | bytes 1572896 | tf_op jit(solution)/shard_map/ppermute | solution.py:599
  1199.7 23.6 %collective-permute-done.48 = bf16[1024,768]{1,0:T(8,128)(2,1)} collective-permute-done((bf16[1024,768]{1,0:T(8,128)(2,1)}, bf16[1024,768]{1,0:T(8,128)(2,1)}, u32[]{:S(2)}, u32[]{:S(2)}) %collective-permute-start.48) | collective-permute-done | bytes 1572896 | tf_op jit(solution)/shard_map/ppermute | solution.py:595
  1252.8 13.5 collective-permute-start.52
  1266.2 70.4 %collective-permute-done.44 = bf16[768,1024]{1,0:T(8,128)(2,1)} collective-permute-done((bf16[768,1024]{1,0:T(8,128)(2,1)}, bf16[768,1024]{1,0:T(8,128)(2,1)}, u32[]{:S(2)}, u32[]{:S(2)}) %collective-permute-start.44) | collective-permute-done | bytes 1572896 | tf_op jit(solution)/shard_map/ppermute | solution.py:599
  1346.2 58.2 %psum.23 = f32[6144]{0:T(1024)S(1)} all-reduce(f32[6144]{0:T(1024)} %tie.49), channel_id=1, replica_groups=mesh['y'=2,'core'=2,'ctx'=4,'tp'=2] {'y','core','ctx'}, use_global_device_ids=true, to_apply=%region_27.28 | all-reduce | flops 6144 | bytes 49152 | tf_op jit(solution)/shard_map/psum | solution.py:984
  (659 shorter events, 540.2 us)
Async XLA Ops:
  7.2 125.8 %all-gather.4.cloned.1.call-start = ((), (), s32[]{:S(2)}) async-start(), calls=%async_computation.3 | async-start | bytes 2359296 | tf_op jit(solution)/shard_map/all_gather | solution.py:668
  22.1 49.6 %collective-permute-start = (bf16[384,2048]{1,0:T(8,128)(2,1)}, bf16[384,2048]{1,0:T(8,128)(2,1)S(1)}, u32[]{:S(2)}, u32[]{:S(2)}) collective-permute-start(bf16[384,2048]{1,0:T(8,128)(2,1)} %constant_dynamic-slice_fusion.32), channel_id=1, source_target_pairs={{0,2},{2,4},{4,6},{6,0},{1,3},{3,5},{5,7},{7,1},{8,10},{10,12},{12... | collective-permute-start | bytes 4718600 | tf_op jit(solution)/shard_map/ppermute | solution.py:599
  24.8 230.4 %all-gather.6.cloned.1.call-start = ((), (), s32[]{:S(2)}) async-start(), calls=%async_computation.4 | async-start | bytes 5242880 | tf_op jit(solution)/shard_map/all_gather | solution.py:668
  37.8 51.0 %collective-permute-start.6 = (bf16[1024,768]{1,0:T(8,128)(2,1)S(1)}, bf16[1024,768]{1,0:T(8,128)(2,1)}, u32[]{:S(2)}, u32[]{:S(2)}) collective-permute-start(bf16[1024,768]{1,0:T(8,128)(2,1)S(1)} %bitcast.247), channel_id=1, source_target_pairs={{0,16},{16,0},{1,17},{17,1},{2,18},{18,2},{3,19},{19,3},{4,20},{20... | collective-permute-start | bytes 4718600 | tf_op jit(solution)/shard_map/ppermute | solution.py:595
  74.3 58.7 %collective-permute-start.7 = (bf16[384,2048]{1,0:T(8,128)(2,1)}, bf16[384,2048]{1,0:T(8,128)(2,1)S(1)}, u32[]{:S(2)}, u32[]{:S(2)}) collective-permute-start(bf16[384,2048]{1,0:T(8,128)(2,1)} %tie.25), channel_id=1, source_target_pairs={{0,2},{2,4},{4,6},{6,0},{1,3},{3,5},{5,7},{7,1},{8,10},{10,12},{12... | collective-permute-start | bytes 4718600 | tf_op jit(solution)/shard_map/ppermute | solution.py:599
  173.6 348.6 %all-gather.8.cloned.1.call-start = ((), (), s32[]{:S(2)}) async-start(), calls=%async_computation.5 | async-start | bytes 18874368 | tf_op jit(solution)/shard_map/all_gather | solution.py:668
  183.5 1232.2 %reduce-scatter.8.cloned.1.call-start = ((), (), s32[]{:S(2)}) async-start(), calls=%async_computation.8 | async-start | bytes 9437184 | tf_op jit(solution)/shard_map/reduce_scatter | solution.py:671
  200.1 59.7 %collective-permute-start.11 = (bf16[384,2048]{1,0:T(8,128)(2,1)}, bf16[384,2048]{1,0:T(8,128)(2,1)}, u32[]{:S(2)}, u32[]{:S(2)}) collective-permute-start(bf16[384,2048]{1,0:T(8,128)(2,1)} %collective-permute-done.10.refs_1_), channel_id=1, source_target_pairs={{0,1},{1,0},{2,3},{3,2},{4,5},{5,4},{6,7},{7,6},{8,9},{9,8},{10,11... | collective-permute-start | bytes 4718600 | tf_op jit(solution)/shard_map/ppermute | solution.py:595
  255.2 134.6 %collective-permute-start.14 = (bf16[1024,2048]{1,0:T(8,128)(2,1)}, bf16[1024,2048]{1,0:T(8,128)(2,1)}, u32[]{:S(2)}, u32[]{:S(2)}) collective-permute-start(bf16[1024,2048]{1,0:T(8,128)(2,1)} %all-gather.6.cloned.1.call-done), channel_id=1, source_target_pairs={{0,16},{16,0},{1,17},{17,1},{2,18},{18,2},{3,19},{19,3},{4,20},{20... | collective-permute-start | bytes 12582920 | tf_op jit(solution)/shard_map/ppermute | solution.py:595
  362.6 79.5 %collective-permute-start.15 = (bf16[768,256]{1,0:T(8,128)(2,1)}, bf16[768,256]{1,0:T(8,128)(2,1)S(1)}, u32[]{:S(2)}, u32[]{:S(2)}) collective-permute-start(bf16[768,256]{1,0:T(8,128)(2,1)} %get-tuple-element.148), channel_id=1, source_target_pairs={{0,4},{2,6},{4,0},{6,2},{1,5},{3,7},{5,1},{7,3},{8,12},{10,14},{12... | collective-permute-start | bytes 1179656 | tf_op jit(solution)/shard_map/ppermute | solution.py:599
  362.7 79.5 %collective-permute-start.16 = (bf16[768,256]{1,0:T(8,128)(2,1)S(1)}, bf16[768,256]{1,0:T(8,128)(2,1)S(1)}, u32[]{:S(2)}, u32[]{:S(2)}) collective-permute-start(bf16[768,256]{1,0:T(8,128)(2,1)S(1)} %get-tuple-element.147), channel_id=1, source_target_pairs={{0,2},{2,4},{4,6},{6,0},{1,3},{3,5},{5,7},{7,1},{8,10},{10,12},{12... | collective-permute-start | bytes 1179656 | tf_op jit(solution)/shard_map/ppermute | solution.py:599
  500.0 56.0 %collective-permute-start.25 = (bf16[384,2048]{1,0:T(8,128)(2,1)}, bf16[384,2048]{1,0:T(8,128)(2,1)}, u32[]{:S(2)}, u32[]{:S(2)}) collective-permute-start(bf16[384,2048]{1,0:T(8,128)(2,1)} %reduce-precision_convert_fusion.4), channel_id=1, source_target_pairs={{0,1},{1,0},{2,3},{3,2},{4,5},{5,4},{6,7},{7,6},{8,9},{9,8},{10,11... | collective-permute-start | bytes 4718600 | tf_op jit(solution)/shard_map/ppermute | solution.py:595
  693.0 731.6 %reduce-scatter.6.cloned.1.call-start = ((), (), s32[]{:S(2)}) async-start(), calls=%async_computation.7 | async-start | bytes 9437184 | tf_op jit(solution)/shard_map/reduce_scatter | solution.py:671
  750.4 676.0 %reduce-scatter.4.cloned.1.call-start = ((), (), s32[]{:S(2)}) async-start(), calls=%async_computation.6 | async-start | bytes 9437184 | tf_op jit(solution)/shard_map/reduce_scatter | solution.py:671
  757.7 65.6 %collective-permute-start.35 = (bf16[384,2048]{1,0:T(8,128)(2,1)}, bf16[384,2048]{1,0:T(8,128)(2,1)}, u32[]{:S(2)}, u32[]{:S(2)}) collective-permute-start(bf16[384,2048]{1,0:T(8,128)(2,1)} %reduce-precision_convert_fusion.1), channel_id=1, source_target_pairs={{0,1},{1,0},{2,3},{3,2},{4,5},{5,4},{6,7},{7,6},{8,9},{9,8},{10,11... | collective-permute-start | bytes 4718600 | tf_op jit(solution)/shard_map/ppermute | solution.py:595
  853.9 73.1 %collective-permute-start.39 = (bf16[768,256]{1,0:T(8,128)(2,1)S(1)}, bf16[768,256]{1,0:T(8,128)(2,1)S(1)}, u32[]{:S(2)}, u32[]{:S(2)}) collective-permute-start(bf16[768,256]{1,0:T(8,128)(2,1)S(1)} %get-tuple-element.144), channel_id=1, source_target_pairs={{0,4},{2,6},{4,0},{6,2},{1,5},{3,7},{5,1},{7,3},{8,12},{10,14},{12... | collective-permute-start | bytes 1179656 | tf_op jit(solution)/shard_map/ppermute | solution.py:599
  853.9 73.1 %collective-permute-start.40 = (bf16[768,256]{1,0:T(8,128)(2,1)S(1)}, bf16[768,256]{1,0:T(8,128)(2,1)S(1)}, u32[]{:S(2)}, u32[]{:S(2)}) collective-permute-start(bf16[768,256]{1,0:T(8,128)(2,1)S(1)} %get-tuple-element.142), channel_id=1, source_target_pairs={{0,2},{2,4},{4,6},{6,0},{1,3},{3,5},{5,7},{7,1},{8,10},{10,12},{12... | collective-permute-start | bytes 1179656 | tf_op jit(solution)/shard_map/ppermute | solution.py:599
  1057.0 41.6 %collective-permute-start.54 = (bf16[1024,512]{1,0:T(8,128)(2,1)S(1)}, bf16[1024,512]{1,0:T(8,128)(2,1)}, u32[]{:S(2)}, u32[]{:S(2)}) collective-permute-start(bf16[1024,512]{1,0:T(8,128)(2,1)S(1)} %outer.8), channel_id=1, source_target_pairs={{0,16},{16,0},{1,17},{17,1},{2,18},{18,2},{3,19},{19,3},{4,20},{20... | collective-permute-start | bytes 3145736 | tf_op jit(solution)/shard_map/ppermute | solution.py:595
  1067.2 46.5 %collective-permute-start.43 = (bf16[768,1024]{1,0:T(8,128)(2,1)}, bf16[768,1024]{1,0:T(8,128)(2,1)}, u32[]{:S(2)}, u32[]{:S(2)}) collective-permute-start(bf16[768,1024]{1,0:T(8,128)(2,1)} %convolution_convert_fusion.3), channel_id=1, source_target_pairs={{0,1},{1,0},{2,3},{3,2},{4,5},{5,4},{6,7},{7,6},{8,9},{9,8},{10,11... | collective-permute-start | bytes 4718600 | tf_op jit(solution)/shard_map/ppermute | solution.py:595
  1071.7 75.7 %collective-permute-start.45 = (bf16[768,1024]{1,0:T(8,128)(2,1)}, bf16[768,1024]{1,0:T(8,128)(2,1)}, u32[]{:S(2)}, u32[]{:S(2)}) collective-permute-start(bf16[768,1024]{1,0:T(8,128)(2,1)} %convolution_convert_fusion.2), channel_id=1, source_target_pairs={{0,1},{1,0},{2,3},{3,2},{4,5},{5,4},{6,7},{7,6},{8,9},{9,8},{10,11... | collective-permute-start | bytes 4718600 | tf_op jit(solution)/shard_map/ppermute | solution.py:595
  1084.0 80.5 %collective-permute-start.42 = (bf16[768,1024]{1,0:T(8,128)(2,1)}, bf16[768,1024]{1,0:T(8,128)(2,1)}, u32[]{:S(2)}, u32[]{:S(2)}) collective-permute-start(bf16[768,1024]{1,0:T(8,128)(2,1)} %add_convert_fusion.3), channel_id=1, source_target_pairs={{0,6},{2,0},{4,2},{6,4},{1,7},{3,1},{5,3},{7,5},{8,14},{10,8},{12,... | collective-permute-start | bytes 4718600 | tf_op jit(solution)/shard_map/ppermute | solution.py:599
  1098.5 145.4 %collective-permute-start.47 = (bf16[768,1024]{1,0:T(8,128)(2,1)}, bf16[768,1024]{1,0:T(8,128)(2,1)}, u32[]{:S(2)}, u32[]{:S(2)}) collective-permute-start(bf16[768,1024]{1,0:T(8,128)(2,1)} %convolution_convert_fusion.5.refs_1_), channel_id=1, source_target_pairs={{0,1},{1,0},{2,3},{3,2},{4,5},{5,4},{6,7},{7,6},{8,9},{9,8},{10,11... | collective-permute-start | bytes 4718600 | tf_op jit(solution)/shard_map/ppermute | solution.py:595
  1101.1 79.9 %collective-permute-start.55 = (bf16[256,512]{1,0:T(8,128)(2,1)}, bf16[256,512]{1,0:T(8,128)(2,1)}, u32[]{:S(2)}, u32[]{:S(2)}) collective-permute-start(bf16[256,512]{1,0:T(8,128)(2,1)} %get-tuple-element.150), channel_id=1, source_target_pairs={{0,2},{2,4},{4,6},{6,0},{1,3},{3,5},{5,7},{7,1},{8,10},{10,12},{12... | collective-permute-start | bytes 786440 | tf_op jit(solution)/shard_map/ppermute | solution.py:599
  1113.6 67.3 %collective-permute-start.56 = (bf16[256,512]{1,0:T(8,128)(2,1)}, bf16[256,512]{1,0:T(8,128)(2,1)}, u32[]{:S(2)}, u32[]{:S(2)}) collective-permute-start(bf16[256,512]{1,0:T(8,128)(2,1)} %get-tuple-element.152), channel_id=1, source_target_pairs={{0,4},{2,6},{4,0},{6,2},{1,5},{3,7},{5,1},{7,3},{8,12},{10,14},{12... | collective-permute-start | bytes 786440 | tf_op jit(solution)/shard_map/ppermute | solution.py:599
  1180.9 42.4 %collective-permute-start.48 = (bf16[1024,768]{1,0:T(8,128)(2,1)}, bf16[1024,768]{1,0:T(8,128)(2,1)}, u32[]{:S(2)}, u32[]{:S(2)}) collective-permute-start(bf16[1024,768]{1,0:T(8,128)(2,1)} %add_convert_fusion.refs_1_), channel_id=1, source_target_pairs={{0,16},{16,0},{1,17},{17,1},{2,18},{18,2},{3,19},{19,3},{4,20},{20... | collective-permute-start | bytes 4718600 | tf_op jit(solution)/shard_map/ppermute | solution.py:595
  1183.0 56.9 %collective-permute-start.58 = (bf16[128,512]{1,0:T(8,128)(2,1)}, bf16[128,512]{1,0:T(8,128)(2,1)}, u32[]{:S(2)}, u32[]{:S(2)}) collective-permute-start(bf16[128,512]{1,0:T(8,128)(2,1)} %constant_dynamic-slice_fusion.3), channel_id=1, source_target_pairs={{0,8},{8,0},{1,9},{9,1},{2,10},{10,2},{3,11},{11,3},{4,12},{12,4},... | collective-permute-start | bytes 393224 | tf_op jit(solution)/shard_map/ppermute | solution.py:595
  1183.0 153.7 %collective-permute-start.44 = (bf16[768,1024]{1,0:T(8,128)(2,1)}, bf16[768,1024]{1,0:T(8,128)(2,1)}, u32[]{:S(2)}, u32[]{:S(2)}) collective-permute-start(bf16[768,1024]{1,0:T(8,128)(2,1)} %add_convert_fusion.2.refs_1_), channel_id=1, source_target_pairs={{0,4},{2,6},{4,0},{6,2},{1,5},{3,7},{5,1},{7,3},{8,12},{10,14},{12... | collective-permute-start | bytes 4718600 | tf_op jit(solution)/shard_map/ppermute | solution.py:599
  1191.5 145.1 %collective-permute-start.46 = (bf16[768,1024]{1,0:T(8,128)(2,1)}, bf16[768,1024]{1,0:T(8,128)(2,1)}, u32[]{:S(2)}, u32[]{:S(2)}) collective-permute-start(bf16[768,1024]{1,0:T(8,128)(2,1)} %add_convert_fusion.1), channel_id=1, source_target_pairs={{0,2},{2,4},{4,6},{6,0},{1,3},{3,5},{5,7},{7,1},{8,10},{10,12},{12... | collective-permute-start | bytes 4718600 | tf_op jit(solution)/shard_map/ppermute | solution.py:599
  1252.3 90.2 %collective-permute-start.51 = (bf16[128,768]{1,0:T(8,128)(2,1)S(1)}, bf16[128,768]{1,0:T(8,128)(2,1)S(1)}, u32[]{:S(2)}, u32[]{:S(2)}) collective-permute-start(bf16[128,768]{1,0:T(8,128)(2,1)S(1)} %get-tuple-element.161), channel_id=1, source_target_pairs={{0,6},{2,0},{4,2},{6,4},{1,7},{3,1},{5,3},{7,5},{8,14},{10,8},{12,... | collective-permute-start | bytes 589832 | tf_op jit(solution)/shard_map/ppermute | solution.py:599
  1252.8 92.0 %collective-permute-start.52 = (bf16[128,768]{1,0:T(8,128)(2,1)S(1)}, bf16[128,768]{1,0:T(8,128)(2,1)S(1)}, u32[]{:S(2)}, u32[]{:S(2)}) collective-permute-start(bf16[128,768]{1,0:T(8,128)(2,1)S(1)} %get-tuple-element.160), channel_id=1, source_target_pairs={{0,4},{2,6},{4,0},{6,2},{1,5},{3,7},{5,1},{7,3},{8,12},{10,14},{12... | collective-permute-start | bytes 589832 | tf_op jit(solution)/shard_map/ppermute | solution.py:599
  1266.2 78.6 %collective-permute-start.53 = (bf16[128,768]{1,0:T(8,128)(2,1)S(1)}, bf16[128,768]{1,0:T(8,128)(2,1)S(1)}, u32[]{:S(2)}, u32[]{:S(2)}) collective-permute-start(bf16[128,768]{1,0:T(8,128)(2,1)S(1)} %get-tuple-element.159), channel_id=1, source_target_pairs={{0,2},{2,4},{4,6},{6,0},{1,3},{3,5},{5,7},{7,1},{8,10},{10,12},{12... | collective-permute-start | bytes 589832 | tf_op jit(solution)/shard_map/ppermute | solution.py:599
  1342.3 71.3 %collective-permute-start.50 = (bf16[768,1024]{1,0:T(8,128)(2,1)}, bf16[768,1024]{1,0:T(8,128)(2,1)}, u32[]{:S(2)}, u32[]{:S(2)}) collective-permute-start(bf16[768,1024]{1,0:T(8,128)(2,1)} %reduce-precision_convert_fusion.refs_1_), channel_id=1, source_target_pairs={{0,1},{1,0},{2,3},{3,2},{4,5},{5,4},{6,7},{7,6},{8,9},{9,8},{10,11... | collective-permute-start | bytes 4718600 | tf_op jit(solution)/shard_map/ppermute | solution.py:595
  (149 other events, 1935.8 us)
Sparse Core Ops, SparseCore 0:
  24.9 94.5 all-gather.3
  173.7 81.4 all-gather.5
  257.9 264.2 all-gather.7
  693.1 147.5 reduce-scatter.7
  844.5 183.2 reduce-scatter.5
  1042.4 281.8 reduce-scatter.3
